TPU v7x, 32 devices: a whole 2x2x4 slice. The times are simulated.
32 devices in a mesh: dp: 8 (over y, x, core), ffn: 4 (over z).
Axes of the slice: x: 2, y: 2, z: 4, core: 2. Of those that a mesh axis runs over, the one named last changes fastest.
Arguments:
- text_hidden: bfloat16 [16384, 768], P(('dp', 'ffn')), may hold values from -6 to 6
- visual_maps: bfloat16 [1568, 2048], P(('dp', 'ffn')), may hold values from -1200 to 1200
- patch_order: int32 [32, 49], P(('dp', 'ffn')), may hold values from 0 to 48, each once within a row
- segment_ids: int32 [32, 561], P(('dp', 'ffn')), may hold values from 0 to 2, never falling along the last dimension, each value on 1 to 280 neighbouring positions
- rel_bucket: int32 [32, 561, 561], P(('dp', 'ffn')), may hold values from 0 to 31
- x_bucket: int32 [32, 561, 561], P(('dp', 'ffn')), may hold values from 0 to 63
- y_bucket: int32 [32, 561, 561], P(('dp', 'ffn')), may hold values from 0 to 63
- bn_scale: float32 [2048], replicated, may hold values from 0.1 to 1.9
- bn_shift: float32 [2048], replicated, may hold values from -3 to 3
- vis_proj: bfloat16 [2048, 768], P(('dp', 'ffn')), may hold values from -0.125 to 0.125
- w_query: bfloat16 [768, 768], P(('dp', 'ffn')), may hold values from -0.21875 to 0.21875
- w_key: bfloat16 [768, 768], P(('dp', 'ffn')), may hold values from -0.21875 to 0.21875
- w_value: bfloat16 [768, 768], P(('dp', 'ffn')), may hold values from -0.21875 to 0.21875
- w_output: bfloat16 [768, 768], P(('dp', 'ffn')), may hold values from -0.625 to 0.625
- rel_table: float32 [32, 12], replicated, may hold values from -4 to 4
- x_table: float32 [64, 12], replicated, may hold values from -4 to 4
- y_table: float32 [64, 12], replicated, may hold values from -4 to 4
- first_gain: float32 [768], replicated, may hold values from 0.1 to 1.9
- first_bias: float32 [768], replicated, may hold values from -2 to 2
- w_inner: bfloat16 [768, 3072], P('dp', 'ffn'), may hold values from -0.21875 to 0.21875
- b_inner: float32 [3072], replicated, may hold values from -2 to 2
- w_outer: bfloat16 [3072, 768], P('ffn', 'dp'), may hold values from -0.109375 to 0.109375
- b_outer: float32 [768], replicated, may hold values from -2 to 2
- second_gain: float32 [768], replicated, may hold values from 0.1 to 1.9
- second_bias: float32 [768], replicated, may hold values from -2 to 2
- cotangent: bfloat16 [17952, 768], P(('dp', 'ffn')), may hold values from -6 to 6
Outputs:
- output: bfloat16 [17952, 768], P(('dp', 'ffn'))
- text_grad: float32 [16384, 768], P(('dp', 'ffn'))
- visual_grad: float32 [1568, 2048], P(('dp', 'ffn'))
- bn_scale_grad: float32 [2048], replicated
- bn_shift_grad: float32 [2048], replicated
- vis_proj_grad: float32 [2048, 768], P(('dp', 'ffn'))
- w_query_grad: float32 [768, 768], P(('dp', 'ffn'))
- w_key_grad: float32 [768, 768], P(('dp', 'ffn'))
- w_value_grad: float32 [768, 768], P(('dp', 'ffn'))
- w_output_grad: float32 [768, 768], P(('dp', 'ffn'))
- rel_table_grad: float32 [32, 12], replicated
- x_table_grad: float32 [64, 12], replicated
- y_table_grad: float32 [64, 12], replicated
- first_gain_grad: float32 [768], replicated
- first_bias_grad: float32 [768], replicated
- w_inner_grad: float32 [768, 3072], P('dp', 'ffn')
- b_inner_grad: float32 [3072], replicated
- w_outer_grad: float32 [3072, 768], P('ffn', 'dp')
- b_outer_grad: float32 [768], replicated
- second_gain_grad: float32 [768], replicated
- second_bias_grad: float32 [768], replicated
Inputs may be any that keep to these rules, and one draw needn't show every extreme that they name: Each row of patch_order names every one of the 49 cells of its packed row once. `segment_ids`: document numbers never fall along a packed row.
All inputs are finite; a program needn't handle non-finite values.
Results may differ from a plain program's by a relative error of at most 0.019.
Values may be sent and summed in bfloat16 or wider, within the bound.
No kernel may reach another device: no remote copies, remote signals or barrier semaphores. Data moves between devices by JAX's collectives and lax.ppermute only.
A program may use at most 320 MiB of HBM per device.

v0:
```python
import functools

import jax
import jax.numpy as jnp
from jax import lax
from jax.experimental import pallas as pl
from jax.experimental.pallas import tpu as pltpu
from jax.sharding import PartitionSpec as P

EPS = 1e-05
NEG = -1e30
F32 = jnp.float32
BF16 = jnp.bfloat16
ALL = ("dp", "ffn")
LEVELS = 21845.0
MIB = 2**20


def dot_nn(a, b):
    return lax.dot_general(a, b, (((1,), (0,)), ((), ())), preferred_element_type=F32)


def dot_nt(a, b):
    return lax.dot_general(a, b, (((1,), (1,)), ((), ())), preferred_element_type=F32)


def dot_tn(a, b):
    return lax.dot_general(a, b, (((0,), (0,)), ((), ())), preferred_element_type=F32)


def pad_rows(values, rows):
    return jnp.pad(values, ((0, rows - values.shape[0]), (0, 0)))


def send_dp(values, bits):
    size = lax.axis_size("dp")
    return lax.ppermute(values, "dp", [(i, i ^ bits) for i in range(size)])


def send_ffn(values, shift):
    size = lax.axis_size("ffn")
    return lax.ppermute(values, "ffn", [(i, (i + shift) % size) for i in range(size)])


def swap_ffn(values, bits):
    size = lax.axis_size("ffn")
    return lax.ppermute(values, "ffn", [(i, i ^ bits) for i in range(size)])


def exchanges():
    steps = []
    for axis, send in (("dp", send_dp), ("ffn", swap_ffn)):
        bit = 1
        while bit < lax.axis_size(axis):
            steps.append(functools.partial(send, bits=bit))
            bit *= 2
    return steps


class Sum:
    def __init__(self, values):
        self.values = values
        self.steps = exchanges()

    def step(self):
        if self.steps:
            self.values = self.values + self.steps.pop(0)(self.values)

    def finish(self):
        while self.steps:
            self.step()
        return self.values


class Gather:
    def __init__(self, own, rows):
        self.own = own
        self.rows = rows

    def along_ffn(self, begin=1, end=None):
        size = lax.axis_size("ffn")
        self.far = self.far[:begin] if begin > 1 else [self.own]
        self.far += [send_ffn(self.own, k) for k in range(begin, end or size)]

    def order(self):
        size = lax.axis_size("ffn")
        here = lax.axis_index("ffn")
        if all(rows % 8 == 0 for rows in self.rows):
            self.block = order_blocks(here, self.far, self.rows)
            return
        pieces = []
        for slot in range(size):
            value = self.far[0]
            for k in range(1, size):
                value = jnp.where((here - k + size) % size == slot, self.far[k], value)
            pieces.append(value)
        begin, ordered = 0, []
        for rows in self.rows:
            ordered += [value[begin : begin + rows] for value in pieces]
            begin += rows
        self.block = jnp.concatenate(ordered, 0)

    def near(self, cut):
        quads = lax.axis_size("dp") // 2
        self.cut = cut
        self.others = [send_dp(self.block, 1)]
        if quads == 4:
            self.mine = [self.block, send_dp(self.block, 2), send_dp(self.block, 4)]
        else:
            self.mine = [self.block] + [send_dp(self.block, 2 * k) for k in range(1, quads)]

    def diagonal(self):
        self.others += [send_dp(block, 1) for block in self.mine[1:]]
        if lax.axis_size("dp") == 8:
            low = send_dp(self.mine[1][: self.cut], 4)
            high = send_dp(self.mine[2][self.cut :], 2)
            self.mine.append((low, high))

    def across(self):
        if lax.axis_size("dp") == 8:
            self.others.append(tuple(send_dp(piece, 1) for piece in self.mine[3]))

    def state(self):
        return {k: v for k, v in vars(self).items() if k in ("own", "far", "block", "mine", "others")}

    def hold(self, state):
        vars(self).update(state)

    def parts(self):
        found = []
        for k, (mine, other) in enumerate(zip(self.mine, self.others)):
            for bits, block in ((2 * k, mine), (2 * k + 1, other)):
                if isinstance(block, tuple):
                    found += [(block[0], bits, 0), (block[1], bits, self.cut)]
                else:
                    found.append((block, bits, 0))
        return found


def epoch(*values):
    return lax.optimization_barrier(values)


def pick(values, index, axis):
    return lax.dynamic_index_in_dim(values, index, axis, keepdims=False)


def plus(a, b):
    return (a.astype(F32) + b.astype(F32)).astype(BF16)


class Scatter:
    def __init__(self, mine, away, far):
        self.value = mine
        self.away = away
        self.far = far

    def core(self):
        self.got = send_dp(self.away, 1)

    def near(self):
        mine, got = self.value, self.got
        if mine.shape[0] == 4:
            half = mine.shape[1] // 2
            self.low = send_dp(plus(mine[3, :half], got[3, :half]), 4)
            self.high = send_dp(plus(mine[3, half:], got[3, half:]), 2)

    def prepare(self):
        mine, got = self.value, self.got
        half = mine.shape[1] // 2
        self.blocks = []
        for k in range(1, mine.shape[0]):
            block = mine[k].astype(F32) + got[k].astype(F32)
            if mine.shape[0] == 4 and k == 1:
                block = jnp.concatenate([block[:half] + self.low.astype(F32), block[half:]], 0)
            if mine.shape[0] == 4 and k == 2:
                block = jnp.concatenate([block[:half], block[half:] + self.high.astype(F32)], 0)
            if mine.shape[0] == 4 and k == 3:
                continue
            self.blocks.append(block.astype(BF16))

    def quads(self):
        self.blocks = [send_dp(block, 2 * k) for k, block in enumerate(self.blocks, 1)]

    def join(self):
        own = self.value[0].astype(F32) + self.got[0].astype(F32)
        self.value = (own + sum(block.astype(F32) for block in self.blocks)).astype(BF16)

    def held(self):
        return {k: v for k, v in vars(self).items() if k != "far"}

    def hold(self, state):
        vars(self).update(state)

    def along_ffn(self, begin=1, end=None):
        size = lax.axis_size("ffn")
        here = lax.axis_index("ffn")
        self.pieces = self.pieces[:begin] if begin > 1 else [self.far(self.value, here)]
        for k in range(begin, end or size):
            self.pieces.append(send_ffn(self.far(self.value, (here + k) % size), k))

    def total(self):
        return sum(piece.astype(F32) for piece in self.pieces)


LIMIT = 56 * MIB


def whole(shape):
    return pl.BlockSpec(shape, lambda *_: (0,) * len(shape))


def cost(flops, nbytes):
    return pl.CostEstimate(flops=flops // 1000, bytes_accessed=nbytes // 1000, transcendentals=0)


def pack_kernel(q_ref, k_ref, v_ref, p_ref, visual_ref, out_ref):
    row = 0
    for ref in (q_ref, k_ref, v_ref, p_ref):
        out_ref[row : row + ref.shape[0], :] = ref[...]
        row += ref.shape[0]
    width = out_ref.shape[1]
    count = visual_ref.shape[0]
    visual = visual_ref[...].astype(F32)
    mean = jnp.sum(visual, 0, keepdims=True) * (1.0 / count)
    gap = visual - mean
    spread = jnp.sum(gap * gap, 0, keepdims=True)
    channels = visual_ref.shape[1]
    chunks = pl.cdiv(channels, width)
    blank = jnp.zeros((1, chunks * width - channels), F32)
    pieces = []
    for values, times in ((mean, 3), (spread, 2)):
        if chunks * width > channels:
            values = jnp.concatenate([values, blank], 1)
        for _ in range(times):
            piece = values.astype(BF16).astype(F32)
            values = values - piece
            pieces += [piece[:, n * width : (n + 1) * width] for n in range(chunks)]
    pieces += [jnp.zeros((1, width), F32)] * (out_ref.shape[0] - row - len(pieces))
    out_ref[row:, :] = jnp.concatenate(pieces, 0).astype(BF16)


def pack_first(w_query, w_key, w_value, vis_proj, visual):
    width = w_query.shape[1]
    moments = pl.cdiv(5 * pl.cdiv(visual.shape[1], width), 16) * 16
    rows = [w.shape[0] for w in (w_query, w_key, w_value, vis_proj)] + [moments]
    own = pl.pallas_call(
        pack_kernel,
        out_shape=jax.ShapeDtypeStruct((sum(rows), width), BF16),
        name="pack_first",
    )(w_query, w_key, w_value, vis_proj, visual)
    return own, rows


def order_kernel(rows, here_ref, *refs):
    parts, out_ref = refs[:-1], refs[-1]
    size = len(parts)
    here = here_ref[0]
    for index in range(size):

        @pl.when(here == index)
        def _(index=index):
            begin = 0
            for count in rows:
                for k in range(size):
                    row = begin * size + (index - k) % size * count
                    out_ref[row : row + count, :] = parts[k][begin : begin + count, :]
                begin += count


def order_blocks(here, parts, rows):
    width = parts[0].shape[1]
    return pl.pallas_call(
        functools.partial(order_kernel, rows),
        in_specs=[pl.BlockSpec(memory_space=pltpu.SMEM)]
        + [pl.BlockSpec(memory_space=pltpu.VMEM)] * len(parts),
        out_specs=pl.BlockSpec(memory_space=pltpu.VMEM),
        out_shape=jax.ShapeDtypeStruct((len(parts) * sum(rows), width), BF16),
        name="order_blocks",
    )(here.reshape(1).astype(jnp.int32), *parts)


def place_entries(parts, layout):
    entries = []
    for n, (block, _, first) in enumerate(parts):
        for begin, rows, out, base, lane in layout:
            if first <= begin and begin + rows <= first + block.shape[0]:
                entries.append((n, begin - first, rows, out, base, lane))
    return entries


def place_index(parts):
    place = lax.axis_index("dp")
    return jnp.stack([place ^ bits for _, bits, _ in parts]).astype(jnp.int32)


def part_copies(entries, place_ref, parts, outs, sems):
    copies = []
    for n, (part, begin, rows, out, base, lane) in enumerate(entries):
        target = pl.multiple_of(base + place_ref[part] * rows, 16)
        width = parts[part].shape[1]
        copies.append(
            pltpu.make_async_copy(
                parts[part].at[pl.ds(begin, rows), :],
                outs[out].at[pl.ds(target, rows), pl.ds(lane, width)],
                sems.at[n],
            )
        )
    return copies


def picked(order_col, size):
    lane = lax.broadcasted_iota(jnp.int32, (size, size), 1)
    return (order_col == lane).astype(F32)


def exact(a, b, dims):
    return lax.dot_general(
        a, b, (dims, ((), ())), precision=lax.Precision.HIGHEST, preferred_element_type=F32
    )


def first_kernel(entries, count, devices, place_ref, *refs):
    parts, refs = refs[:count], refs[count:]
    text_ref, visual_ref, order_ref, lines_ref = refs[:4]
    qkv_w_ref, proj_ref, hidden_ref, low_ref, qkv_ref, bn_ref, stats_ref = refs[4:11]
    moments_ref, sems = refs[11:]
    outs = (qkv_w_ref, proj_ref, moments_ref)
    copies = part_copies(entries, place_ref, parts, outs, sems)
    for copy in copies:
        copy.start()
    copies = [(entry[3], copy) for entry, copy in zip(entries, copies)]
    text_len, width = text_ref.shape
    visual_len, channels = visual_ref.shape
    hidden_ref[:text_len, :] = text_ref[...].astype(F32)
    low_ref[:text_len, :] = text_ref[...]
    for out, copy in copies:
        if out == 2:
            copy.wait()
    chunks = pl.cdiv(channels, width)
    moments = moments_ref[...].astype(F32).reshape(devices, -1, width)
    means = sum(moments[:, n * chunks : (n + 1) * chunks] for n in range(3))
    spreads = sum(moments[:, n * chunks : (n + 1) * chunks] for n in range(3, 5))
    average = jnp.sum(means, 0) * (1.0 / devices)
    gap = means - average[None]
    rows = visual_len * devices
    spread = (jnp.sum(spreads, 0) + visual_len * jnp.sum(gap * gap, 0)) * (1.0 / rows)
    inverse = lax.rsqrt(spread + EPS)

    def flat(values):
        pieces = [values[n : n + 1, :] for n in range(chunks)]
        return jnp.concatenate(pieces, 1)[:, :channels]

    average, inverse = flat(average), flat(inverse)
    stats_ref[0:1, :] = average
    stats_ref[1:2, :] = inverse
    normed = (visual_ref[...].astype(F32) - average) * inverse
    bn_rows = (normed * lines_ref[0:1, :] + lines_ref[1:2, :]).astype(BF16)
    bn_ref[...] = bn_rows
    for out, copy in copies:
        if out == 1:
            copy.wait()
    tokens = dot_nn(bn_rows, proj_ref[...])
    tokens = exact(picked(order_ref[...], visual_len), tokens, ((1,), (0,)))
    blank = jnp.zeros((hidden_ref.shape[0] - text_len - visual_len, width), F32)
    tokens = jnp.concatenate([tokens, blank], 0)
    hidden_ref[text_len:, :] = tokens
    low_ref[text_len:, :] = tokens.astype(BF16)
    for out, copy in copies:
        if out == 0:
            copy.wait()
    low = low_ref[...]
    for n in range(3):
        lanes = slice(n * width, (n + 1) * width)
        values = dot_nn(low, qkv_w_ref[:, lanes])
        qkv_ref[:, lanes] = (values * 0.125 if n == 0 else values).astype(BF16)


def first_rows(parts, layout, text, visual, order, lines, rows, proj_rows, moment_rows):
    devices = lax.axis_size("dp") * lax.axis_size("ffn")
    width = text.shape[1]
    channels = visual.shape[1]
    entries = place_entries(parts, layout)
    vmem = pl.BlockSpec(memory_space=pltpu.VMEM)
    shapes = [
        ((width, 3 * width), BF16),
        ((proj_rows, width), BF16),
        ((rows, width), F32),
        ((rows, width), BF16),
        ((rows, 3 * width), BF16),
        ((visual.shape[0], channels), BF16),
        ((2, channels), F32),
    ]
    return pl.pallas_call(
        functools.partial(first_kernel, entries, len(parts), devices),
        in_specs=[pl.BlockSpec(memory_space=pltpu.SMEM)]
        + [pl.BlockSpec(memory_space=pl.ANY)] * len(parts)
        + [vmem] * 4,
        out_specs=[vmem] * len(shapes),
        out_shape=[jax.ShapeDtypeStruct(*shape) for shape in shapes],
        scratch_shapes=[
            pltpu.VMEM((moment_rows * devices, width), BF16),
            pltpu.SemaphoreType.DMA((len(entries),)),
        ],
        compiler_params=pltpu.CompilerParams(vmem_limit_bytes=LIMIT),
        cost_estimate=cost(0, 25_000_000),
        name="first_rows",
    )(
        place_index(parts),
        *[block for block, _, _ in parts],
        text,
        visual,
        order,
        lines,
    )


def store_blocks(mine_ref, away_ref, core, quad, store):
    quads = mine_ref.shape[0]
    for bit in range(2):

        @pl.when(core == bit)
        def _(bit=bit):
            for dp in range(2 * quads):
                ref = mine_ref if dp % 2 == bit else away_ref
                store(ref, (dp // 2) ^ quad, dp)


def place_pair():
    place = lax.axis_index("dp")
    return jnp.stack([place % 2, place // 2]).astype(jnp.int32)


def feed_kernel(entries, count, length, ffn, place_ref, core_ref, *refs):
    parts, refs = refs[:count], refs[count:]
    mixed_ref, hidden_ref, lines_ref, inner_b_ref, ct_ref = refs[:5]
    normed_ref, scale_ref, output_ref, total_ref, sums_ref, inner_sums_ref = refs[5:11]
    out_w_ref, mine_ref, away_ref = refs[11:14]
    outer_w_ref, inner_w_ref, act_ref, slope_ref, first_ref, low_ref = refs[14:20]
    first_turned, low_turned, sems = refs[20:]
    step = pl.program_id(0)
    width = hidden_ref.shape[1]
    outs = (out_w_ref, outer_w_ref, inner_w_ref)
    gain1, bias1, outer_b, gain2, bias2 = [lines_ref[n : n + 1, :] for n in range(5)]

    @pl.when(step == 0)
    def _():
        for copy in part_copies(entries, place_ref, parts, outs, sems):
            copy.start()

    for index in range(ffn):

        @pl.when(step == index)
        def _(index=index):
            copies = part_copies(entries, place_ref, parts, outs, sems)
            for (_, _, _, out, base, _), copy in zip(entries, copies):
                if (out == 0 and index == 0) or (out > 0 and base == index * width):
                    copy.wait()

    @pl.when(step == 0)
    def _():
        attended = dot_nn(mixed_ref[...], out_w_ref[...])
        normed, scale = norm_stats(hidden_ref[...] + attended)
        first = normed * gain1 + bias1
        normed_ref[...] = normed
        scale_ref[...] = scale
        low = first.astype(BF16)
        first_ref[...] = low
        total_ref[...] = first + outer_b
        first_turned[...] = low.T

    @pl.when(step < ffn)
    def _():
        rows = pl.ds(pl.multiple_of(step * width, width), width)
        inner = dot_nn(first_ref[...], inner_w_ref[rows, :]) + inner_b_ref[step]
        root = 0.7978845608028654
        square = inner * inner
        half = 0.5 + 0.5 * jnp.tanh(inner * (root + (0.044715 * root) * square))
        act = inner * half
        slope = half + act * (1.0 - half) * (2 * root + (6 * 0.044715 * root) * square)
        slope_ref[step] = slope.astype(BF16)
        act = act.astype(BF16)
        act_ref[step] = act
        total_ref[...] += dot_nt(act, outer_w_ref[rows, :])

    @pl.when(step == ffn - 1)
    def _():
        normed, scale = norm_stats(total_ref[...])
        output_ref[...] = (normed * gain2 + bias2).astype(BF16)
        row = lax.broadcasted_iota(jnp.int32, (normed.shape[0], 1), 0)
        ct = jnp.where(row < length, ct_ref[...].astype(F32), 0.0)
        grad = norm_back(ct, normed, scale, gain2)
        total_ref[...] = grad
        low = grad.astype(BF16)
        low_ref[...] = low
        low_turned[...] = low.T
        sums_ref[0:1, :] = jnp.sum(ct * normed, 0, keepdims=True)
        sums_ref[1:2, :] = jnp.sum(ct, 0, keepdims=True)
        sums_ref[2:3, :] = jnp.sum(grad, 0, keepdims=True)

    @pl.when(step >= ffn)
    def _():
        f = step - ffn
        rows = pl.ds(pl.multiple_of(f * width, width), width)
        grad = dot_nn(low_ref[...], outer_w_ref[rows, :]) * slope_ref[f].astype(F32)
        inner_sums_ref[0] = jnp.sum(grad, 0, keepdims=True)
        grad = grad.astype(BF16)
        total_ref[...] += dot_nt(grad, inner_w_ref[rows, :])
        inner = dot_nn(first_turned[...], grad).astype(BF16)
        outer = dot_nn(low_turned[...], act_ref[f]).astype(BF16)
        size = mine_ref.shape[3]

        def store(ref, slot, dp):
            ref[slot, 0, 0] = inner[dp * size : (dp + 1) * size]
            ref[slot, 1, 0] = outer[dp * size : (dp + 1) * size]

        store_blocks(mine_ref, away_ref, core_ref[0], core_ref[1], store)


def feed_forward(feeds, mixed, hidden, lines, inner_b, ct, inner_rows):
    parts, entries = [], []
    for some, layout in feeds:
        for part, *entry in place_entries(some, layout):
            entries.append((part + len(parts), *entry))
        parts += some
    entries.sort(key=lambda entry: (entry[3] > 0, entry[4], -entry[3]))
    rows, width = hidden.shape
    ffn, _, columns = inner_b.shape
    quads = lax.axis_size("dp") // 2
    square = whole((rows, width))
    back = lambda i: jnp.maximum(i - ffn, 0)
    block = pl.BlockSpec((quads, 2, 1, inner_rows, columns), lambda i: (0, 0, back(i), 0, 0))
    blocks = jax.ShapeDtypeStruct((quads, 2, ffn, inner_rows, columns), BF16)
    smem = pl.BlockSpec(memory_space=pltpu.SMEM)
    shapes = [
        ((rows, width), F32),
        ((rows, 1), F32),
        (ct.shape, BF16),
        ((rows, width), F32),
        ((3, width), F32),
        ((ffn, 1, columns), F32),
        ((width, width), BF16),
    ]
    return pl.pallas_call(
        functools.partial(feed_kernel, entries, len(parts), ct.shape[0], ffn),
        grid=(2 * ffn,),
        in_specs=[smem, smem]
        + [pl.BlockSpec(memory_space=pl.ANY)] * len(parts)
        + [square, square, whole(lines.shape), whole(inner_b.shape), square],
        out_specs=[square, whole((rows, 1)), square, square, whole((3, width))]
        + [pl.BlockSpec((1, 1, columns), lambda i: (back(i), 0, 0)), whole((width, width))]
        + [block, block],
        out_shape=[jax.ShapeDtypeStruct(*shape) for shape in shapes] + [blocks, blocks],
        scratch_shapes=[
            pltpu.VMEM((ffn * width, columns), BF16),
            pltpu.VMEM((ffn * width, columns), BF16),
            pltpu.VMEM((ffn, rows, columns), BF16),
            pltpu.VMEM((ffn, rows, columns), BF16),
            pltpu.VMEM((rows, width), BF16),
            pltpu.VMEM((rows, width), BF16),
            pltpu.VMEM((width, rows), BF16),
            pltpu.VMEM((width, rows), BF16),
            pltpu.SemaphoreType.DMA((len(entries),)),
        ],
        compiler_params=pltpu.CompilerParams(vmem_limit_bytes=LIMIT),
        cost_estimate=cost(0, 100_000_000),
        name="feed_forward",
    )(
        place_index(parts),
        place_pair(),
        *[part for part, _, _ in parts],
        mixed,
        hidden,
        lines,
        inner_b,
        ct,
    )


def norm_kernel(
    grad_ref, normed_ref, scale_ref, lines_ref, w_ref, out_ref, low_ref, mix_ref, sums_ref
):
    grad, normed = grad_ref[...], normed_ref[...]
    attn = norm_back(grad, normed, scale_ref[...], lines_ref[0:1, :])
    out_ref[...] = attn
    low = attn.astype(BF16)
    low_ref[...] = low
    mix_ref[...] = dot_nt(low, w_ref[...]).astype(BF16)
    sums_ref[0:1, :] = jnp.sum(grad * normed, 0, keepdims=True)
    sums_ref[1:2, :] = jnp.sum(grad, 0, keepdims=True)


def norm_rows(grad, normed, scale, lines, out_w):
    rows, width = grad.shape
    low = jax.ShapeDtypeStruct((rows, width), BF16)
    return pl.pallas_call(
        norm_kernel,
        out_shape=[
            jax.ShapeDtypeStruct((rows, width), F32),
            low,
            low,
            jax.ShapeDtypeStruct((2, width), F32),
        ],
        compiler_params=pltpu.CompilerParams(vmem_limit_bytes=LIMIT),
        cost_estimate=cost(0, 12_000_000),
        name="norm_rows",
    )(grad, normed, scale, lines, out_w)


def tail_kernel(text_len, place_ref, *refs):
    inputs, (order_ref, attn_ref, tokens_ref), refs = refs[:11], refs[11:14], refs[14:]
    outputs, buffers = refs[:2], refs[2:13]
    mine, away, in_sems, out_sems = refs[13:]
    low_ref, mixed_ref, attn_low_ref, qkv_w_ref, bn_ref = buffers[6:]
    names = (6, 0, 1, 2, 3, 4, 5, 7, 8, 9, 10)
    copies = {n: pltpu.make_async_copy(inputs[n], buffers[n], in_sems.at[n]) for n in names}
    for n in names:
        copies[n].start()
    visual_len = bn_ref.shape[0]
    width = attn_low_ref.shape[1]
    core, quad = place_ref[0], place_ref[1]
    sent = []

    def spread(values, begin, n):
        values = values.astype(BF16)
        rows = values.shape[0] // (2 * mine.shape[0])

        def store(ref, slot, dp):
            ref[slot, begin : begin + rows, :] = values[dp * rows : (dp + 1) * rows]

        store_blocks(mine, away, core, quad, store)
        part = pl.ds(begin, rows)
        for k, ref in enumerate((mine, away)):
            copy = pltpu.make_async_copy(
                ref.at[:, part, :], outputs[k].at[:, part, :], out_sems.at[n, k]
            )
            copy.start()
            sent.append(copy)
        return begin + rows

    copies[6].wait()
    turned = low_ref[...].T
    begin = 0
    grads = []
    for n in range(3):
        copies[2 * n].wait()
        copies[2 * n + 1].wait()
        grads.append(jnp.concatenate([buffers[2 * n][...], buffers[2 * n + 1][...]], 1))
        begin = spread(dot_nn(turned, grads[n]), begin, n)
    copies[7].wait()
    copies[8].wait()
    begin = spread(dot_nn(mixed_ref[...].T, attn_low_ref[...]), begin, 3)
    copies[9].wait()
    tokens = attn_ref[...]
    for n in range(3):
        lanes = slice(n * width, (n + 1) * width)
        tokens = tokens + dot_nt(grads[n][text_len:], qkv_w_ref[:, lanes])
    picker = picked(order_ref[...], visual_len)
    tokens = exact(picker, tokens[:visual_len], ((0,), (0,))).astype(BF16)
    tokens_ref[...] = tokens
    copies[10].wait()
    spread(dot_tn(bn_ref[...], tokens), begin, 4)
    for copy in sent:
        copy.wait()


def tail_rows(back, qkv_w, attn, attn_low, mixed, low, order, bn_rows, text_len):
    dp, ffn = lax.axis_size("dp"), lax.axis_size("ffn")
    rows, width = attn.shape
    visual_len, channels = bn_rows.shape
    size = 4 * (width // dp) + channels // dp
    vmem = pl.BlockSpec(memory_space=pltpu.VMEM)
    anywhere = pl.BlockSpec(memory_space=pl.ANY)
    inputs = [g for pair in back for g in pair] + [low, mixed, attn_low, qkv_w, bn_rows]
    rest = rows - text_len
    tail = pl.BlockSpec((rest, width), lambda *_: (text_len // rest, 0))
    blocks = jax.ShapeDtypeStruct((dp // 2, size, width), BF16)
    return pl.pallas_call(
        functools.partial(tail_kernel, text_len),
        grid=(1,),
        in_specs=[pl.BlockSpec(memory_space=pltpu.SMEM)]
        + [anywhere] * len(inputs)
        + [whole(order.shape), tail],
        out_specs=[whole((visual_len, width))] + [anywhere] * 2,
        out_shape=[jax.ShapeDtypeStruct((visual_len, width), BF16), blocks, blocks],
        scratch_shapes=[pltpu.VMEM(x.shape, BF16) for x in inputs]
        + [
            pltpu.VMEM(blocks.shape, BF16),
            pltpu.VMEM(blocks.shape, BF16),
            pltpu.SemaphoreType.DMA((len(inputs),)),
            pltpu.SemaphoreType.DMA((5, 2)),
        ],
        compiler_params=pltpu.CompilerParams(vmem_limit_bytes=LIMIT),
        cost_estimate=cost(0, 40_000_000),
        name="tail_rows",
    )(place_pair(), *inputs, order, attn)


def batch_kernel(tokens_ref, visual_ref, stats_ref, proj_ref, grad_bn_ref, sums_ref):
    grad_bn = dot_nt(tokens_ref[...], proj_ref[...])
    grad_bn_ref[...] = grad_bn
    normed = (visual_ref[...].astype(F32) - stats_ref[0:1, :]) * stats_ref[1:2, :]
    sums_ref[0:1, :] = jnp.sum(grad_bn, 0, keepdims=True)
    sums_ref[1:2, :] = jnp.sum(grad_bn * normed, 0, keepdims=True)


def batch_rows(tokens, visual, stats, proj):
    return pl.pallas_call(
        batch_kernel,
        out_shape=[
            jax.ShapeDtypeStruct(visual.shape, F32),
            jax.ShapeDtypeStruct((2, visual.shape[1]), F32),
        ],
        compiler_params=pltpu.CompilerParams(vmem_limit_bytes=LIMIT),
        cost_estimate=cost(0, 6_000_000),
        name="batch_rows",
    )(tokens, visual, stats, proj)


def text_kernel(*refs):
    dq, dk, dv = refs[0:2], refs[2:4], refs[4:6]
    qkv_w_ref, attn_ref, text_ref = refs[6:]
    width = text_ref.shape[1]
    total = attn_ref[...]
    for n, (low, high) in enumerate((dq, dk, dv)):
        grads = jnp.concatenate([low[...], high[...]], 1)
        total = total + dot_nt(grads, qkv_w_ref[:, n * width : (n + 1) * width])
    text_ref[...] = total


def text_rows(back, qkv_w, attn, text_len):
    width = attn.shape[1]
    step = text_len // 2
    grads = [g for pair in back for g in pair]
    return pl.pallas_call(
        text_kernel,
        grid=(2,),
        in_specs=[pl.BlockSpec((step, g.shape[1]), lambda i: (i, 0)) for g in grads]
        + [whole(qkv_w.shape), pl.BlockSpec((step, width), lambda i: (i, 0))],
        out_specs=pl.BlockSpec((step, width), lambda i: (i, 0)),
        out_shape=jax.ShapeDtypeStruct((text_len, width), F32),
        compiler_params=pltpu.CompilerParams(vmem_limit_bytes=LIMIT),
        cost_estimate=cost(0, 25_000_000),
        name="text_rows",
    )(*grads, qkv_w, attn)


def lane_rows(values, width):
    lanes = values.shape[1]
    pieces = pl.cdiv(lanes, width)
    if pieces * width > lanes:
        values = jnp.concatenate([values, jnp.zeros((1, pieces * width - lanes), F32)], 1)
    return [values[:, n * width : (n + 1) * width] for n in range(pieces)]


def sums_kernel(bn_ref, one_ref, two_ref, inner_ref, *refs):
    out_ref = refs[-1]
    width = out_ref.shape[1]
    rows = []
    for n in range(bn_ref.shape[0]):
        rows += lane_rows(bn_ref[n : n + 1, :], width)
    for ref in (one_ref, two_ref):
        rows += [ref[n : n + 1, :] for n in range(ref.shape[0])]
    inner = [inner_ref[n] for n in range(inner_ref.shape[0])]
    rows += lane_rows(jnp.concatenate(inner, 1), width)
    tables = sum(ref[...] for ref in refs[:-1]).T
    blank = jnp.zeros((tables.shape[0], 256 - tables.shape[1]), F32)
    tables = jnp.concatenate([tables, blank], 1)
    group = width // 256
    for n in range(0, 12, group):
        rows.append(jnp.concatenate([tables[h : h + 1] for h in range(n, n + group)], 1))
    rows += [jnp.zeros((1, width), F32)] * (out_ref.shape[0] - len(rows))
    out_ref[...] = jnp.concatenate(rows, 0)


def pack_sums(bn_sums, one, two, inner, tables):
    width = one.shape[1]
    rows = 2 * pl.cdiv(bn_sums.shape[1], width) + 5 + inner.size // width + 12 * 256 // width
    return pl.pallas_call(
        sums_kernel,
        out_shape=jax.ShapeDtypeStruct((pl.cdiv(rows, 8) * 8, width), F32),
        cost_estimate=cost(0, 1_000_000),
        name="pack_sums",
    )(bn_sums, one, two, inner, *tables)


def finish_kernel(levels, count, *refs):
    left_ref, right_ref, grad_bn_ref, visual_ref, stats_ref, lines_ref = refs[:6]
    shift_ref, scale_ref, grad_ref, inner_ref = refs[6:10]
    vectors, tables = refs[10:15], refs[15:]
    total = left_ref[...] + right_ref[...]
    width = total.shape[1]
    channels = grad_bn_ref.shape[1]
    row = 0

    def take(lanes):
        nonlocal row
        pieces = pl.cdiv(lanes, width)
        row += pieces
        return jnp.concatenate([total[n : n + 1] for n in range(row - pieces, row)], 1)[:, :lanes]

    shift, scale = take(channels), take(channels)
    shift_ref[...] = shift.reshape(channels)
    scale_ref[...] = scale.reshape(channels)
    for ref in vectors:
        ref[...] = take(width).reshape(width)
    inner_ref[...] = take(inner_ref.shape[0]).reshape(inner_ref.shape[0])
    inverse = stats_ref[1:2, :]
    normed = (visual_ref[...].astype(F32) - stats_ref[0:1, :]) * inverse
    grad = grad_bn_ref[...] - shift * (1.0 / count) - normed * (scale * (1.0 / count))
    grad_ref[...] = lines_ref[0:1, :] * inverse * grad
    group = width // 256
    heads = []
    for n in range(12):
        lane = n % group * 256
        heads.append(total[row + n // group : row + n // group + 1, lane : lane + 256])
    heads = jnp.concatenate(heads, 0)
    begin = 0
    for ref, size in zip(tables, levels):
        ref[...] = heads[:, begin : begin + size]
        begin += size


def finish(left, right, grad_bn, visual, stats, lines, inner, levels, count):
    width = left.shape[1]
    channels = visual.shape[1]
    line = lambda n: jax.ShapeDtypeStruct((n,), F32)
    return pl.pallas_call(
        functools.partial(finish_kernel, levels, count),
        out_shape=[line(channels), line(channels), jax.ShapeDtypeStruct(visual.shape, F32)]
        + [line(inner)]
        + [line(width)] * 5
        + [jax.ShapeDtypeStruct((12, n), F32) for n in levels],
        cost_estimate=cost(0, 3_000_000),
        name="finish",
    )(left, right, grad_bn, visual, stats, lines)


def bias_kernel(rows_step, rel_ref, x_ref, y_ref, tab_ref, out_ref, unit_ref, level_ref):
    pairs = out_ref.shape[0]
    table = tab_ref[...]
    top = jnp.max(jnp.max(jnp.abs(table), 1, keepdims=True), 0, keepdims=True)
    top = jnp.maximum(top, 1e-30)
    unit_ref[...] = top * (2.0 / LEVELS)
    level = jnp.floor((table / top + 1.0) * (0.5 * LEVELS) + 0.5).astype(jnp.int32)
    level_ref[0] = level[:, :128]
    level_ref[1] = level[:, 128:]
    words = []
    for n in range(2):
        low = level_ref[n, pl.ds(0, pairs, stride=2), :]
        high = level_ref[n, pl.ds(1, pairs, stride=2), :]
        words.append(low + high * 65536)
    both = [jnp.broadcast_to(words[0][p : p + 1, :], (8, 128)) for p in range(pairs)]
    rel = [jnp.broadcast_to(words[1][p : p + 1, :], (8, 128)) for p in range(pairs)]

    def look(table, index):
        return jnp.take_along_axis(table, index, axis=1, mode="promise_in_bounds")

    for c in range(out_ref.shape[2] // 128):
        for r in range(rows_step // 8):
            rows, cols = pl.ds(r * 8, 8), pl.ds(c * 128, 128)
            rel_id = rel_ref[0, rows, cols] & 31
            x_id = x_ref[0, rows, cols] & 63
            y_id = (y_ref[0, rows, cols] & 63) + 64
            for p in range(pairs):
                out_ref[p, rows, cols] = (
                    look(rel[p], rel_id) + look(both[p], x_id) + look(both[p], y_id)
                )


def bias_words(rel, x, y, table, first, steps):
    step = 64
    rows = steps * step
    pairs = table.shape[0] // 2
    lanes = pl.cdiv(rel.shape[2], 128) * 128
    ids = pl.BlockSpec((1, step, lanes), lambda i: (0, i + first, 0))
    return pl.pallas_call(
        functools.partial(bias_kernel, step),
        grid=(steps,),
        in_specs=[ids, ids, ids, whole(table.shape)],
        out_specs=[pl.BlockSpec((pairs, step, lanes), lambda i: (0, i, 0)), whole((1, 1))],
        out_shape=[
            jax.ShapeDtypeStruct((pairs, rows, lanes), jnp.int32),
            jax.ShapeDtypeStruct((1, 1), F32),
        ],
        scratch_shapes=[pltpu.VMEM((2, table.shape[0], 128), jnp.int32)],
        compiler_params=pltpu.CompilerParams(vmem_limit_bytes=LIMIT),
        cost_estimate=cost(0, 6_000_000 * steps),
        name="bias_words",
    )(rel, x, y, table)


def lane_halves(rows):
    lane = lax.broadcasted_iota(jnp.int32, (rows, 128), 1)
    return lane < 64, lane >= 64


def attend_kernel(unit_ref, q_ref, k_ref, v_ref, col_ref, row_ref, *refs):
    word_refs, (p_ref, o_ref, mask_ref) = refs[:-3], refs[-3:]

    @pl.when(pl.program_id(0) == 0)
    def _():
        mask_ref[...] = jnp.where(col_ref[...] == row_ref[...], 0.0, NEG)

    unit = unit_ref[...]
    rows = q_ref.shape[0]
    halves = lane_halves(rows)
    q, k, v = q_ref[...], k_ref[...], v_ref[...]
    none = jnp.zeros_like(q)
    words = jnp.concatenate([ref[0][:, :rows] for ref in word_refs], 0)
    mask = mask_ref[...]
    mixed = jnp.zeros((rows, 128), F32)
    for h in range(2):
        scores = dot_nt(jnp.where(halves[h], q, none), k)
        word = (words & 0xFFFF) if h == 0 else lax.shift_right_logical(words, 16)
        scores = scores + word.astype(F32) * unit + mask
        expo = jnp.exp(scores - jnp.max(scores, -1, keepdims=True))
        probs = (expo * (1.0 / jnp.sum(expo, -1, keepdims=True))).astype(BF16)
        p_ref[h] = probs
        mixed = mixed + dot_nn(probs, jnp.where(halves[h], v, none))
    o_ref[...] = mixed.astype(BF16)


def attend(unit, qkv, words, segments):
    pairs = words[0].shape[0]
    rows = qkv.shape[0]
    col = [pl.BlockSpec((rows, 128), lambda p, n=n: (0, n * pairs + p)) for n in range(3)]
    flops = pairs * 4 * 2 * rows * rows * 128
    return pl.pallas_call(
        attend_kernel,
        grid=(pairs,),
        in_specs=[
            whole((1, 1)),
            col[0],
            col[1],
            col[2],
            whole((rows, 1)),
            whole((1, rows)),
        ]
        + [pl.BlockSpec((1,) + w.shape[1:], lambda p: (p, 0, 0)) for w in words],
        out_specs=[
            pl.BlockSpec((2, rows, rows), lambda p: (p, 0, 0)),
            pl.BlockSpec((rows, 128), lambda p: (0, p)),
        ],
        out_shape=[
            jax.ShapeDtypeStruct((2 * pairs, rows, rows), BF16),
            jax.ShapeDtypeStruct((rows, pairs * 128), BF16),
        ],
        scratch_shapes=[pltpu.VMEM((rows, rows), F32)],
        compiler_params=pltpu.CompilerParams(vmem_limit_bytes=LIMIT),
        cost_estimate=cost(flops, 40_000_000),
        name="attend",
    )(unit, qkv, qkv, qkv, *segments, *words)


def attend_back_kernel(q_ref, k_ref, v_ref, g_ref, p_ref, ds_ref, dq_ref, dk_ref, dv_ref):
    rows = q_ref.shape[0]
    halves = lane_halves(rows)
    q, k, v, g = q_ref[...], k_ref[...], v_ref[...], g_ref[...]
    none = jnp.zeros_like(q)
    blank = jnp.zeros((rows, ds_ref.shape[2] - rows), BF16)
    dq = jnp.zeros((rows, 128), F32)
    dk, dv = dq, dq
    for h in range(2):
        low = p_ref[h]
        probs = low.astype(F32)
        weighted = probs * dot_nt(g, jnp.where(halves[h], v, none))
        ds = (weighted - probs * jnp.sum(weighted, -1, keepdims=True)).astype(BF16)
        ds_ref[h] = jnp.concatenate([ds, blank], 1)
        dq = dq + dot_nn(ds, jnp.where(halves[h], k, none))
        dv = dv + dot_tn(low, jnp.where(halves[h], g, none))
        dk = dk + dot_tn(ds, jnp.where(halves[h], q, none))
    dq_ref[...] = (dq * 0.125).astype(BF16)
    dk_ref[...] = dk.astype(BF16)
    dv_ref[...] = dv.astype(BF16)


def attend_back(qkv, grad, probs, first, pairs):
    every = probs.shape[0] // 2
    rows = qkv.shape[0]
    col = [pl.BlockSpec((rows, 128), lambda p, n=n: (0, n * every + p + first)) for n in range(3)]
    new = pl.BlockSpec((rows, 128), lambda p: (0, p))
    big = pl.BlockSpec((2, rows, rows), lambda p: (p + first, 0, 0))
    lanes = pl.cdiv(rows, 128) * 128
    out = jax.ShapeDtypeStruct((rows, pairs * 128), BF16)
    flops = pairs * 2 * 4 * 2 * rows * rows * 128
    return pl.pallas_call(
        attend_back_kernel,
        grid=(pairs,),
        in_specs=[col[0], col[1], col[2], col[0], big],
        out_specs=[pl.BlockSpec((2, rows, lanes), lambda p: (p, 0, 0)), new, new, new],
        out_shape=[jax.ShapeDtypeStruct((2 * pairs, rows, lanes), BF16), out, out, out],
        compiler_params=pltpu.CompilerParams(vmem_limit_bytes=LIMIT),
        cost_estimate=cost(flops, 8_000_000 * pairs),
        name="attend_back",
    )(qkv, qkv, qkv, grad, probs)


def table_kernel(first, levels, block_ref, count_ref, rel_ref, x_ref, y_ref, *refs):
    ds_refs, out_ref, rows_ref = refs[:-2], refs[-2], refs[-1]
    place = pl.program_id(0)
    step = rel_ref.shape[1]
    every = rel_ref.shape[2] // 128

    @pl.when(place == 0)
    def _():
        out_ref[...] = jnp.zeros_like(out_ref)
        rows_ref[...] = jnp.zeros_like(rows_ref)

    heads = [(ref, n) for ref in ds_refs for n in range(ref.shape[0])]

    def group(r, start, blocks):
        width = blocks * 128
        level = lax.broadcasted_iota(jnp.int32, (16, width), 0).astype(F32).astype(BF16)
        one = jnp.ones((16, width), BF16)
        none = jnp.zeros((16, width), BF16)

        def one_hot(ids, count):
            wide = jnp.broadcast_to(ids, (16, width)).astype(BF16)
            return [jnp.where(wide == level + BF16(16 * t), one, none) for t in range(count // 16)]

        rows = pl.ds(pl.multiple_of(r * 16, 16), 16)
        lanes = pl.ds(pl.multiple_of(start * 128, 128), width)
        for h, (ref, n) in enumerate(heads):
            values = ref[n, rows, lanes].astype(F32)
            for c in range(blocks):
                rows_ref[c, pl.ds(h, 16, stride=16), :] = values[:, 128 * c : 128 * c + 128]
        total = out_ref[...]
        ids = [ref[0, rows, lanes].astype(F32) for ref in (x_ref, y_ref, rel_ref)]
        counts = (levels[1], levels[2], levels[0])
        for n in range(16):
            grads = jnp.concatenate(
                [rows_ref[c, 16 * n : 16 * n + 16, :].astype(BF16) for c in range(blocks)], 1
            )
            hot = [one_hot(i[n : n + 1], count) for i, count in zip(ids, counts)]
            hot = jnp.concatenate(hot[0] + hot[1] + hot[2], 0)
            total = total + dot_nt(hot, grads)
        out_ref[...] = total

    def body(r, _):
        index = (place + first) * (step // 16) + r
        start, count = block_ref[index], count_ref[index]
        for blocks in range(1, every + 1):

            @pl.when(count == blocks)
            def _(blocks=blocks):
                group(r, start, blocks)

        return 0

    lax.fori_loop(0, step // 16, body, 0)


def table_sums(ranges, rel, x, y, ds, levels, first, steps):
    step = 64
    lanes = ds[0].shape[2]
    ids = pl.BlockSpec((1, step, lanes), lambda i, *_: (0, i + first, 0))
    return pl.pallas_call(
        functools.partial(table_kernel, first, levels),
        grid_spec=pltpu.PrefetchScalarGridSpec(
            num_scalar_prefetch=2,
            grid=(steps,),
            in_specs=[ids, ids, ids]
            + [pl.BlockSpec((d.shape[0], step, lanes), lambda i, *_: (0, i + first, 0)) for d in ds],
            out_specs=whole((sum(levels), 16)),
            scratch_shapes=[pltpu.VMEM((lanes // 128, 256, 128), F32)],
        ),
        out_shape=jax.ShapeDtypeStruct((sum(levels), 16), F32),
        compiler_params=pltpu.CompilerParams(vmem_limit_bytes=LIMIT),
        cost_estimate=cost(0, 8_000_000 * steps),
        name="table_sums",
    )(*ranges, rel, x, y, *ds)


def document_blocks(segments, rows):
    length = segments.shape[0]
    first = segments[0:rows:16]
    last = segments[jnp.minimum(jnp.arange(15, rows, 16), length - 1)]
    begin = jnp.sum(segments[None, :] < first[:, None], 1, dtype=jnp.int32)
    end = jnp.sum(segments[None, :] <= last[:, None], 1, dtype=jnp.int32)
    return begin // 128, (end + 127) // 128 - begin // 128


def norm_stats(values):
    center = values - jnp.mean(values, -1, keepdims=True)
    scale = lax.rsqrt(jnp.mean(center * center, -1, keepdims=True) + EPS)
    return center * scale, scale


def norm_back(grad, normed, scale, gain):
    scaled = grad * gain
    return scale * (
        scaled
        - jnp.mean(scaled, -1, keepdims=True)
        - normed * jnp.mean(scaled * normed, -1, keepdims=True)
    )


def on_device(
    text_hidden,
    visual_maps,
    patch_order,
    segment_ids,
    rel_bucket,
    x_bucket,
    y_bucket,
    bn_scale,
    bn_shift,
    vis_proj,
    w_query,
    w_key,
    w_value,
    w_output,
    rel_table,
    x_table,
    y_table,
    first_gain,
    first_bias,
    w_inner,
    b_inner,
    w_outer,
    b_outer,
    second_gain,
    second_bias,
    cotangent,
):
    heads = rel_table.shape[1]
    pairs = heads // 2
    visual_len = patch_order.shape[1]
    length = segment_ids.shape[1]
    text_len = length - visual_len
    width = w_query.shape[1]
    dp, ffn = lax.axis_size("dp"), lax.axis_size("ffn")
    place, here = lax.axis_index("dp"), lax.axis_index("ffn")
    devices = dp * ffn
    rows = pl.cdiv(length, 64) * 64
    count = visual_maps.shape[0] * devices
    levels = (rel_table.shape[0], x_table.shape[0], y_table.shape[0])

    inner_rows, columns = w_inner.shape
    outer_shard = w_outer.T
    steps = rows // 64

    first_set = Gather(*pack_first(w_query, w_key, w_value, vis_proj, visual_maps))
    plain = columns == width
    wide_shards = jnp.concatenate([outer_shard, w_inner], 0)
    if plain:
        late_set = Gather(
            jnp.concatenate([w_output, wide_shards], 0), [w_output.shape[0], inner_rows, inner_rows]
        )
    else:
        late_set = Gather(w_output, [w_output.shape[0]])
        wide_set = Gather(wide_shards, [inner_rows, inner_rows])

    first_set.along_ffn()
    tables = jnp.concatenate([x_table, y_table, rel_table], 0).T
    tables = jnp.pad(tables, ((0, 0), (0, 256 - tables.shape[1])))
    cuts = [0, steps * 2 // 9, steps * 6 // 9, steps]
    words = [None] * 3
    words[0], unit = bias_words(rel_bucket, x_bucket, y_bucket, tables, 0, cuts[1])
    ranges = document_blocks(segment_ids[0], rows)
    lines = jnp.stack([first_gain, first_bias, b_outer, second_gain, second_bias])
    inner_b = b_inner.reshape(ffn, 1, columns)
    segments = jnp.pad(segment_ids[0], (0, rows - length), constant_values=-1)
    segments = (segments[:, None], segments[None, :])
    bn_lines = jnp.stack([bn_scale, bn_shift])
    state, late, words[0], tables, ranges, lines, inner_b, segments, bn_lines = epoch(
        first_set.state(),
        late_set.state(),
        words[0],
        tables,
        ranges,
        lines,
        inner_b,
        segments,
        bn_lines,
    )
    first_set.hold(state)
    late_set.hold(late)

    first_set.order()
    first_set.near(3 * w_query.shape[0] * ffn)
    late_set.along_ffn(1, ffn - 1)
    words[1], _ = bias_words(rel_bucket, x_bucket, y_bucket, tables, cuts[1], cuts[2] - cuts[1])
    state, late, words[1], tables = epoch(first_set.state(), late_set.state(), words[1], tables)
    first_set.hold(state)
    late_set.hold(late)

    first_set.diagonal()
    late_set.along_ffn(ffn - 1)
    state, late, tables = epoch(first_set.state(), late_set.state(), tables)
    first_set.hold(state)
    late_set.hold(late)

    late_set.order()
    first_set.across()
    state, late = epoch(first_set.state(), late_set.state())
    first_set.hold(state)
    late_set.hold(late)

    late_rows = w_output.shape[0] * ffn
    late_set.near(late_rows + ffn * inner_rows if plain else 0)
    layout, row = [], 0
    for n, size in enumerate(first_set.rows):
        layout.append((row, size * ffn, max(n - 2, 0), 0, n * width if n < 3 else 0))
        row += size * ffn
    order_col = patch_order.reshape(visual_len, 1)
    qkv_full, proj_full, hidden, lowered, qkv, bn_rows, bn_stats = first_rows(
        first_set.parts(),
        layout,
        text_hidden,
        visual_maps,
        order_col,
        bn_lines,
        rows,
        vis_proj.shape[0] * devices,
        first_set.rows[-1],
    )
    qkv, tables = epoch(qkv, tables)
    words[2], _ = bias_words(rel_bucket, x_bucket, y_bucket, tables, cuts[2], cuts[3] - cuts[2])
    qkv, state, words[2] = epoch(qkv, late_set.state(), words[2])
    late_set.hold(state)

    late_set.diagonal()
    probs, mixed = attend(unit, qkv, words, segments)
    probs, mixed, state = epoch(probs, mixed, late_set.state())
    late_set.hold(state)
    late_set.across()
    layout = [(0, late_rows, 0, 0, 0)]
    shift = late_rows
    parts = late_set.parts()
    if not plain:
        parts = [(block, bits, 0) for block, bits, _ in parts]
        wide_set.along_ffn()
        wide_set.order()
        wide_set.near(0)
        wide_set.diagonal()
        wide_set.across()
        shift = 0
    wide_layout = [
        (shift + (n * ffn + f) * inner_rows, inner_rows, 1 + n, f * width, 0)
        for n in range(2)
        for f in range(ffn)
    ]
    feeds = [(parts, layout + wide_layout if plain else layout)]
    if not plain:
        feeds.append((wide_set.parts(), wide_layout))
    (
        first_n,
        first_r,
        output,
        grad_first,
        sums_two,
        inner_sums,
        output_full,
        mine,
        away,
    ) = feed_forward(feeds, mixed, hidden, lines, inner_b, cotangent, inner_rows)

    wide = Scatter(mine, away, lambda value, index: pick(value, index, 1))
    wide.core()
    grad_attn, attn_low, grad_mixed, sums_one = norm_rows(grad_first, first_n, first_r, lines, output_full)
    state, grad_mixed = epoch(wide.held(), grad_mixed)
    wide.hold(state)

    wide.near()
    half = pairs - pairs // 3
    back_low = attend_back(qkv, grad_mixed, probs, 0, half)
    state, back_low, qkv = epoch(wide.held(), back_low, qkv)
    wide.hold(state)
    wide.prepare()
    wide.blocks, qkv = epoch(wide.blocks, qkv)

    wide.quads()
    back_high = attend_back(qkv, grad_mixed, probs, half, pairs - half)
    back = list(zip(back_low[1:], back_high[1:]))
    tokens_grad, mine, away = tail_rows(
        back, qkv_full, grad_attn, attn_low, mixed, lowered, order_col, bn_rows, text_len
    )
    ds = (back_low[0], back_high[0])
    wide.blocks, mine, away, ds, tokens_grad = epoch(wide.blocks, mine, away, ds, tokens_grad)

    def tail_far(value, index):
        size = 4 * (width // dp)
        square = pick(value[:size].reshape(4, ffn, -1, width), index, 1)
        return jnp.concatenate(
            [square.reshape(-1, width), pick(value[size:].reshape(ffn, -1, width), index, 0)], 0
        )

    cuts = [0, steps * 2 // 9, steps * 5 // 9, steps]
    sums = []

    def tables(ds):
        n = len(sums)
        return sums + [
            table_sums(
                ranges, rel_bucket, x_bucket, y_bucket, ds, levels, cuts[n], cuts[n + 1] - cuts[n]
            )
        ]

    tail = Scatter(mine, away, tail_far)
    tail.core()
    wide.join()
    wide.along_ffn(1, 2)
    grad_bn, bn_sums = batch_rows(tokens_grad, visual_maps, bn_stats, proj_full)
    sums = tables(ds)
    state, bn_sums, ds, sums, wide.pieces = epoch(tail.held(), bn_sums, ds, sums, wide.pieces)
    tail.hold(state)

    tail.near()
    if ffn > 2:
        wide.along_ffn(2, 3)
    sums = tables(ds)
    state, ds, sums, wide.pieces = epoch(tail.held(), ds, sums, wide.pieces)
    tail.hold(state)
    tail.prepare()
    tail.blocks, ds = epoch(tail.blocks, ds)

    tail.quads()
    if ffn > 3:
        wide.along_ffn(3)
    sums = tables(ds)
    tail.blocks, sums, back, wide.pieces = epoch(tail.blocks, sums, back, wide.pieces)

    tail.join()
    tail.along_ffn()
    total = Sum(pack_sums(bn_sums, sums_one, sums_two, inner_sums, sums))
    while len(total.steps) > ffn.bit_length() - 1:
        total.step()
    text_grad = text_rows(back, qkv_full, grad_attn, text_len)
    wide_sum = wide.total()
    tail.pieces, total.values = epoch(tail.pieces, total.values)
    tail_sum = tail.total()
    while len(total.steps) > 1:
        total.step()
    other = total.steps[0](total.values)
    (
        shift_grad,
        scale_grad,
        visual_grad,
        inner_grad,
        gain_one,
        bias_one,
        gain_two,
        bias_two,
        outer_grad,
        x_grad,
        y_grad,
        rel_grad,
    ) = finish(
        total.values,
        other,
        grad_bn,
        visual_maps,
        bn_stats,
        bn_lines,
        b_inner.shape[0],
        (levels[1], levels[2], levels[0]),
        count,
    )
    shards, row = [], 0
    for size in [w_query.shape[0]] * 4 + [vis_proj.shape[0]]:
        shards.append(tail_sum[row : row + size])
        row += size
    return (
        output,
        text_grad,
        visual_grad,
        scale_grad.reshape(-1),
        shift_grad.reshape(-1),
        shards[4],
        shards[0],
        shards[1],
        shards[2],
        shards[3],
        rel_grad.T,
        x_grad.T,
        y_grad.T,
        gain_one.reshape(-1),
        bias_one.reshape(-1),
        wide_sum[0],
        inner_grad.reshape(-1),
        wide_sum[1].T,
        outer_grad.reshape(-1),
        gain_two.reshape(-1),
        bias_two.reshape(-1),
    )


def solution(mesh):
    rows = P(ALL, None)
    cube = P(ALL, None, None)
    return jax.shard_map(
        on_device,
        mesh=mesh,
        in_specs=(rows,) * 4
        + (cube,) * 3
        + (P(),) * 2
        + (rows,) * 5
        + (P(),) * 5
        + (P("dp", "ffn"), P(), P("ffn", "dp"))
        + (P(),) * 3
        + (rows,),
        out_specs=(rows,) * 3
        + (P(),) * 2
        + (rows,) * 5
        + (P(),) * 5
        + (P("dp", "ffn"), P(), P("ffn", "dp"))
        + (P(),) * 3,
        check_vma=False,
    )
```

profile of v0, /device:TPU:0, one launch (start us, length us, event | category | flops | bytes accessed | tf_op | source)
XLA Modules:
  0.0 332.1 jit_solution(17074078932008164589)
XLA Ops:
  19.6 6.1 %bias_words.3 = (s32[6,128,640]{2,1,0:T(8,128)}, f32[1,1]{1,0:T(1,128)}) custom-call(s32[1,561,561]{2,1,0:T(8,128)} %copy.88.rel_ref, s32[1,561,561]{2,1,0:T(8,128)} %copy.89.x_ref, s32[1,561,561]{2,1,0:T(8,128)} %copy.90.y_ref, f32[12,256]{1,0:T(8,128)} %pad.8.tab_ref), custom_call_target="tpu_custom_call" | custom-call | bytes 12000 | tf_op jit(solution)/shard_map/bias_words/pallas_call | solution.py:877
  36.3 10.4 %bias_words.4 = (s32[6,256,640]{2,1,0:T(8,128)}, f32[1,1]{1,0:T(1,128)}) custom-call(s32[1,561,561]{2,1,0:T(8,128)} %copy.88.rel_ref, s32[1,561,561]{2,1,0:T(8,128)} %copy.89.x_ref, s32[1,561,561]{2,1,0:T(8,128)} %copy.90.y_ref, f32[12,256]{1,0:T(8,128)} %pad.8.tab_ref), custom_call_target="tpu_custom_call" | custom-call | bytes 24000 | tf_op jit(solution)/shard_map/bias_words/pallas_call | solution.py:877
  46.6 12.6 %collective-permute-done.7.refs_2_ = bf16[216,768]{1,0:T(8,128)(2,1)S(1)} collective-permute-done((bf16[216,768]{1,0:T(8,128)(2,1)S(1)}, bf16[216,768]{1,0:T(8,128)(2,1)S(1)}, u32[]{:S(2)}, u32[]{:S(2)}) %collective-permute-start.7) | collective-permute-done | bytes 331808 | tf_op jit(solution)/shard_map/ppermute | solution.py:42
  62.0 8.7 %collective-permute-done.12.refs_3_ = bf16[216,768]{1,0:T(8,128)(2,1)S(1)} collective-permute-done((bf16[216,768]{1,0:T(8,128)(2,1)S(1)}, bf16[216,768]{1,0:T(8,128)(2,1)S(1)}, u32[]{:S(2)}, u32[]{:S(2)}) %collective-permute-start.12) | collective-permute-done | bytes 331808 | tf_op jit(solution)/shard_map/ppermute | solution.py:42
  81.0 11.2 %first_rows.1 = (bf16[768,2304]{1,0:T(8,128)(2,1)}, bf16[2048,768]{1,0:T(8,128)(2,1)}, f32[576,768]{1,0:T(8,128)}, bf16[576,768]{1,0:T(8,128)(2,1)}, bf16[576,23...) custom-call(s32[10]{0:T(128)} %stack.87.place_ref, bf16[608,768]{1,0:T(8,128)(2,1)} %order_blocks.2.refs_0_, ...), custom_call_target="tpu_custom_call" | custom-call | bytes 25000 | tf_op jit(solution)/shard_map/first_rows/pallas_call | solution.py:394
  92.2 8.2 %bias_words.5 = (s32[6,192,640]{2,1,0:T(8,128)}, f32[1,1]{1,0:T(1,128)}) custom-call(s32[1,561,561]{2,1,0:T(8,128)} %copy.88.rel_ref, s32[1,561,561]{2,1,0:T(8,128)} %copy.89.x_ref, s32[1,561,561]{2,1,0:T(8,128)} %copy.90.y_ref, f32[12,256]{1,0:T(8,128)} %pad.8.tab_ref), custom_call_target="tpu_custom_call" | custom-call | bytes 18000 | tf_op jit(solution)/shard_map/bias_words/pallas_call | solution.py:877
  100.4 9.7 %collective-permute-done.15.refs_2_ = bf16[864,768]{1,0:T(8,128)(2,1)S(1)} collective-permute-done((bf16[864,768]{1,0:T(8,128)(2,1)}, bf16[864,768]{1,0:T(8,128)(2,1)S(1)}, u32[]{:S(2)}, u32[]{:S(2)}) %collective-permute-start.15) | collective-permute-done | bytes 1327136 | tf_op jit(solution)/shard_map/ppermute | solution.py:37
  114.7 14.6 %attend.1 = (bf16[12,576,576]{2,1,0:T(8,128)(2,1)}, bf16[576,768]{1,0:T(8,128)(2,1)}) custom-call(f32[1,1]{1,0:T(1,128)} %get-tuple-element.203.unit_ref, bf16[576,2304]{1,0:T(8,128)(2,1)} %get-tuple-element.298.q_ref.k_ref.v_ref, bf16[576,2304]{1,0:T(8,128)(2,1)} %get-tuple-element.298.q_ref.k_ref.v_ref, ...), custom_call_target="tpu_custom_call" | custom-call | flops 2038431 | bytes 40000 | tf_op jit(solution)/shard_map/attend/pallas_call | solution.py:929
  134.2 36.4 %feed_forward.1 = (f32[576,768]{1,0:T(8,128)}, f32[576,1]{1,0:T(8,128)}, bf16[561,768]{1,0:T(8,128)(2,1)}, f32[576,768]{1,0:T(8,128)}, f32[3,768]{1,0:T(4,128)},...) custom-call(s32[10]{0:T(128)} %stack.87.place_ref, ...), custom_call_target="tpu_custom_call" | custom-call | bytes 100000 | tf_op jit(solution)/shard_map/feed_forward/pallas_call | solution.py:544
  170.8 5.3 %norm_rows.1 = (f32[576,768]{1,0:T(8,128)}, bf16[576,768]{1,0:T(8,128)(2,1)}, bf16[576,768]{1,0:T(8,128)(2,1)}, f32[2,768]{1,0:T(2,128)}) custom-call(f32[576,768]{1,0:T(8,128)} %get-tuple-element.277.grad_ref, f32[576,768]{1,0:T(8,128)} %get-tuple-element.278.normed_ref, f32[576,1]{1,0:T(8,128)} %get-tuple-element.279.scale_ref, ...), custom_call_target="tpu_custom_call" | custom-call | bytes 12000 | tf_op jit(solution)/shard_map/norm_rows/pallas_call | solution.py:596
  182.3 12.0 %attend_back.2 = (bf16[8,576,640]{2,1,0:T(8,128)(2,1)}, bf16[576,512]{1,0:T(8,128)(2,1)}, bf16[576,512]{1,0:T(8,128)(2,1)}, bf16[576,512]{1,0:T(8,128)(2,1)}) custom-call(bf16[576,2304]{1,0:T(8,128)(2,1)} %get-tuple-element.298.q_ref.k_ref.v_ref, bf16[576,2304]{1,0:T(8,128)(2,1)} %get-tuple-element.298.q_ref.k_ref.v_ref, ...), custom_call_target="tpu_custom_call" | custom-call | flops 2717908 | bytes 32000 | tf_op jit(solution)/shard_map/attend_back/pallas_call | solution.py:987
  201.6 7.1 %attend_back.3 = (bf16[4,576,640]{2,1,0:T(8,128)(2,1)}, bf16[576,256]{1,0:T(8,128)(2,1)}, bf16[576,256]{1,0:T(8,128)(2,1)}, bf16[576,256]{1,0:T(8,128)(2,1)}) custom-call(bf16[576,2304]{1,0:T(8,128)(2,1)} %get-tuple-element.298.q_ref.k_ref.v_ref, bf16[576,2304]{1,0:T(8,128)(2,1)} %get-tuple-element.298.q_ref.k_ref.v_ref, ...), custom_call_target="tpu_custom_call" | custom-call | flops 1358954 | bytes 16000 | tf_op jit(solution)/shard_map/attend_back/pallas_call | solution.py:987
  208.7 14.4 %tail_rows.1 = (bf16[49,768]{1,0:T(8,128)(2,1)}, bf16[4,640,768]{2,1,0:T(8,128)(2,1)}, bf16[4,640,768]{2,1,0:T(8,128)(2,1)}) custom-call(s32[2]{0:T(128)} %pad_add_fusion.core_ref.place_ref, bf16[576,512]{1,0:T(8,128)(2,1)} %get-tuple-element.348.refs_0_, bf16[576,256]{1,0:T(8,128)(2,1)} %get-tuple-element.349.refs_1_, ...), custom_call_target="tpu_custom_call" | custom-call | bytes 40000 | tf_op jit(solution)/shard_map/tail_rows/pallas_call | solution.py:678
  223.1 3.5 %collective-permute-done.27 = bf16[2,4,96,768]{3,2,1,0:T(8,128)(2,1)S(1)} collective-permute-done((bf16[2,4,96,768]{3,2,1,0:T(8,128)(2,1)S(1)}, bf16[2,4,96,768]{3,2,1,0:T(8,128)(2,1)S(1)}, u32[]{:S(2)}, u32[]{:S(2)}) %collective-permute-start.27) | collective-permute-done | bytes 1179680 | tf_op jit(solution)/shard_map/ppermute | solution.py:37
  230.1 3.9 %batch_rows.1 = (f32[49,2048]{1,0:T(8,128)}, f32[2,2048]{1,0:T(2,128)}) custom-call(bf16[49,768]{1,0:T(8,128)(2,1)} %get-tuple-element.316.tokens_ref, bf16[49,2048]{1,0:T(8,128)(2,1)} %refs_3_.1, f32[2,2048]{1,0:T(2,128)} %get-tuple-element.317.stats_ref.refs_4_, bf16[2048,768]{1,0:T(8,128)(2,1)} %get-tuple-element.318.proj_ref), custom_call_target="tpu_custom_call" | custom-call | bytes 6000 | tf_op jit(solution)/shard_map/batch_rows/pallas_call | solution.py:708
  234.0 7.8 %table_sums.3.refs_0_ = f32[160,16]{1,0:T(8,128)} custom-call(s32[36]{0:T(128)} %get-tuple-element.322.block_ref, s32[36]{0:T(128)} %get-tuple-element.323.count_ref, s32[1,561,561]{2,1,0:T(8,128)} %copy.88.rel_ref, s32[1,561,561]{2,1,0:T(8,128)} %copy.89.x_ref, s32[1,561,561]{2,1,0:T(8,128)} %copy.90.y_ref, ...), custom_call_target="tpu_custom_call" | custom-call | bytes 16000 | tf_op jit(solution)/shard_map/table_sums/pallas_call | solution.py:1058
  248.3 10.7 %table_sums.4.refs_1_ = f32[160,16]{1,0:T(8,128)} custom-call(s32[36]{0:T(128)} %get-tuple-element.322.block_ref, s32[36]{0:T(128)} %get-tuple-element.323.count_ref, s32[1,561,561]{2,1,0:T(8,128)} %copy.88.rel_ref, s32[1,561,561]{2,1,0:T(8,128)} %copy.89.x_ref, s32[1,561,561]{2,1,0:T(8,128)} %copy.90.y_ref, ...), custom_call_target="tpu_custom_call" | custom-call | bytes 24000 | tf_op jit(solution)/shard_map/table_sums/pallas_call | solution.py:1058
  259.0 4.1 %collective-permute-done.33 = bf16[2,96,768]{2,1,0:T(8,128)(2,1)S(1)} collective-permute-done((bf16[2,96,768]{2,1,0:T(8,128)(2,1)S(1)}, bf16[2,96,768]{2,1,0:T(8,128)(2,1)S(1)}, u32[]{:S(2)}, u32[]{:S(2)}) %collective-permute-start.33) | collective-permute-done | bytes 294944 | tf_op jit(solution)/shard_map/ppermute | solution.py:42
  269.8 15.5 %table_sums.5.refs_2_ = f32[160,16]{1,0:T(8,128)} custom-call(s32[36]{0:T(128)} %get-tuple-element.322.block_ref, s32[36]{0:T(128)} %get-tuple-element.323.count_ref, s32[1,561,561]{2,1,0:T(8,128)} %copy.88.rel_ref, s32[1,561,561]{2,1,0:T(8,128)} %copy.89.x_ref, s32[1,561,561]{2,1,0:T(8,128)} %copy.90.y_ref, ...), custom_call_target="tpu_custom_call" | custom-call | bytes 32000 | tf_op jit(solution)/shard_map/table_sums/pallas_call | solution.py:1058
  285.2 4.9 %collective-permute-done.34 = bf16[640,768]{1,0:T(8,128)(2,1)S(1)} collective-permute-done((bf16[640,768]{1,0:T(8,128)(2,1)}, bf16[640,768]{1,0:T(8,128)(2,1)S(1)}, u32[]{:S(2)}, u32[]{:S(2)}) %collective-permute-start.34) | collective-permute-done | bytes 983072 | tf_op jit(solution)/shard_map/ppermute | solution.py:37
  299.6 5.8 %text_rows.1 = f32[512,768]{1,0:T(8,128)} custom-call(bf16[576,512]{1,0:T(8,128)(2,1)} %get-tuple-element.348.refs_0_, bf16[576,256]{1,0:T(8,128)(2,1)} %get-tuple-element.349.refs_1_, bf16[576,512]{1,0:T(8,128)(2,1)} %get-tuple-element.350.refs_2_, bf16[576,256]{1,0:T(8,128)(2,1)} %get-tuple-element.351.refs_3_, ...), custom_call_target="tpu_custom_call" | custom-call | bytes 25000 | tf_op jit(solution)/shard_map/text_rows/pallas_call | solution.py:735
  306.2 3.7 %collective-permute-done.42 = f32[24,768]{1,0:T(8,128)S(1)} collective-permute-done((f32[24,768]{1,0:T(8,128)S(1)}, f32[24,768]{1,0:T(8,128)S(1)}, u32[]{:S(2)}, u32[]{:S(2)}) %collective-permute-start.42) | collective-permute-done | bytes 73760 | tf_op jit(solution)/shard_map/ppermute | solution.py:37
  309.9 9.2 %collective-permute-done.38 = bf16[160,768]{1,0:T(8,128)(2,1)S(1)} collective-permute-done((bf16[160,768]{1,0:T(8,128)(2,1)S(1)}, bf16[160,768]{1,0:T(8,128)(2,1)S(1)}, u32[]{:S(2)}, u32[]{:S(2)}) %collective-permute-start.38) | collective-permute-done | bytes 245792 | tf_op jit(solution)/shard_map/ppermute | solution.py:42
  319.2 4.2 %collective-permute-done.43 = f32[24,768]{1,0:T(8,128)S(1)} collective-permute-done((f32[24,768]{1,0:T(8,128)S(1)}, f32[24,768]{1,0:T(8,128)S(1)}, u32[]{:S(2)}, u32[]{:S(2)}) %collective-permute-start.43) | collective-permute-done | bytes 73760 | tf_op jit(solution)/shard_map/ppermute | solution.py:47
  (227 shorter events, 100.7 us)
Async XLA Ops:
  2.7 24.3 %collective-permute-start = (bf16[152,768]{1,0:T(8,128)(2,1)}, bf16[152,768]{1,0:T(8,128)(2,1)S(1)}, u32[]{:S(2)}, u32[]{:S(2)}) collective-permute-start(bf16[152,768]{1,0:T(8,128)(2,1)} %pack_first.1.refs_0_), channel_id=1, source_target_pairs={{0,1},{1,2},{2,3},{3,0},{4,5},{5,6},{6,7},{7,4},{8,9},{9,10},{10,1... | collective-permute-start | bytes 700424 | tf_op jit(solution)/shard_map/ppermute | solution.py:42
  5.7 21.3 %collective-permute-start.1 = (bf16[152,768]{1,0:T(8,128)(2,1)}, bf16[152,768]{1,0:T(8,128)(2,1)}, u32[]{:S(2)}, u32[]{:S(2)}) collective-permute-start(bf16[152,768]{1,0:T(8,128)(2,1)} %pack_first.1.refs_0_), channel_id=1, source_target_pairs={{0,2},{1,3},{2,0},{3,1},{4,6},{5,7},{6,4},{7,5},{8,10},{9,11},{10,... | collective-permute-start | bytes 700424 | tf_op jit(solution)/shard_map/ppermute | solution.py:42
  8.3 18.7 %collective-permute-start.2 = (bf16[152,768]{1,0:T(8,128)(2,1)}, bf16[152,768]{1,0:T(8,128)(2,1)}, u32[]{:S(2)}, u32[]{:S(2)}) collective-permute-start(bf16[152,768]{1,0:T(8,128)(2,1)} %pack_first.1.refs_0_), channel_id=1, source_target_pairs={{0,3},{1,0},{2,1},{3,2},{4,7},{5,4},{6,5},{7,6},{8,11},{9,8},{10,9... | collective-permute-start | bytes 700424 | tf_op jit(solution)/shard_map/ppermute | solution.py:42
  30.0 29.2 %collective-permute-start.3 = (bf16[608,768]{1,0:T(8,128)(2,1)}, bf16[608,768]{1,0:T(8,128)(2,1)S(1)}, u32[]{:S(2)}, u32[]{:S(2)}) collective-permute-start(bf16[608,768]{1,0:T(8,128)(2,1)} %order_blocks.2.refs_0_), channel_id=1, source_target_pairs={{0,8},{4,12},{8,0},{12,4},{16,24},{20,28},{24,16},{28,20},{1,9},{5... | collective-permute-start | bytes 2801672 | tf_op jit(solution)/shard_map/ppermute | solution.py:37
  31.5 27.8 %collective-permute-start.4 = (bf16[608,768]{1,0:T(8,128)(2,1)}, bf16[608,768]{1,0:T(8,128)(2,1)S(1)}, u32[]{:S(2)}, u32[]{:S(2)}) collective-permute-start(bf16[608,768]{1,0:T(8,128)(2,1)} %order_blocks.2.refs_0_), channel_id=1, source_target_pairs={{0,16},{4,20},{8,24},{12,28},{16,0},{20,4},{24,8},{28,12},{1,17},{... | collective-permute-start | bytes 2801672 | tf_op jit(solution)/shard_map/ppermute | solution.py:37
  33.0 26.3 %collective-permute-start.5 = (bf16[608,768]{1,0:T(8,128)(2,1)}, bf16[608,768]{1,0:T(8,128)(2,1)S(1)}, u32[]{:S(2)}, u32[]{:S(2)}) collective-permute-start(bf16[608,768]{1,0:T(8,128)(2,1)} %order_blocks.2.refs_0_), channel_id=1, source_target_pairs={{0,4},{4,0},{8,12},{12,8},{16,20},{20,16},{24,28},{28,24},{1,5},{5... | collective-permute-start | bytes 2801672 | tf_op jit(solution)/shard_map/ppermute | solution.py:37
  34.7 24.5 %collective-permute-start.7 = (bf16[216,768]{1,0:T(8,128)(2,1)S(1)}, bf16[216,768]{1,0:T(8,128)(2,1)S(1)}, u32[]{:S(2)}, u32[]{:S(2)}) collective-permute-start(bf16[216,768]{1,0:T(8,128)(2,1)S(1)} %pad_maximum_fusion.4.refs_0_), channel_id=1, source_target_pairs={{0,2},{1,3},{2,0},{3,1},{4,6},{5,7},{6,4},{7,5},{8,10},{9,11},{10,... | collective-permute-start | bytes 995336 | tf_op jit(solution)/shard_map/ppermute | solution.py:42
  78.3 31.7 %collective-permute-start.15 = (bf16[864,768]{1,0:T(8,128)(2,1)}, bf16[864,768]{1,0:T(8,128)(2,1)S(1)}, u32[]{:S(2)}, u32[]{:S(2)}) collective-permute-start(bf16[864,768]{1,0:T(8,128)(2,1)} %order_blocks.3.refs_0_), channel_id=1, source_target_pairs={{0,8},{4,12},{8,0},{12,4},{16,24},{20,28},{24,16},{28,20},{1,9},{5... | collective-permute-start | bytes 3981320 | tf_op jit(solution)/shard_map/ppermute | solution.py:37
  79.1 31.5 %collective-permute-start.16 = (bf16[864,768]{1,0:T(8,128)(2,1)}, bf16[864,768]{1,0:T(8,128)(2,1)S(1)}, u32[]{:S(2)}, u32[]{:S(2)}) collective-permute-start(bf16[864,768]{1,0:T(8,128)(2,1)} %order_blocks.3.refs_0_), channel_id=1, source_target_pairs={{0,16},{4,20},{8,24},{12,28},{16,0},{20,4},{24,8},{28,12},{1,17},{... | collective-permute-start | bytes 3981320 | tf_op jit(solution)/shard_map/ppermute | solution.py:37
  79.6 31.0 %collective-permute-start.17 = (bf16[864,768]{1,0:T(8,128)(2,1)}, bf16[864,768]{1,0:T(8,128)(2,1)}, u32[]{:S(2)}, u32[]{:S(2)}) collective-permute-start(bf16[864,768]{1,0:T(8,128)(2,1)} %order_blocks.3.refs_0_), channel_id=1, source_target_pairs={{0,4},{4,0},{8,12},{12,8},{16,20},{20,16},{24,28},{28,24},{1,5},{5... | collective-permute-start | bytes 3981320 | tf_op jit(solution)/shard_map/ppermute | solution.py:37
  110.6 19.2 %collective-permute-start.20 = (bf16[864,768]{1,0:T(8,128)(2,1)S(1)}, bf16[864,768]{1,0:T(8,128)(2,1)}, u32[]{:S(2)}, u32[]{:S(2)}) collective-permute-start(bf16[864,768]{1,0:T(8,128)(2,1)S(1)} %collective-permute-done.15.refs_2_), channel_id=1, source_target_pairs={{0,4},{4,0},{8,12},{12,8},{16,20},{20,16},{24,28},{28,24},{1,5},{5... | collective-permute-start | bytes 3981320 | tf_op jit(solution)/shard_map/ppermute | solution.py:37
  110.6 19.2 %collective-permute-start.21 = (bf16[864,768]{1,0:T(8,128)(2,1)S(1)}, bf16[864,768]{1,0:T(8,128)(2,1)}, u32[]{:S(2)}, u32[]{:S(2)}) collective-permute-start(bf16[864,768]{1,0:T(8,128)(2,1)S(1)} %collective-permute-done.16.refs_4_), channel_id=1, source_target_pairs={{0,4},{4,0},{8,12},{12,8},{16,20},{20,16},{24,28},{28,24},{1,5},{5... | collective-permute-start | bytes 3981320 | tf_op jit(solution)/shard_map/ppermute | solution.py:37
  111.2 18.6 %collective-permute-start.18 = (bf16[480,768]{1,0:T(8,128)(2,1)S(1)}, bf16[480,768]{1,0:T(8,128)(2,1)}, u32[]{:S(2)}, u32[]{:S(2)}) collective-permute-start(bf16[480,768]{1,0:T(8,128)(2,1)S(1)} %slice.163), channel_id=1, source_target_pairs={{0,16},{4,20},{8,24},{12,28},{16,0},{20,4},{24,8},{28,12},{1,17},{... | collective-permute-start | bytes 2211848 | tf_op jit(solution)/shard_map/ppermute | solution.py:37
  112.6 16.7 %collective-permute-start.19 = (bf16[384,768]{1,0:T(8,128)(2,1)}, bf16[384,768]{1,0:T(8,128)(2,1)}, u32[]{:S(2)}, u32[]{:S(2)}) collective-permute-start(bf16[384,768]{1,0:T(8,128)(2,1)} %slice.164), channel_id=1, source_target_pairs={{0,8},{4,12},{8,0},{12,4},{16,24},{20,28},{24,16},{28,20},{1,9},{5... | collective-permute-start | bytes 1769480 | tf_op jit(solution)/shard_map/ppermute | solution.py:37
  199.6 26.9 %collective-permute-start.27 = (bf16[2,4,96,768]{3,2,1,0:T(8,128)(2,1)S(1)}, bf16[2,4,96,768]{3,2,1,0:T(8,128)(2,1)S(1)}, u32[]{:S(2)}, u32[]{:S(2)}) collective-permute-start(bf16[2,4,96,768]{3,2,1,0:T(8,128)(2,1)S(1)} %pad_maximum_fusion), channel_id=1, source_target_pairs={{0,8},{4,12},{8,0},{12,4},{16,24},{20,28},{24,16},{28,20},{1,9},{5... | collective-permute-start | bytes 3538952 | tf_op jit(solution)/shard_map/ppermute | solution.py:37
  200.5 26.6 %collective-permute-start.28 = (bf16[2,4,96,768]{3,2,1,0:T(8,128)(2,1)S(1)}, bf16[2,4,96,768]{3,2,1,0:T(8,128)(2,1)S(1)}, u32[]{:S(2)}, u32[]{:S(2)}) collective-permute-start(bf16[2,4,96,768]{3,2,1,0:T(8,128)(2,1)S(1)} %pad_maximum_fusion.1), channel_id=1, source_target_pairs={{0,16},{4,20},{8,24},{12,28},{16,0},{20,4},{24,8},{28,12},{1,17},{... | collective-permute-start | bytes 3538952 | tf_op jit(solution)/shard_map/ppermute | solution.py:37
  243.3 19.8 %collective-permute-start.31 = (bf16[320,768]{1,0:T(8,128)(2,1)S(1)}, bf16[320,768]{1,0:T(8,128)(2,1)S(1)}, u32[]{:S(2)}, u32[]{:S(2)}) collective-permute-start(bf16[320,768]{1,0:T(8,128)(2,1)S(1)} %get-tuple-element.396), channel_id=1, source_target_pairs={{0,8},{4,12},{8,0},{12,4},{16,24},{20,28},{24,16},{28,20},{1,9},{5... | collective-permute-start | bytes 1474568 | tf_op jit(solution)/shard_map/ppermute | solution.py:37
  246.3 16.8 %collective-permute-start.32 = (bf16[320,768]{1,0:T(8,128)(2,1)S(1)}, bf16[320,768]{1,0:T(8,128)(2,1)S(1)}, u32[]{:S(2)}, u32[]{:S(2)}) collective-permute-start(bf16[320,768]{1,0:T(8,128)(2,1)S(1)} %get-tuple-element.395), channel_id=1, source_target_pairs={{0,16},{4,20},{8,24},{12,28},{16,0},{20,4},{24,8},{28,12},{1,17},{... | collective-permute-start | bytes 1474568 | tf_op jit(solution)/shard_map/ppermute | solution.py:37
  247.0 16.1 %collective-permute-start.33 = (bf16[2,96,768]{2,1,0:T(8,128)(2,1)S(1)}, bf16[2,96,768]{2,1,0:T(8,128)(2,1)S(1)}, u32[]{:S(2)}, u32[]{:S(2)}) collective-permute-start(bf16[2,96,768]{2,1,0:T(8,128)(2,1)S(1)} %get-tuple-element.398), channel_id=1, source_target_pairs={{0,2},{1,3},{2,0},{3,1},{4,6},{5,7},{6,4},{7,5},{8,10},{9,11},{10,... | collective-permute-start | bytes 884744 | tf_op jit(solution)/shard_map/ppermute | solution.py:42
  266.7 23.5 %collective-permute-start.34 = (bf16[640,768]{1,0:T(8,128)(2,1)}, bf16[640,768]{1,0:T(8,128)(2,1)S(1)}, u32[]{:S(2)}, u32[]{:S(2)}) collective-permute-start(bf16[640,768]{1,0:T(8,128)(2,1)} %pad_maximum_fusion.2), channel_id=1, source_target_pairs={{0,8},{4,12},{8,0},{12,4},{16,24},{20,28},{24,16},{28,20},{1,9},{5... | collective-permute-start | bytes 2949128 | tf_op jit(solution)/shard_map/ppermute | solution.py:37
  267.5 23.5 %collective-permute-start.35 = (bf16[640,768]{1,0:T(8,128)(2,1)S(1)}, bf16[640,768]{1,0:T(8,128)(2,1)S(1)}, u32[]{:S(2)}, u32[]{:S(2)}) collective-permute-start(bf16[640,768]{1,0:T(8,128)(2,1)S(1)} %pad_maximum_fusion.3), channel_id=1, source_target_pairs={{0,16},{4,20},{8,24},{12,28},{16,0},{20,4},{24,8},{28,12},{1,17},{... | collective-permute-start | bytes 2949128 | tf_op jit(solution)/shard_map/ppermute | solution.py:37
  268.4 16.9 %collective-permute-start.36 = (bf16[2,96,768]{2,1,0:T(8,128)(2,1)S(1)}, bf16[2,96,768]{2,1,0:T(8,128)(2,1)S(1)}, u32[]{:S(2)}, u32[]{:S(2)}) collective-permute-start(bf16[2,96,768]{2,1,0:T(8,128)(2,1)S(1)} %copy-done.27), channel_id=1, source_target_pairs={{0,3},{1,0},{2,1},{3,2},{4,7},{5,4},{6,5},{7,6},{8,11},{9,8},{10,9... | collective-permute-start | bytes 884744 | tf_op jit(solution)/shard_map/ppermute | solution.py:42
  296.4 22.6 %collective-permute-start.38 = (bf16[160,768]{1,0:T(8,128)(2,1)S(1)}, bf16[160,768]{1,0:T(8,128)(2,1)S(1)}, u32[]{:S(2)}, u32[]{:S(2)}) collective-permute-start(bf16[160,768]{1,0:T(8,128)(2,1)S(1)} %pad_maximum_fusion.7), channel_id=1, source_target_pairs={{0,2},{1,3},{2,0},{3,1},{4,6},{5,7},{6,4},{7,5},{8,10},{9,11},{10,... | collective-permute-start | bytes 737288 | tf_op jit(solution)/shard_map/ppermute | solution.py:42
  297.0 22.0 %collective-permute-start.37 = (bf16[160,768]{1,0:T(8,128)(2,1)S(1)}, bf16[160,768]{1,0:T(8,128)(2,1)S(1)}, u32[]{:S(2)}, u32[]{:S(2)}) collective-permute-start(bf16[160,768]{1,0:T(8,128)(2,1)S(1)} %pad_maximum_fusion.6), channel_id=1, source_target_pairs={{0,1},{1,2},{2,3},{3,0},{4,5},{5,6},{6,7},{7,4},{8,9},{9,10},{10,1... | collective-permute-start | bytes 737288 | tf_op jit(solution)/shard_map/ppermute | solution.py:42
  (59 other events, 481.3 us)
where the time goes:
time: 337 us; the launch traced here: 332 us
  Pallas kernels  180 us (53%)
  waiting for transfers between devices  75.6 us (22%)
  starting transfers between devices  38.1 us (11%)
  local copies, waits for them, and re-layouts  18.4 us (5%)
  other arithmetic  18 us (5%)
    pallas_call x1, Pallas kernels, feed_forward(): pl.pallas_call(functools.partial(feed_kernel, entries, len(parts), ct.sha...  36.4 us
    ppermute x12, waiting for transfers between devices, send_ffn(): lax.ppermute(values, 'ffn', [(i, (i + shift) % size) for i in range(size)])  34.5 us
    ppermute x31, waiting for transfers between devices, send_dp(): return lax.ppermute(values, 'dp', [(i, i ^ bits) for i in range(size)])  34.5 us
    pallas_call x3, Pallas kernels, table_sums(): pl.pallas_call(functools.partial(table_kernel, first, levels), grid_spec=...  34 us
    pallas_call x3, Pallas kernels, bias_words(): pl.pallas_call(functools.partial(bias_kernel, step), grid=(steps,), in_sp...  24.7 us
    ppermute x31, starting transfers between devices, send_dp(): return lax.ppermute(values, 'dp', [(i, i ^ bits) for i in range(size)])  20.6 us
    pallas_call x2, Pallas kernels, attend_back(): pl.pallas_call(attend_back_kernel, grid=(pairs,), in_specs=[col[0], col[1...  19.1 us
    ppermute x12, starting transfers between devices, send_ffn(): lax.ppermute(values, 'ffn', [(i, (i + shift) % size) for i in range(size)])  15.7 us
  transfers between devices with their start and end apart: 45, of which 20 were waited for; matrix products, arithmetic and copies ran while one was open for 6% of the time, Pallas kernels for 41%

commit v1 on v0

--- a/solution.py
+++ b/solution.py
@@ -49,7 +49,7 @@
 
 def exchanges():
     steps = []
-    for axis, send in (("dp", send_dp), ("ffn", swap_ffn)):
+    for axis, send in (("ffn", swap_ffn), ("dp", send_dp)):
         bit = 1
         while bit < lax.axis_size(axis):
             steps.append(functools.partial(send, bits=bit))
@@ -276,6 +276,7 @@
         + [pl.BlockSpec(memory_space=pltpu.VMEM)] * len(parts),
         out_specs=pl.BlockSpec(memory_space=pltpu.VMEM),
         out_shape=jax.ShapeDtypeStruct((len(parts) * sum(rows), width), BF16),
+        compiler_params=pltpu.CompilerParams(vmem_limit_bytes=LIMIT),
         name="order_blocks",
     )(here.reshape(1).astype(jnp.int32), *parts)
 
@@ -433,33 +434,40 @@
 
 def feed_kernel(entries, count, length, ffn, place_ref, core_ref, *refs):
     parts, refs = refs[:count], refs[count:]
-    mixed_ref, hidden_ref, lines_ref, inner_b_ref, ct_ref = refs[:5]
-    normed_ref, scale_ref, output_ref, total_ref, sums_ref, inner_sums_ref = refs[5:11]
-    out_w_ref, mine_ref, away_ref = refs[11:14]
-    outer_w_ref, inner_w_ref, act_ref, slope_ref, first_ref, low_ref = refs[14:20]
-    first_turned, low_turned, sems = refs[20:]
+    inputs, (lines_ref, inner_b_ref), refs = refs[:3], refs[3:5], refs[5:]
+    results, (scale_ref, total_ref, sums_ref, inner_sums_ref), refs = refs[:3], refs[3:7], refs[7:]
+    mine_ref, away_ref = refs[:2]
+    outer_w_ref, inner_w_ref, act_ref, slope_ref, first_ref, low_ref = refs[2:8]
+    first_turned, low_turned = refs[8:10]
+    mixed_ref, hidden_ref, ct_ref, normed_ref, out_w_ref, output_ref = refs[10:16]
+    sems, in_sems, out_sems = refs[16:]
     step = pl.program_id(0)
     width = hidden_ref.shape[1]
     outs = (out_w_ref, outer_w_ref, inner_w_ref)
+    fetch = [
+        pltpu.make_async_copy(source, target, in_sems.at[n])
+        for n, (source, target) in enumerate(zip(inputs, (mixed_ref, hidden_ref, ct_ref)))
+    ]
+    leave = [
+        pltpu.make_async_copy(source, target, out_sems.at[n])
+        for n, (source, target) in enumerate(zip((normed_ref, out_w_ref, output_ref), results))
+    ]
     gain1, bias1, outer_b, gain2, bias2 = [lines_ref[n : n + 1, :] for n in range(5)]
 
     @pl.when(step == 0)
     def _():
-        for copy in part_copies(entries, place_ref, parts, outs, sems):
+        copies = part_copies(entries, place_ref, parts, outs, sems)
+        square = [copy for entry, copy in zip(entries, copies) if entry[3] == 0]
+        now = [copy for entry, copy in zip(entries, copies) if entry[3] > 0 and entry[4] == 0]
+        later = [copy for entry, copy in zip(entries, copies) if entry[3] > 0 and entry[4] > 0]
+        for copy in [fetch[0]] + square + [fetch[1]] + now:
             copy.start()
-
-    for index in range(ffn):
-
-        @pl.when(step == index)
-        def _(index=index):
-            copies = part_copies(entries, place_ref, parts, outs, sems)
-            for (_, _, _, out, base, _), copy in zip(entries, copies):
-                if (out == 0 and index == 0) or (out > 0 and base == index * width):
-                    copy.wait()
-
-    @pl.when(step == 0)
-    def _():
+        for copy in [fetch[0]] + square:
+            copy.wait()
+        for copy in later + [fetch[2], leave[1]]:
+            copy.start()
         attended = dot_nn(mixed_ref[...], out_w_ref[...])
+        fetch[1].wait()
         normed, scale = norm_stats(hidden_ref[...] + attended)
         first = normed * gain1 + bias1
         normed_ref[...] = normed
@@ -468,6 +476,16 @@
         first_ref[...] = low
         total_ref[...] = first + outer_b
         first_turned[...] = low.T
+        leave[0].start()
+
+    for index in range(ffn):
+
+        @pl.when(step == index)
+        def _(index=index):
+            copies = part_copies(entries, place_ref, parts, outs, sems)
+            for entry, copy in zip(entries, copies):
+                if entry[3] > 0 and entry[4] == index * width:
+                    copy.wait()
 
     @pl.when(step < ffn)
     def _():
@@ -485,10 +503,13 @@
 
     @pl.when(step == ffn - 1)
     def _():
+        fetch[2].wait()
         normed, scale = norm_stats(total_ref[...])
-        output_ref[...] = (normed * gain2 + bias2).astype(BF16)
+        output_ref[...] = (normed * gain2 + bias2).astype(BF16)[:length]
+        leave[2].start()
         row = lax.broadcasted_iota(jnp.int32, (normed.shape[0], 1), 0)
-        ct = jnp.where(row < length, ct_ref[...].astype(F32), 0.0)
+        blank = jnp.zeros((normed.shape[0] - length, width), BF16)
+        ct = jnp.concatenate([ct_ref[...], blank], 0).astype(F32)
         grad = norm_back(ct, normed, scale, gain2)
         total_ref[...] = grad
         low = grad.astype(BF16)
@@ -515,6 +536,11 @@
             ref[slot, 1, 0] = outer[dp * size : (dp + 1) * size]
 
         store_blocks(mine_ref, away_ref, core_ref[0], core_ref[1], store)
+
+    @pl.when(step == 2 * ffn - 1)
+    def _():
+        for copy in leave:
+            copy.wait()
 
 
 def feed_forward(feeds, mixed, hidden, lines, inner_b, ct, inner_rows):
@@ -534,22 +560,23 @@
     smem = pl.BlockSpec(memory_space=pltpu.SMEM)
     shapes = [
         ((rows, width), F32),
+        ((width, width), BF16),
+        (ct.shape, BF16),
         ((rows, 1), F32),
-        (ct.shape, BF16),
         ((rows, width), F32),
         ((3, width), F32),
         ((ffn, 1, columns), F32),
-        ((width, width), BF16),
     ]
+    anywhere = pl.BlockSpec(memory_space=pl.ANY)
     return pl.pallas_call(
         functools.partial(feed_kernel, entries, len(parts), ct.shape[0], ffn),
         grid=(2 * ffn,),
         in_specs=[smem, smem]
-        + [pl.BlockSpec(memory_space=pl.ANY)] * len(parts)
-        + [square, square, whole(lines.shape), whole(inner_b.shape), square],
-        out_specs=[square, whole((rows, 1)), square, square, whole((3, width))]
-        + [pl.BlockSpec((1, 1, columns), lambda i: (back(i), 0, 0)), whole((width, width))]
-        + [block, block],
+        + [anywhere] * (len(parts) + 3)
+        + [whole(lines.shape), whole(inner_b.shape)],
+        out_specs=[anywhere] * 3
+        + [whole((rows, 1)), square, whole((3, width))]
+        + [pl.BlockSpec((1, 1, columns), lambda i: (back(i), 0, 0)), block, block],
         out_shape=[jax.ShapeDtypeStruct(*shape) for shape in shapes] + [blocks, blocks],
         scratch_shapes=[
             pltpu.VMEM((ffn * width, columns), BF16),
@@ -560,7 +587,15 @@
             pltpu.VMEM((rows, width), BF16),
             pltpu.VMEM((width, rows), BF16),
             pltpu.VMEM((width, rows), BF16),
+            pltpu.VMEM((rows, width), BF16),
+            pltpu.VMEM((rows, width), F32),
+            pltpu.VMEM(ct.shape, BF16),
+            pltpu.VMEM((rows, width), F32),
+            pltpu.VMEM((width, width), BF16),
+            pltpu.VMEM(ct.shape, BF16),
             pltpu.SemaphoreType.DMA((len(entries),)),
+            pltpu.SemaphoreType.DMA((3,)),
+            pltpu.SemaphoreType.DMA((3,)),
         ],
         compiler_params=pltpu.CompilerParams(vmem_limit_bytes=LIMIT),
         cost_estimate=cost(0, 100_000_000),
@@ -571,9 +606,9 @@
         *[part for part, _, _ in parts],
         mixed,
         hidden,
+        ct,
         lines,
         inner_b,
-        ct,
     )
 
 
@@ -753,7 +788,7 @@
     return [values[:, n * width : (n + 1) * width] for n in range(pieces)]
 
 
-def sums_kernel(bn_ref, one_ref, two_ref, inner_ref, *refs):
+def sums_kernel(half_levels, bn_ref, one_ref, two_ref, inner_ref, *refs):
     out_ref = refs[-1]
     width = out_ref.shape[1]
     rows = []
@@ -763,7 +798,13 @@
         rows += [ref[n : n + 1, :] for n in range(ref.shape[0])]
     inner = [inner_ref[n] for n in range(inner_ref.shape[0])]
     rows += lane_rows(jnp.concatenate(inner, 1), width)
-    tables = sum(ref[...] for ref in refs[:-1]).T
+    halves = sum(ref[...] for ref in refs[:-1])
+    tables, lane = [], 0
+    for n, size in enumerate(half_levels):
+        for row in (32 * n, 32 * n + 16):
+            tables.append(halves[row : row + 16, lane : lane + size])
+        lane += size
+    tables = jnp.concatenate(tables, 1)
     blank = jnp.zeros((tables.shape[0], 256 - tables.shape[1]), F32)
     tables = jnp.concatenate([tables, blank], 1)
     group = width // 256
@@ -773,11 +814,11 @@
     out_ref[...] = jnp.concatenate(rows, 0)
 
 
-def pack_sums(bn_sums, one, two, inner, tables):
+def pack_sums(bn_sums, one, two, inner, tables, half_levels):
     width = one.shape[1]
     rows = 2 * pl.cdiv(bn_sums.shape[1], width) + 5 + inner.size // width + 12 * 256 // width
     return pl.pallas_call(
-        sums_kernel,
+        functools.partial(sums_kernel, half_levels),
         out_shape=jax.ShapeDtypeStruct((pl.cdiv(rows, 8) * 8, width), F32),
         cost_estimate=cost(0, 1_000_000),
         name="pack_sums",
@@ -1019,6 +1060,10 @@
             wide = jnp.broadcast_to(ids, (16, width)).astype(BF16)
             return [jnp.where(wide == level + BF16(16 * t), one, none) for t in range(count // 16)]
 
+        def halves(values, top):
+            chosen = jnp.broadcast_to(top, (16, width)).astype(BF16) == one
+            return [jnp.where(chosen, none, values), jnp.where(chosen, values, none)]
+
         rows = pl.ds(pl.multiple_of(r * 16, 16), 16)
         lanes = pl.ds(pl.multiple_of(start * 128, 128), width)
         for h, (ref, n) in enumerate(heads):
@@ -1027,14 +1072,18 @@
                 rows_ref[c, pl.ds(h, 16, stride=16), :] = values[:, 128 * c : 128 * c + 128]
         total = out_ref[...]
         ids = [ref[0, rows, lanes].astype(F32) for ref in (x_ref, y_ref, rel_ref)]
-        counts = (levels[1], levels[2], levels[0])
+        counts = (levels[1] // 2, levels[2] // 2, levels[0] // 2)
+        tops = [(i >= count).astype(F32) for i, count in zip(ids, counts)]
+        rest = [i - top * count for i, top, count in zip(ids, tops, counts)]
         for n in range(16):
             grads = jnp.concatenate(
                 [rows_ref[c, 16 * n : 16 * n + 16, :].astype(BF16) for c in range(blocks)], 1
             )
-            hot = [one_hot(i[n : n + 1], count) for i, count in zip(ids, counts)]
-            hot = jnp.concatenate(hot[0] + hot[1] + hot[2], 0)
-            total = total + dot_nt(hot, grads)
+            hot, split = [], []
+            for top, low, count in zip(tops, rest, counts):
+                hot += one_hot(low[n : n + 1], count)
+                split += halves(grads, top[n : n + 1])
+            total = total + dot_nt(jnp.concatenate(split, 0), jnp.concatenate(hot, 0))
         out_ref[...] = total
 
     def body(r, _):
@@ -1062,10 +1111,10 @@
             grid=(steps,),
             in_specs=[ids, ids, ids]
             + [pl.BlockSpec((d.shape[0], step, lanes), lambda i, *_: (0, i + first, 0)) for d in ds],
-            out_specs=whole((sum(levels), 16)),
+            out_specs=whole((96, sum(levels) // 2)),
             scratch_shapes=[pltpu.VMEM((lanes // 128, 256, 128), F32)],
         ),
-        out_shape=jax.ShapeDtypeStruct((sum(levels), 16), F32),
+        out_shape=jax.ShapeDtypeStruct((96, sum(levels) // 2), F32),
         compiler_params=pltpu.CompilerParams(vmem_limit_bytes=LIMIT),
         cost_estimate=cost(0, 8_000_000 * steps),
         name="table_sums",
@@ -1247,12 +1296,12 @@
         feeds.append((wide_set.parts(), wide_layout))
     (
         first_n,
+        output_full,
+        output,
         first_r,
-        output,
         grad_first,
         sums_two,
         inner_sums,
-        output_full,
         mine,
         away,
     ) = feed_forward(feeds, mixed, hidden, lines, inner_b, cotangent, inner_rows)
@@ -1264,7 +1313,7 @@
     wide.hold(state)
 
     wide.near()
-    half = pairs - pairs // 3
+    half = pairs // 2
     back_low = attend_back(qkv, grad_mixed, probs, 0, half)
     state, back_low, qkv = epoch(wide.held(), back_low, qkv)
     wide.hold(state)
@@ -1287,7 +1336,7 @@
             [square.reshape(-1, width), pick(value[size:].reshape(ffn, -1, width), index, 0)], 0
         )
 
-    cuts = [0, steps * 2 // 9, steps * 5 // 9, steps]
+    cuts = [0, steps // 3, steps]
     sums = []
 
     def tables(ds):
@@ -1303,8 +1352,7 @@
     wide.join()
     wide.along_ffn(1, 2)
     grad_bn, bn_sums = batch_rows(tokens_grad, visual_maps, bn_stats, proj_full)
-    sums = tables(ds)
-    state, bn_sums, ds, sums, wide.pieces = epoch(tail.held(), bn_sums, ds, sums, wide.pieces)
+    state, bn_sums, ds, wide.pieces = epoch(tail.held(), bn_sums, ds, wide.pieces)
     tail.hold(state)
 
     tail.near()
@@ -1323,16 +1371,28 @@
     tail.blocks, sums, back, wide.pieces = epoch(tail.blocks, sums, back, wide.pieces)
 
     tail.join()
-    tail.along_ffn()
-    total = Sum(pack_sums(bn_sums, sums_one, sums_two, inner_sums, sums))
-    while len(total.steps) > ffn.bit_length() - 1:
+    tail.along_ffn(1, 2)
+    total = Sum(
+        pack_sums(
+            bn_sums,
+            sums_one,
+            sums_two,
+            inner_sums,
+            sums,
+            (levels[1] // 2, levels[2] // 2, levels[0] // 2),
+        )
+    )
+    for _ in range(ffn.bit_length() - 1):
+        total.step()
+    wide_sum = wide.total()
+    state, total.values, back = epoch(tail.held(), total.values, back)
+    tail.hold(state)
+    if ffn > 2:
+        tail.along_ffn(2)
+    while len(total.steps) > 1:
         total.step()
     text_grad = text_rows(back, qkv_full, grad_attn, text_len)
-    wide_sum = wide.total()
-    tail.pieces, total.values = epoch(tail.pieces, total.values)
     tail_sum = tail.total()
-    while len(total.steps) > 1:
-        total.step()
     other = total.steps[0](total.values)
     (
         shift_grad,

time: 337 us -> 323 us (0.958)
  Pallas kernels: 180 us -> 174 us
    pallas_call x3 -> x2, Pallas kernels: 34 us -> 28.7 us  [table_sums(): pl.pallas_call(functools.partial(table_kernel, first, levels), grid_spec=...]
    ppermute x2, waiting for transfers between devices: 6.64 us -> 11 us  [swap_ffn(): return lax.ppermute(values, 'ffn', [(i, i ^ bits) for i in range(size)])]
    ppermute x31, waiting for transfers between devices: 34.5 us -> 30.6 us  [send_dp(): return lax.ppermute(values, 'dp', [(i, i ^ bits) for i in range(size)])]
    ppermute x12, waiting for transfers between devices: 34.5 us -> 31.1 us  [send_ffn(): lax.ppermute(values, 'ffn', [(i, (i + shift) % size) for i in range(size)])]
  transfers between devices with their start and end apart: 45 -> 45, of which waited for: 20 -> 21; matrix products, arithmetic and copies ran while one was open for 6% -> 6% of each run, Pallas kernels for 41% -> 42%
where the time goes in v1:
time: 323 us; the launch traced here: 317 us
  Pallas kernels  174 us (54%)
  waiting for transfers between devices  72.7 us (23%)
  starting transfers between devices  35.3 us (11%)
  other arithmetic  17.2 us (5%)
  local copies, waits for them, and re-layouts  16.9 us (5%)
    pallas_call x1, Pallas kernels, feed_forward(): pl.pallas_call(functools.partial(feed_kernel, entries, len(parts), ct.sha...  34 us
    ppermute x12, waiting for transfers between devices, send_ffn(): lax.ppermute(values, 'ffn', [(i, (i + shift) % size) for i in range(size)])  31.1 us
    ppermute x31, waiting for transfers between devices, send_dp(): return lax.ppermute(values, 'dp', [(i, i ^ bits) for i in range(size)])  30.6 us
    pallas_call x2, Pallas kernels, table_sums(): pl.pallas_call(functools.partial(table_kernel, first, levels), grid_spec=...  28.7 us
    pallas_call x3, Pallas kernels, bias_words(): pl.pallas_call(functools.partial(bias_kernel, step), grid=(steps,), in_sp...  24.7 us
    ppermute x31, starting transfers between devices, send_dp(): return lax.ppermute(values, 'dp', [(i, i ^ bits) for i in range(size)])  19.8 us
    pallas_call x2, Pallas kernels, attend_back(): pl.pallas_call(attend_back_kernel, grid=(pairs,), in_specs=[col[0], col[1...  19.3 us
    ppermute x12, starting transfers between devices, send_ffn(): lax.ppermute(values, 'ffn', [(i, (i + shift) % size) for i in range(size)])  15.4 us
  transfers between devices with their start and end apart: 45, of which 21 were waited for; matrix products, arithmetic and copies ran while one was open for 6% of the time, Pallas kernels for 42%

profile of v1, /device:TPU:0, one launch (start us, length us, event | category | flops | bytes accessed | tf_op | source)
XLA Modules:
  0.0 317.3 jit_solution(15407927762692377625)
XLA Ops:
  2.7 3.0 collective-permute-start
  19.6 6.1 %bias_words.3 = (s32[6,128,640]{2,1,0:T(8,128)}, f32[1,1]{1,0:T(1,128)}) custom-call(s32[1,561,561]{2,1,0:T(8,128)} %copy.82.rel_ref, s32[1,561,561]{2,1,0:T(8,128)} %copy.83.x_ref, s32[1,561,561]{2,1,0:T(8,128)} %copy.84.y_ref, f32[12,256]{1,0:T(8,128)} %pad.8.tab_ref), custom_call_target="tpu_custom_call" | custom-call | bytes 12000 | tf_op jit(solution)/shard_map/bias_words/pallas_call | solution.py:918
  36.3 10.4 %bias_words.4 = (s32[6,256,640]{2,1,0:T(8,128)}, f32[1,1]{1,0:T(1,128)}) custom-call(s32[1,561,561]{2,1,0:T(8,128)} %copy.82.rel_ref, s32[1,561,561]{2,1,0:T(8,128)} %copy.83.x_ref, s32[1,561,561]{2,1,0:T(8,128)} %copy.84.y_ref, f32[12,256]{1,0:T(8,128)} %pad.8.tab_ref), custom_call_target="tpu_custom_call" | custom-call | bytes 24000 | tf_op jit(solution)/shard_map/bias_words/pallas_call | solution.py:918
  46.6 12.5 %collective-permute-done.7.refs_2_ = bf16[216,768]{1,0:T(8,128)(2,1)S(1)} collective-permute-done((bf16[216,768]{1,0:T(8,128)(2,1)S(1)}, bf16[216,768]{1,0:T(8,128)(2,1)S(1)}, u32[]{:S(2)}, u32[]{:S(2)}) %collective-permute-start.7) | collective-permute-done | bytes 331808 | tf_op jit(solution)/shard_map/ppermute | solution.py:42
  61.6 8.7 %collective-permute-done.12.refs_3_ = bf16[216,768]{1,0:T(8,128)(2,1)S(1)} collective-permute-done((bf16[216,768]{1,0:T(8,128)(2,1)S(1)}, bf16[216,768]{1,0:T(8,128)(2,1)S(1)}, u32[]{:S(2)}, u32[]{:S(2)}) %collective-permute-start.12) | collective-permute-done | bytes 331808 | tf_op jit(solution)/shard_map/ppermute | solution.py:42
  73.7 2.9 order_blocks.3.refs_0_
  80.2 11.3 %first_rows.1 = (bf16[768,2304]{1,0:T(8,128)(2,1)}, bf16[2048,768]{1,0:T(8,128)(2,1)}, f32[576,768]{1,0:T(8,128)}, bf16[576,768]{1,0:T(8,128)(2,1)}, bf16[576,23...) custom-call(s32[10]{0:T(128)} %stack.87.place_ref, bf16[608,768]{1,0:T(8,128)(2,1)} %order_blocks.2.refs_0_, ...), custom_call_target="tpu_custom_call" | custom-call | bytes 25000 | tf_op jit(solution)/shard_map/first_rows/pallas_call | solution.py:395
  91.4 8.2 %bias_words.5 = (s32[6,192,640]{2,1,0:T(8,128)}, f32[1,1]{1,0:T(1,128)}) custom-call(s32[1,561,561]{2,1,0:T(8,128)} %copy.82.rel_ref, s32[1,561,561]{2,1,0:T(8,128)} %copy.83.x_ref, s32[1,561,561]{2,1,0:T(8,128)} %copy.84.y_ref, f32[12,256]{1,0:T(8,128)} %pad.8.tab_ref), custom_call_target="tpu_custom_call" | custom-call | bytes 18000 | tf_op jit(solution)/shard_map/bias_words/pallas_call | solution.py:918
  99.7 8.8 %collective-permute-done.15.refs_2_ = bf16[864,768]{1,0:T(8,128)(2,1)S(1)} collective-permute-done((bf16[864,768]{1,0:T(8,128)(2,1)}, bf16[864,768]{1,0:T(8,128)(2,1)S(1)}, u32[]{:S(2)}, u32[]{:S(2)}) %collective-permute-start.15) | collective-permute-done | bytes 1327136 | tf_op jit(solution)/shard_map/ppermute | solution.py:37
  113.2 14.5 %attend.1 = (bf16[12,576,576]{2,1,0:T(8,128)(2,1)}, bf16[576,768]{1,0:T(8,128)(2,1)}) custom-call(f32[1,1]{1,0:T(1,128)} %get-tuple-element.205.unit_ref, bf16[576,2304]{1,0:T(8,128)(2,1)} %get-tuple-element.300.q_ref.k_ref.v_ref, bf16[576,2304]{1,0:T(8,128)(2,1)} %get-tuple-element.300.q_ref.k_ref.v_ref, ...), custom_call_target="tpu_custom_call" | custom-call | flops 2038431 | bytes 40000 | tf_op jit(solution)/shard_map/attend/pallas_call | solution.py:970
  132.6 34.0 %feed_forward.1 = (f32[576,768]{1,0:T(8,128)}, bf16[768,768]{1,0:T(8,128)(2,1)}, bf16[561,768]{1,0:T(8,128)(2,1)}, f32[576,1]{1,0:T(8,128)}, f32[576,768]{1,0:T(...) custom-call(s32[10]{0:T(128)} %stack.87.place_ref, ...), custom_call_target="tpu_custom_call" | custom-call | bytes 100000 | tf_op jit(solution)/shard_map/feed_forward/pallas_call | solution.py:571
  166.8 5.4 %norm_rows.1 = (f32[576,768]{1,0:T(8,128)}, bf16[576,768]{1,0:T(8,128)(2,1)}, bf16[576,768]{1,0:T(8,128)(2,1)}, f32[2,768]{1,0:T(2,128)}) custom-call(f32[576,768]{1,0:T(8,128)} %get-tuple-element.279.grad_ref, f32[576,768]{1,0:T(8,128)} %get-tuple-element.280.normed_ref, f32[576,1]{1,0:T(8,128)} %get-tuple-element.281.scale_ref, ...), custom_call_target="tpu_custom_call" | custom-call | bytes 12000 | tf_op jit(solution)/shard_map/norm_rows/pallas_call | solution.py:631
  178.4 9.9 %attend_back.2 = (bf16[6,576,640]{2,1,0:T(8,128)(2,1)}, bf16[576,384]{1,0:T(8,128)(2,1)}, bf16[576,384]{1,0:T(8,128)(2,1)}, bf16[576,384]{1,0:T(8,128)(2,1)}) custom-call(bf16[576,2304]{1,0:T(8,128)(2,1)} %get-tuple-element.300.q_ref.k_ref.v_ref, bf16[576,2304]{1,0:T(8,128)(2,1)} %get-tuple-element.300.q_ref.k_ref.v_ref, ...), custom_call_target="tpu_custom_call" | custom-call | flops 2038431 | bytes 24000 | tf_op jit(solution)/shard_map/attend_back/pallas_call | solution.py:1028
  188.3 3.6 %collective-permute-done.25 = bf16[1,4,96,768]{3,2,1,0:T(8,128)(2,1)S(1)} collective-permute-done((bf16[1,4,96,768]{3,2,1,0:T(8,128)(2,1)S(1)}, bf16[1,4,96,768]{3,2,1,0:T(8,128)(2,1)S(1)}, u32[]{:S(2)}, u32[]{:S(2)}) %collective-permute-start.25) | collective-permute-done | bytes 589856 | tf_op jit(solution)/shard_map/ppermute | solution.py:37
  197.6 9.5 %attend_back.3 = (bf16[6,576,640]{2,1,0:T(8,128)(2,1)}, bf16[576,384]{1,0:T(8,128)(2,1)}, bf16[576,384]{1,0:T(8,128)(2,1)}, bf16[576,384]{1,0:T(8,128)(2,1)}) custom-call(bf16[576,2304]{1,0:T(8,128)(2,1)} %get-tuple-element.300.q_ref.k_ref.v_ref, bf16[576,2304]{1,0:T(8,128)(2,1)} %get-tuple-element.300.q_ref.k_ref.v_ref, ...), custom_call_target="tpu_custom_call" | custom-call | flops 2038431 | bytes 24000 | tf_op jit(solution)/shard_map/attend_back/pallas_call | solution.py:1028
  207.1 14.4 %tail_rows.1 = (bf16[49,768]{1,0:T(8,128)(2,1)}, bf16[4,640,768]{2,1,0:T(8,128)(2,1)}, bf16[4,640,768]{2,1,0:T(8,128)(2,1)}) custom-call(s32[2]{0:T(128)} %pad_add_fusion.core_ref.place_ref, bf16[576,384]{1,0:T(8,128)(2,1)} %get-tuple-element.362.refs_0_, bf16[576,384]{1,0:T(8,128)(2,1)} %get-tuple-element.363.refs_1_, ...), custom_call_target="tpu_custom_call" | custom-call | bytes 40000 | tf_op jit(solution)/shard_map/tail_rows/pallas_call | solution.py:713
  226.2 4.4 %batch_rows.1 = (f32[49,2048]{1,0:T(8,128)}, f32[2,2048]{1,0:T(2,128)}) custom-call(bf16[49,768]{1,0:T(8,128)(2,1)} %get-tuple-element.318.tokens_ref, bf16[49,2048]{1,0:T(8,128)(2,1)} %refs_3_.1, f32[2,2048]{1,0:T(2,128)} %get-tuple-element.319.stats_ref.refs_4_, bf16[2048,768]{1,0:T(8,128)(2,1)} %get-tuple-element.320.proj_ref), custom_call_target="tpu_custom_call" | custom-call | bytes 6000 | tf_op jit(solution)/shard_map/batch_rows/pallas_call | solution.py:743
  230.6 6.8 %collective-permute-done.30 = bf16[2,96,768]{2,1,0:T(8,128)(2,1)S(1)} collective-permute-done((bf16[2,96,768]{2,1,0:T(8,128)(2,1)S(1)}, bf16[2,96,768]{2,1,0:T(8,128)(2,1)S(1)}, u32[]{:S(2)}, u32[]{:S(2)}) %collective-permute-start.30) | collective-permute-done | bytes 294944 | tf_op jit(solution)/shard_map/ppermute | solution.py:42
  240.8 10.4 %table_sums.2.refs_0_ = f32[96,80]{1,0:T(8,128)} custom-call(s32[36]{0:T(128)} %get-tuple-element.330.block_ref, s32[36]{0:T(128)} %get-tuple-element.331.count_ref, s32[1,561,561]{2,1,0:T(8,128)} %copy.82.rel_ref, s32[1,561,561]{2,1,0:T(8,128)} %copy.83.x_ref, s32[1,561,561]{2,1,0:T(8,128)} %copy.84.y_ref, bf16[6,576,640]{2,1,0:T(8,128)(2,1)} %get-tuple-element.343.refs_0_, ...), custom_call_target="tpu_custom_call" | custom-call | bytes 24000 | tf_op jit(solution)/shard_map/table_sums/pallas_call | solution.py:1107
  251.1 3.1 collective-permute-done.33
  260.4 18.4 %table_sums.3.refs_1_ = f32[96,80]{1,0:T(8,128)} custom-call(s32[36]{0:T(128)} %get-tuple-element.330.block_ref, s32[36]{0:T(128)} %get-tuple-element.331.count_ref, s32[1,561,561]{2,1,0:T(8,128)} %copy.82.rel_ref, s32[1,561,561]{2,1,0:T(8,128)} %copy.83.x_ref, s32[1,561,561]{2,1,0:T(8,128)} %copy.84.y_ref, bf16[6,576,640]{2,1,0:T(8,128)(2,1)} %get-tuple-element.343.refs_0_, ...), custom_call_target="tpu_custom_call" | custom-call | bytes 48000 | tf_op jit(solution)/shard_map/table_sums/pallas_call | solution.py:1107
  287.9 5.8 %collective-permute-done.38 = f32[24,768]{1,0:T(8,128)S(1)} collective-permute-done((f32[24,768]{1,0:T(8,128)}, f32[24,768]{1,0:T(8,128)S(1)}, u32[]{:S(2)}, u32[]{:S(2)}) %collective-permute-start.38) | collective-permute-done | bytes 73760 | tf_op jit(solution)/shard_map/ppermute | solution.py:47
  293.8 5.2 %collective-permute-done.39 = f32[24,768]{1,0:T(8,128)S(1)} collective-permute-done((f32[24,768]{1,0:T(8,128)S(1)}, f32[24,768]{1,0:T(8,128)S(1)}, u32[]{:S(2)}, u32[]{:S(2)}) %collective-permute-start.39) | collective-permute-done | bytes 73760 | tf_op jit(solution)/shard_map/ppermute | solution.py:47
  306.8 5.9 %text_rows.1 = f32[512,768]{1,0:T(8,128)} custom-call(bf16[576,384]{1,0:T(8,128)(2,1)} %get-tuple-element.362.refs_0_, bf16[576,384]{1,0:T(8,128)(2,1)} %get-tuple-element.363.refs_1_, bf16[576,384]{1,0:T(8,128)(2,1)} %get-tuple-element.364.refs_2_, bf16[576,384]{1,0:T(8,128)(2,1)} %get-tuple-element.365.refs_3_, ...), custom_call_target="tpu_custom_call" | custom-call | bytes 25000 | tf_op jit(solution)/shard_map/text_rows/pallas_call | solution.py:770
  (230 shorter events, 92.8 us)
Async XLA Ops:
  2.7 24.2 %collective-permute-start = (bf16[152,768]{1,0:T(8,128)(2,1)}, bf16[152,768]{1,0:T(8,128)(2,1)S(1)}, u32[]{:S(2)}, u32[]{:S(2)}) collective-permute-start(bf16[152,768]{1,0:T(8,128)(2,1)} %pack_first.1.refs_0_), channel_id=1, source_target_pairs={{0,1},{1,2},{2,3},{3,0},{4,5},{5,6},{6,7},{7,4},{8,9},{9,10},{10,1... | collective-permute-start | bytes 700424 | tf_op jit(solution)/shard_map/ppermute | solution.py:42
  5.7 21.2 %collective-permute-start.1 = (bf16[152,768]{1,0:T(8,128)(2,1)}, bf16[152,768]{1,0:T(8,128)(2,1)}, u32[]{:S(2)}, u32[]{:S(2)}) collective-permute-start(bf16[152,768]{1,0:T(8,128)(2,1)} %pack_first.1.refs_0_), channel_id=1, source_target_pairs={{0,2},{1,3},{2,0},{3,1},{4,6},{5,7},{6,4},{7,5},{8,10},{9,11},{10,... | collective-permute-start | bytes 700424 | tf_op jit(solution)/shard_map/ppermute | solution.py:42
  8.3 18.6 %collective-permute-start.2 = (bf16[152,768]{1,0:T(8,128)(2,1)}, bf16[152,768]{1,0:T(8,128)(2,1)}, u32[]{:S(2)}, u32[]{:S(2)}) collective-permute-start(bf16[152,768]{1,0:T(8,128)(2,1)} %pack_first.1.refs_0_), channel_id=1, source_target_pairs={{0,3},{1,0},{2,1},{3,2},{4,7},{5,4},{6,5},{7,6},{8,11},{9,8},{10,9... | collective-permute-start | bytes 700424 | tf_op jit(solution)/shard_map/ppermute | solution.py:42
  29.9 29.2 %collective-permute-start.3 = (bf16[608,768]{1,0:T(8,128)(2,1)}, bf16[608,768]{1,0:T(8,128)(2,1)S(1)}, u32[]{:S(2)}, u32[]{:S(2)}) collective-permute-start(bf16[608,768]{1,0:T(8,128)(2,1)} %order_blocks.2.refs_0_), channel_id=1, source_target_pairs={{0,8},{4,12},{8,0},{12,4},{16,24},{20,28},{24,16},{28,20},{1,9},{5... | collective-permute-start | bytes 2801672 | tf_op jit(solution)/shard_map/ppermute | solution.py:37
  31.4 27.8 %collective-permute-start.4 = (bf16[608,768]{1,0:T(8,128)(2,1)}, bf16[608,768]{1,0:T(8,128)(2,1)S(1)}, u32[]{:S(2)}, u32[]{:S(2)}) collective-permute-start(bf16[608,768]{1,0:T(8,128)(2,1)} %order_blocks.2.refs_0_), channel_id=1, source_target_pairs={{0,16},{4,20},{8,24},{12,28},{16,0},{20,4},{24,8},{28,12},{1,17},{... | collective-permute-start | bytes 2801672 | tf_op jit(solution)/shard_map/ppermute | solution.py:37
  32.9 26.3 %collective-permute-start.5 = (bf16[608,768]{1,0:T(8,128)(2,1)}, bf16[608,768]{1,0:T(8,128)(2,1)S(1)}, u32[]{:S(2)}, u32[]{:S(2)}) collective-permute-start(bf16[608,768]{1,0:T(8,128)(2,1)} %order_blocks.2.refs_0_), channel_id=1, source_target_pairs={{0,4},{4,0},{8,12},{12,8},{16,20},{20,16},{24,28},{28,24},{1,5},{5... | collective-permute-start | bytes 2801672 | tf_op jit(solution)/shard_map/ppermute | solution.py:37
  34.7 24.5 %collective-permute-start.7 = (bf16[216,768]{1,0:T(8,128)(2,1)S(1)}, bf16[216,768]{1,0:T(8,128)(2,1)S(1)}, u32[]{:S(2)}, u32[]{:S(2)}) collective-permute-start(bf16[216,768]{1,0:T(8,128)(2,1)S(1)} %pad_maximum_fusion.4.refs_0_), channel_id=1, source_target_pairs={{0,2},{1,3},{2,0},{3,1},{4,6},{5,7},{6,4},{7,5},{8,10},{9,11},{10,... | collective-permute-start | bytes 995336 | tf_op jit(solution)/shard_map/ppermute | solution.py:42
  77.4 31.1 %collective-permute-start.15 = (bf16[864,768]{1,0:T(8,128)(2,1)}, bf16[864,768]{1,0:T(8,128)(2,1)S(1)}, u32[]{:S(2)}, u32[]{:S(2)}) collective-permute-start(bf16[864,768]{1,0:T(8,128)(2,1)} %order_blocks.3.refs_0_), channel_id=1, source_target_pairs={{0,8},{4,12},{8,0},{12,4},{16,24},{20,28},{24,16},{28,20},{1,9},{5... | collective-permute-start | bytes 3981320 | tf_op jit(solution)/shard_map/ppermute | solution.py:37
  78.4 30.7 %collective-permute-start.16 = (bf16[864,768]{1,0:T(8,128)(2,1)}, bf16[864,768]{1,0:T(8,128)(2,1)S(1)}, u32[]{:S(2)}, u32[]{:S(2)}) collective-permute-start(bf16[864,768]{1,0:T(8,128)(2,1)} %order_blocks.3.refs_0_), channel_id=1, source_target_pairs={{0,16},{4,20},{8,24},{12,28},{16,0},{20,4},{24,8},{28,12},{1,17},{... | collective-permute-start | bytes 3981320 | tf_op jit(solution)/shard_map/ppermute | solution.py:37
  78.9 30.2 %collective-permute-start.17 = (bf16[864,768]{1,0:T(8,128)(2,1)}, bf16[864,768]{1,0:T(8,128)(2,1)}, u32[]{:S(2)}, u32[]{:S(2)}) collective-permute-start(bf16[864,768]{1,0:T(8,128)(2,1)} %order_blocks.3.refs_0_), channel_id=1, source_target_pairs={{0,4},{4,0},{8,12},{12,8},{16,20},{20,16},{24,28},{28,24},{1,5},{5... | collective-permute-start | bytes 3981320 | tf_op jit(solution)/shard_map/ppermute | solution.py:37
  109.1 19.2 %collective-permute-start.20 = (bf16[864,768]{1,0:T(8,128)(2,1)S(1)}, bf16[864,768]{1,0:T(8,128)(2,1)}, u32[]{:S(2)}, u32[]{:S(2)}) collective-permute-start(bf16[864,768]{1,0:T(8,128)(2,1)S(1)} %collective-permute-done.15.refs_2_), channel_id=1, source_target_pairs={{0,4},{4,0},{8,12},{12,8},{16,20},{20,16},{24,28},{28,24},{1,5},{5... | collective-permute-start | bytes 3981320 | tf_op jit(solution)/shard_map/ppermute | solution.py:37
  109.1 19.2 %collective-permute-start.21 = (bf16[864,768]{1,0:T(8,128)(2,1)S(1)}, bf16[864,768]{1,0:T(8,128)(2,1)}, u32[]{:S(2)}, u32[]{:S(2)}) collective-permute-start(bf16[864,768]{1,0:T(8,128)(2,1)S(1)} %collective-permute-done.16.refs_4_), channel_id=1, source_target_pairs={{0,4},{4,0},{8,12},{12,8},{16,20},{20,16},{24,28},{28,24},{1,5},{5... | collective-permute-start | bytes 3981320 | tf_op jit(solution)/shard_map/ppermute | solution.py:37
  109.6 18.6 %collective-permute-start.18 = (bf16[480,768]{1,0:T(8,128)(2,1)S(1)}, bf16[480,768]{1,0:T(8,128)(2,1)}, u32[]{:S(2)}, u32[]{:S(2)}) collective-permute-start(bf16[480,768]{1,0:T(8,128)(2,1)S(1)} %slice.167), channel_id=1, source_target_pairs={{0,16},{4,20},{8,24},{12,28},{16,0},{20,4},{24,8},{28,12},{1,17},{... | collective-permute-start | bytes 2211848 | tf_op jit(solution)/shard_map/ppermute | solution.py:37
  111.1 16.7 %collective-permute-start.19 = (bf16[384,768]{1,0:T(8,128)(2,1)}, bf16[384,768]{1,0:T(8,128)(2,1)}, u32[]{:S(2)}, u32[]{:S(2)}) collective-permute-start(bf16[384,768]{1,0:T(8,128)(2,1)} %slice.168), channel_id=1, source_target_pairs={{0,8},{4,12},{8,0},{12,4},{16,24},{20,28},{24,16},{28,20},{1,9},{5... | collective-permute-start | bytes 1769480 | tf_op jit(solution)/shard_map/ppermute | solution.py:37
  176.4 15.4 %collective-permute-start.25 = (bf16[1,4,96,768]{3,2,1,0:T(8,128)(2,1)S(1)}, bf16[1,4,96,768]{3,2,1,0:T(8,128)(2,1)S(1)}, u32[]{:S(2)}, u32[]{:S(2)}) collective-permute-start(bf16[1,4,96,768]{3,2,1,0:T(8,128)(2,1)S(1)} %get-tuple-element.396), channel_id=1, source_target_pairs={{0,8},{4,12},{8,0},{12,4},{16,24},{20,28},{24,16},{28,20},{1,9},{5... | collective-permute-start | bytes 1769480 | tf_op jit(solution)/shard_map/ppermute | solution.py:37
  177.7 15.1 %collective-permute-start.26 = (bf16[1,4,96,768]{3,2,1,0:T(8,128)(2,1)S(1)}, bf16[1,4,96,768]{3,2,1,0:T(8,128)(2,1)S(1)}, u32[]{:S(2)}, u32[]{:S(2)}) collective-permute-start(bf16[1,4,96,768]{3,2,1,0:T(8,128)(2,1)S(1)} %get-tuple-element.395), channel_id=1, source_target_pairs={{0,16},{4,20},{8,24},{12,28},{16,0},{20,4},{24,8},{28,12},{1,17},{... | collective-permute-start | bytes 1769480 | tf_op jit(solution)/shard_map/ppermute | solution.py:37
  195.7 26.9 %collective-permute-start.27 = (bf16[2,4,96,768]{3,2,1,0:T(8,128)(2,1)S(1)}, bf16[2,4,96,768]{3,2,1,0:T(8,128)(2,1)S(1)}, u32[]{:S(2)}, u32[]{:S(2)}) collective-permute-start(bf16[2,4,96,768]{3,2,1,0:T(8,128)(2,1)S(1)} %pad_maximum_fusion), channel_id=1, source_target_pairs={{0,8},{4,12},{8,0},{12,4},{16,24},{20,28},{24,16},{28,20},{1,9},{5... | collective-permute-start | bytes 3538952 | tf_op jit(solution)/shard_map/ppermute | solution.py:37
  196.5 26.6 %collective-permute-start.28 = (bf16[2,4,96,768]{3,2,1,0:T(8,128)(2,1)S(1)}, bf16[2,4,96,768]{3,2,1,0:T(8,128)(2,1)S(1)}, u32[]{:S(2)}, u32[]{:S(2)}) collective-permute-start(bf16[2,4,96,768]{3,2,1,0:T(8,128)(2,1)S(1)} %pad_maximum_fusion.1), channel_id=1, source_target_pairs={{0,16},{4,20},{8,24},{12,28},{16,0},{20,4},{24,8},{28,12},{1,17},{... | collective-permute-start | bytes 3538952 | tf_op jit(solution)/shard_map/ppermute | solution.py:37
  223.1 14.3 %collective-permute-start.29 = (bf16[4,640,768]{2,1,0:T(8,128)(2,1)}, bf16[4,640,768]{2,1,0:T(8,128)(2,1)}, u32[]{:S(2)}, u32[]{:S(2)}) collective-permute-start(bf16[4,640,768]{2,1,0:T(8,128)(2,1)} %get-tuple-element.316), channel_id=1, source_target_pairs={{0,4},{4,0},{8,12},{12,8},{16,20},{20,16},{24,28},{28,24},{1,5},{5... | collective-permute-start | bytes 11796488 | tf_op jit(solution)/shard_map/ppermute | solution.py:37
  238.8 15.4 %collective-permute-start.31 = (bf16[320,768]{1,0:T(8,128)(2,1)S(1)}, bf16[320,768]{1,0:T(8,128)(2,1)S(1)}, u32[]{:S(2)}, u32[]{:S(2)}) collective-permute-start(bf16[320,768]{1,0:T(8,128)(2,1)S(1)} %get-tuple-element.400), channel_id=1, source_target_pairs={{0,8},{4,12},{8,0},{12,4},{16,24},{20,28},{24,16},{28,20},{1,9},{5... | collective-permute-start | bytes 1474568 | tf_op jit(solution)/shard_map/ppermute | solution.py:37
  256.8 23.7 %collective-permute-start.34 = (bf16[640,768]{1,0:T(8,128)(2,1)S(1)}, bf16[640,768]{1,0:T(8,128)(2,1)S(1)}, u32[]{:S(2)}, u32[]{:S(2)}) collective-permute-start(bf16[640,768]{1,0:T(8,128)(2,1)S(1)} %pad_maximum_fusion.2), channel_id=1, source_target_pairs={{0,8},{4,12},{8,0},{12,4},{16,24},{20,28},{24,16},{28,20},{1,9},{5... | collective-permute-start | bytes 2949128 | tf_op jit(solution)/shard_map/ppermute | solution.py:37
  258.1 23.5 %collective-permute-start.35 = (bf16[640,768]{1,0:T(8,128)(2,1)S(1)}, bf16[640,768]{1,0:T(8,128)(2,1)}, u32[]{:S(2)}, u32[]{:S(2)}) collective-permute-start(bf16[640,768]{1,0:T(8,128)(2,1)S(1)} %pad_maximum_fusion.3), channel_id=1, source_target_pairs={{0,16},{4,20},{8,24},{12,28},{16,0},{20,4},{24,8},{28,12},{1,17},{... | collective-permute-start | bytes 2949128 | tf_op jit(solution)/shard_map/ppermute | solution.py:37
  259.0 19.8 %collective-permute-start.36 = (bf16[2,96,768]{2,1,0:T(8,128)(2,1)S(1)}, bf16[2,96,768]{2,1,0:T(8,128)(2,1)S(1)}, u32[]{:S(2)}, u32[]{:S(2)}) collective-permute-start(bf16[2,96,768]{2,1,0:T(8,128)(2,1)S(1)} %copy-done.27), channel_id=1, source_target_pairs={{0,3},{1,0},{2,1},{3,2},{4,7},{5,4},{6,5},{7,6},{8,11},{9,8},{10,9... | collective-permute-start | bytes 884744 | tf_op jit(solution)/shard_map/ppermute | solution.py:42
  299.3 16.3 %collective-permute-start.43 = (bf16[160,768]{1,0:T(8,128)(2,1)S(1)}, bf16[160,768]{1,0:T(8,128)(2,1)S(1)}, u32[]{:S(2)}, u32[]{:S(2)}) collective-permute-start(bf16[160,768]{1,0:T(8,128)(2,1)S(1)} %pad_maximum_fusion.7), channel_id=1, source_target_pairs={{0,2},{1,3},{2,0},{3,1},{4,6},{5,7},{6,4},{7,5},{8,10},{9,11},{10,... | collective-permute-start | bytes 737288 | tf_op jit(solution)/shard_map/ppermute | solution.py:42
  (59 other events, 511.2 us)

commit v2 on v1

--- a/solution.py
+++ b/solution.py
@@ -73,9 +73,10 @@
 
 
 class Gather:
-    def __init__(self, own, rows):
+    def __init__(self, own, rows, rest=0):
         self.own = own
         self.rows = rows
+        self.rest = rest
 
     def along_ffn(self, begin=1, end=None):
         size = lax.axis_size("ffn")
@@ -86,7 +87,7 @@
         size = lax.axis_size("ffn")
         here = lax.axis_index("ffn")
         if all(rows % 8 == 0 for rows in self.rows):
-            self.block = order_blocks(here, self.far, self.rows)
+            self.block = order_blocks(here, self.far, self.rows, self.rest)
             return
         pieces = []
         for slot in range(size):
@@ -155,15 +156,19 @@
         self.away = away
         self.far = far
 
+    def ahead(self, last):
+        if self.away.shape[0] == 4:
+            self.first = send_dp(last, 1)
+
     def core(self):
         self.got = send_dp(self.away, 1)
 
     def near(self):
-        mine, got = self.value, self.got
-        if mine.shape[0] == 4:
-            half = mine.shape[1] // 2
-            self.low = send_dp(plus(mine[3, :half], got[3, :half]), 4)
-            self.high = send_dp(plus(mine[3, half:], got[3, half:]), 2)
+        if self.away.shape[0] == 4:
+            mine, got = self.value[3], self.first
+            half = mine.shape[0] // 2
+            self.low = send_dp(plus(mine[:half], got[:half]), 4)
+            self.high = send_dp(plus(mine[half:], got[half:]), 2)
 
     def prepare(self):
         mine, got = self.value, self.got
@@ -192,11 +197,12 @@
     def hold(self, state):
         vars(self).update(state)
 
-    def along_ffn(self, begin=1, end=None):
+    def along_ffn(self, shifts):
         size = lax.axis_size("ffn")
         here = lax.axis_index("ffn")
-        self.pieces = self.pieces[:begin] if begin > 1 else [self.far(self.value, here)]
-        for k in range(begin, end or size):
+        if not hasattr(self, "pieces"):
+            self.pieces = [self.far(self.value, here)]
+        for k in shifts:
             self.pieces.append(send_ffn(self.far(self.value, (here + k) % size), k))
 
     def total(self):
@@ -252,7 +258,7 @@
     return own, rows
 
 
-def order_kernel(rows, here_ref, *refs):
+def order_kernel(rows, rest, here_ref, *refs):
     parts, out_ref = refs[:-1], refs[-1]
     size = len(parts)
     here = here_ref[0]
@@ -267,15 +273,21 @@
                     out_ref[row : row + count, :] = parts[k][begin : begin + count, :]
                 begin += count
 
-
-def order_blocks(here, parts, rows):
+    begin = sum(rows)
+    for k in range(1, size if rest else 1):
+        row = begin * size + (k - 1) * rest
+        out_ref[row : row + rest, :] = parts[k][begin:, :]
+
+
+def order_blocks(here, parts, rows, rest):
     width = parts[0].shape[1]
+    count = len(parts)
     return pl.pallas_call(
-        functools.partial(order_kernel, rows),
+        functools.partial(order_kernel, rows, rest),
         in_specs=[pl.BlockSpec(memory_space=pltpu.SMEM)]
         + [pl.BlockSpec(memory_space=pltpu.VMEM)] * len(parts),
         out_specs=pl.BlockSpec(memory_space=pltpu.VMEM),
-        out_shape=jax.ShapeDtypeStruct((len(parts) * sum(rows), width), BF16),
+        out_shape=jax.ShapeDtypeStruct((count * sum(rows) + (count - 1) * rest, width), BF16),
         compiler_params=pltpu.CompilerParams(vmem_limit_bytes=LIMIT),
         name="order_blocks",
     )(here.reshape(1).astype(jnp.int32), *parts)
@@ -290,15 +302,14 @@
     return entries
 
 
-def place_index(parts):
-    place = lax.axis_index("dp")
-    return jnp.stack([place ^ bits for _, bits, _ in parts]).astype(jnp.int32)
-
-
-def part_copies(entries, place_ref, parts, outs, sems):
+def place_bits(parts):
+    return [bits for _, bits, _ in parts]
+
+
+def part_copies(entries, bits, place, parts, outs, sems):
     copies = []
     for n, (part, begin, rows, out, base, lane) in enumerate(entries):
-        target = pl.multiple_of(base + place_ref[part] * rows, 16)
+        target = pl.multiple_of(base + (place ^ bits[part]) * rows, 16)
         width = parts[part].shape[1]
         copies.append(
             pltpu.make_async_copy(
@@ -310,9 +321,9 @@
     return copies
 
 
-def picked(order_col, size):
-    lane = lax.broadcasted_iota(jnp.int32, (size, size), 1)
-    return (order_col == lane).astype(F32)
+def picked(order, size):
+    row = lax.broadcasted_iota(jnp.int32, (size, size), 0)
+    return (order == row).astype(F32)
 
 
 def exact(a, b, dims):
@@ -321,13 +332,13 @@
     )
 
 
-def first_kernel(entries, count, devices, place_ref, *refs):
-    parts, refs = refs[:count], refs[count:]
+def first_kernel(entries, bits, devices, place_ref, *refs):
+    parts, refs = refs[: len(bits)], refs[len(bits) :]
     text_ref, visual_ref, order_ref, lines_ref = refs[:4]
-    qkv_w_ref, proj_ref, hidden_ref, low_ref, qkv_ref, bn_ref, stats_ref = refs[4:11]
-    moments_ref, sems = refs[11:]
+    qkv_w_ref, proj_ref, hidden_ref, turned_ref, qkv_ref, bn_ref, stats_ref = refs[4:11]
+    moments_ref, low_ref, sems = refs[11:]
     outs = (qkv_w_ref, proj_ref, moments_ref)
-    copies = part_copies(entries, place_ref, parts, outs, sems)
+    copies = part_copies(entries, bits, place_ref[0], parts, outs, sems)
     for copy in copies:
         copy.start()
     copies = [(entry[3], copy) for entry, copy in zip(entries, copies)]
@@ -362,7 +373,7 @@
         if out == 1:
             copy.wait()
     tokens = dot_nn(bn_rows, proj_ref[...])
-    tokens = exact(picked(order_ref[...], visual_len), tokens, ((1,), (0,)))
+    tokens = exact(picked(order_ref[...], visual_len), tokens, ((0,), (0,)))
     blank = jnp.zeros((hidden_ref.shape[0] - text_len - visual_len, width), F32)
     tokens = jnp.concatenate([tokens, blank], 0)
     hidden_ref[text_len:, :] = tokens
@@ -371,13 +382,14 @@
         if out == 0:
             copy.wait()
     low = low_ref[...]
+    turned_ref[...] = low.T
     for n in range(3):
         lanes = slice(n * width, (n + 1) * width)
         values = dot_nn(low, qkv_w_ref[:, lanes])
         qkv_ref[:, lanes] = (values * 0.125 if n == 0 else values).astype(BF16)
 
 
-def first_rows(parts, layout, text, visual, order, lines, rows, proj_rows, moment_rows):
+def first_rows(place, parts, layout, text, visual, order, lines, rows, proj_rows, moment_rows):
     devices = lax.axis_size("dp") * lax.axis_size("ffn")
     width = text.shape[1]
     channels = visual.shape[1]
@@ -387,13 +399,13 @@
         ((width, 3 * width), BF16),
         ((proj_rows, width), BF16),
         ((rows, width), F32),
-        ((rows, width), BF16),
+        ((width, rows), BF16),
         ((rows, 3 * width), BF16),
         ((visual.shape[0], channels), BF16),
         ((2, channels), F32),
     ]
     return pl.pallas_call(
-        functools.partial(first_kernel, entries, len(parts), devices),
+        functools.partial(first_kernel, entries, place_bits(parts), devices),
         in_specs=[pl.BlockSpec(memory_space=pltpu.SMEM)]
         + [pl.BlockSpec(memory_space=pl.ANY)] * len(parts)
         + [vmem] * 4,
@@ -401,13 +413,14 @@
         out_shape=[jax.ShapeDtypeStruct(*shape) for shape in shapes],
         scratch_shapes=[
             pltpu.VMEM((moment_rows * devices, width), BF16),
+            pltpu.VMEM((rows, width), BF16),
             pltpu.SemaphoreType.DMA((len(entries),)),
         ],
         compiler_params=pltpu.CompilerParams(vmem_limit_bytes=LIMIT),
         cost_estimate=cost(0, 25_000_000),
         name="first_rows",
     )(
-        place_index(parts),
+        place,
         *[block for block, _, _ in parts],
         text,
         visual,
@@ -416,8 +429,9 @@
     )
 
 
-def store_blocks(mine_ref, away_ref, core, quad, store):
+def store_blocks(mine_ref, away_ref, place, store):
     quads = mine_ref.shape[0]
+    core, quad = place % 2, place // 2
     for bit in range(2):
 
         @pl.when(core == bit)
@@ -427,20 +441,15 @@
                 store(ref, (dp // 2) ^ quad, dp)
 
 
-def place_pair():
-    place = lax.axis_index("dp")
-    return jnp.stack([place % 2, place // 2]).astype(jnp.int32)
-
-
-def feed_kernel(entries, count, length, ffn, place_ref, core_ref, *refs):
-    parts, refs = refs[:count], refs[count:]
+def feed_kernel(entries, bits, length, ffn, place_ref, *refs):
+    parts, refs = refs[: len(bits)], refs[len(bits) :]
     inputs, (lines_ref, inner_b_ref), refs = refs[:3], refs[3:5], refs[5:]
     results, (scale_ref, total_ref, sums_ref, inner_sums_ref), refs = refs[:3], refs[3:7], refs[7:]
-    mine_ref, away_ref = refs[:2]
-    outer_w_ref, inner_w_ref, act_ref, slope_ref, first_ref, low_ref = refs[2:8]
-    first_turned, low_turned = refs[8:10]
-    mixed_ref, hidden_ref, ct_ref, normed_ref, out_w_ref, output_ref = refs[10:16]
-    sems, in_sems, out_sems = refs[16:]
+    mine_ref, away_ref, last_ref = refs[:3]
+    outer_w_ref, inner_w_ref, act_ref, slope_ref, first_ref, low_ref = refs[3:9]
+    first_turned, low_turned = refs[9:11]
+    mixed_ref, hidden_ref, ct_ref, normed_ref, out_w_ref, output_ref = refs[11:17]
+    sems, in_sems, out_sems = refs[17:]
     step = pl.program_id(0)
     width = hidden_ref.shape[1]
     outs = (out_w_ref, outer_w_ref, inner_w_ref)
@@ -456,7 +465,7 @@
 
     @pl.when(step == 0)
     def _():
-        copies = part_copies(entries, place_ref, parts, outs, sems)
+        copies = part_copies(entries, bits, place_ref[0], parts, outs, sems)
         square = [copy for entry, copy in zip(entries, copies) if entry[3] == 0]
         now = [copy for entry, copy in zip(entries, copies) if entry[3] > 0 and entry[4] == 0]
         later = [copy for entry, copy in zip(entries, copies) if entry[3] > 0 and entry[4] > 0]
@@ -482,7 +491,7 @@
 
         @pl.when(step == index)
         def _(index=index):
-            copies = part_copies(entries, place_ref, parts, outs, sems)
+            copies = part_copies(entries, bits, place_ref[0], parts, outs, sems)
             for entry, copy in zip(entries, copies):
                 if entry[3] > 0 and entry[4] == index * width:
                     copy.wait()
@@ -490,7 +499,7 @@
     @pl.when(step < ffn)
     def _():
         rows = pl.ds(pl.multiple_of(step * width, width), width)
-        inner = dot_nn(first_ref[...], inner_w_ref[rows, :]) + inner_b_ref[step]
+        inner = dot_nn(first_ref[...], inner_w_ref[rows, :]) + inner_b_ref[place_ref[1 + step]]
         root = 0.7978845608028654
         square = inner * inner
         half = 0.5 + 0.5 * jnp.tanh(inner * (root + (0.044715 * root) * square))
@@ -524,7 +533,7 @@
         f = step - ffn
         rows = pl.ds(pl.multiple_of(f * width, width), width)
         grad = dot_nn(low_ref[...], outer_w_ref[rows, :]) * slope_ref[f].astype(F32)
-        inner_sums_ref[0] = jnp.sum(grad, 0, keepdims=True)
+        inner_sums_ref[place_ref[1 + f]] = jnp.sum(grad, 0, keepdims=True)
         grad = grad.astype(BF16)
         total_ref[...] += dot_nt(grad, inner_w_ref[rows, :])
         inner = dot_nn(first_turned[...], grad).astype(BF16)
@@ -534,8 +543,14 @@
         def store(ref, slot, dp):
             ref[slot, 0, 0] = inner[dp * size : (dp + 1) * size]
             ref[slot, 1, 0] = outer[dp * size : (dp + 1) * size]
-
-        store_blocks(mine_ref, away_ref, core_ref[0], core_ref[1], store)
+            if ref is away_ref:
+
+                @pl.when(slot == away_ref.shape[0] - 1)
+                def _():
+                    last_ref[0, 0] = inner[dp * size : (dp + 1) * size]
+                    last_ref[1, 0] = outer[dp * size : (dp + 1) * size]
+
+        store_blocks(mine_ref, away_ref, place_ref[0], store)
 
     @pl.when(step == 2 * ffn - 1)
     def _():
@@ -543,7 +558,7 @@
             copy.wait()
 
 
-def feed_forward(feeds, mixed, hidden, lines, inner_b, ct, inner_rows):
+def feed_forward(place, feeds, mixed, hidden, lines, inner_b, ct, inner_rows):
     parts, entries = [], []
     for some, layout in feeds:
         for part, *entry in place_entries(some, layout):
@@ -557,6 +572,7 @@
     back = lambda i: jnp.maximum(i - ffn, 0)
     block = pl.BlockSpec((quads, 2, 1, inner_rows, columns), lambda i: (0, 0, back(i), 0, 0))
     blocks = jax.ShapeDtypeStruct((quads, 2, ffn, inner_rows, columns), BF16)
+    last = pl.BlockSpec((2, 1, inner_rows, columns), lambda i: (0, back(i), 0, 0))
     smem = pl.BlockSpec(memory_space=pltpu.SMEM)
     shapes = [
         ((rows, width), F32),
@@ -569,15 +585,16 @@
     ]
     anywhere = pl.BlockSpec(memory_space=pl.ANY)
     return pl.pallas_call(
-        functools.partial(feed_kernel, entries, len(parts), ct.shape[0], ffn),
+        functools.partial(feed_kernel, entries, place_bits(parts), ct.shape[0], ffn),
         grid=(2 * ffn,),
-        in_specs=[smem, smem]
+        in_specs=[smem]
         + [anywhere] * (len(parts) + 3)
         + [whole(lines.shape), whole(inner_b.shape)],
         out_specs=[anywhere] * 3
         + [whole((rows, 1)), square, whole((3, width))]
-        + [pl.BlockSpec((1, 1, columns), lambda i: (back(i), 0, 0)), block, block],
-        out_shape=[jax.ShapeDtypeStruct(*shape) for shape in shapes] + [blocks, blocks],
+        + [whole((ffn, 1, columns)), block, block, last],
+        out_shape=[jax.ShapeDtypeStruct(*shape) for shape in shapes]
+        + [blocks, blocks, jax.ShapeDtypeStruct((2, ffn, inner_rows, columns), BF16)],
         scratch_shapes=[
             pltpu.VMEM((ffn * width, columns), BF16),
             pltpu.VMEM((ffn * width, columns), BF16),
@@ -601,8 +618,7 @@
         cost_estimate=cost(0, 100_000_000),
         name="feed_forward",
     )(
-        place_index(parts),
-        place_pair(),
+        place,
         *[part for part, _, _ in parts],
         mixed,
         hidden,
@@ -644,8 +660,8 @@
 
 def tail_kernel(text_len, place_ref, *refs):
     inputs, (order_ref, attn_ref, tokens_ref), refs = refs[:11], refs[11:14], refs[14:]
-    outputs, buffers = refs[:2], refs[2:13]
-    mine, away, in_sems, out_sems = refs[13:]
+    outputs, buffers = refs[:3], refs[3:14]
+    mine, away, in_sems, out_sems = refs[14:]
     low_ref, mixed_ref, attn_low_ref, qkv_w_ref, bn_ref = buffers[6:]
     names = (6, 0, 1, 2, 3, 4, 5, 7, 8, 9, 10)
     copies = {n: pltpu.make_async_copy(inputs[n], buffers[n], in_sems.at[n]) for n in names}
@@ -653,7 +669,6 @@
         copies[n].start()
     visual_len = bn_ref.shape[0]
     width = attn_low_ref.shape[1]
-    core, quad = place_ref[0], place_ref[1]
     sent = []
 
     def spread(values, begin, n):
@@ -663,7 +678,7 @@
         def store(ref, slot, dp):
             ref[slot, begin : begin + rows, :] = values[dp * rows : (dp + 1) * rows]
 
-        store_blocks(mine, away, core, quad, store)
+        store_blocks(mine, away, place_ref[0], store)
         part = pl.ds(begin, rows)
         for k, ref in enumerate((mine, away)):
             copy = pltpu.make_async_copy(
@@ -671,10 +686,15 @@
             )
             copy.start()
             sent.append(copy)
+        copy = pltpu.make_async_copy(
+            away.at[away.shape[0] - 1, part, :], outputs[2].at[part, :], out_sems.at[n, 2]
+        )
+        copy.start()
+        sent.append(copy)
         return begin + rows
 
     copies[6].wait()
-    turned = low_ref[...].T
+    turned = low_ref[...]
     begin = 0
     grads = []
     for n in range(3):
@@ -691,7 +711,7 @@
         lanes = slice(n * width, (n + 1) * width)
         tokens = tokens + dot_nt(grads[n][text_len:], qkv_w_ref[:, lanes])
     picker = picked(order_ref[...], visual_len)
-    tokens = exact(picker, tokens[:visual_len], ((0,), (0,))).astype(BF16)
+    tokens = exact(picker, tokens[:visual_len], ((1,), (0,))).astype(BF16)
     tokens_ref[...] = tokens
     copies[10].wait()
     spread(dot_tn(bn_ref[...], tokens), begin, 4)
@@ -699,7 +719,7 @@
         copy.wait()
 
 
-def tail_rows(back, qkv_w, attn, attn_low, mixed, low, order, bn_rows, text_len):
+def tail_rows(place, back, qkv_w, attn, attn_low, mixed, low, order, bn_rows, text_len):
     dp, ffn = lax.axis_size("dp"), lax.axis_size("ffn")
     rows, width = attn.shape
     visual_len, channels = bn_rows.shape
@@ -716,23 +736,24 @@
         in_specs=[pl.BlockSpec(memory_space=pltpu.SMEM)]
         + [anywhere] * len(inputs)
         + [whole(order.shape), tail],
-        out_specs=[whole((visual_len, width))] + [anywhere] * 2,
-        out_shape=[jax.ShapeDtypeStruct((visual_len, width), BF16), blocks, blocks],
+        out_specs=[whole((visual_len, width))] + [anywhere] * 3,
+        out_shape=[jax.ShapeDtypeStruct((visual_len, width), BF16), blocks, blocks]
+        + [jax.ShapeDtypeStruct((size, width), BF16)],
         scratch_shapes=[pltpu.VMEM(x.shape, BF16) for x in inputs]
         + [
             pltpu.VMEM(blocks.shape, BF16),
             pltpu.VMEM(blocks.shape, BF16),
             pltpu.SemaphoreType.DMA((len(inputs),)),
-            pltpu.SemaphoreType.DMA((5, 2)),
+            pltpu.SemaphoreType.DMA((5, 3)),
         ],
         compiler_params=pltpu.CompilerParams(vmem_limit_bytes=LIMIT),
         cost_estimate=cost(0, 40_000_000),
         name="tail_rows",
-    )(place_pair(), *inputs, order, attn)
+    )(place, *inputs, order, attn)
 
 
 def batch_kernel(tokens_ref, visual_ref, stats_ref, proj_ref, grad_bn_ref, sums_ref):
-    grad_bn = dot_nt(tokens_ref[...], proj_ref[...])
+    grad_bn = dot_nt(proj_ref[...], tokens_ref[...]).T
     grad_bn_ref[...] = grad_bn
     normed = (visual_ref[...].astype(F32) - stats_ref[0:1, :]) * stats_ref[1:2, :]
     sums_ref[0:1, :] = jnp.sum(grad_bn, 0, keepdims=True)
@@ -936,12 +957,14 @@
     return lane < 64, lane >= 64
 
 
-def attend_kernel(unit_ref, q_ref, k_ref, v_ref, col_ref, row_ref, *refs):
+def attend_kernel(unit_ref, q_ref, k_ref, v_ref, row_ref, *refs):
     word_refs, (p_ref, o_ref, mask_ref) = refs[:-3], refs[-3:]
 
     @pl.when(pl.program_id(0) == 0)
     def _():
-        mask_ref[...] = jnp.where(col_ref[...] == row_ref[...], 0.0, NEG)
+        row = row_ref[...].astype(F32)
+        col = jnp.broadcast_to(row, (8, row.shape[1])).T[:, :1]
+        mask_ref[...] = jnp.where(col == row, 0.0, NEG)
 
     unit = unit_ref[...]
     rows = q_ref.shape[0]
@@ -975,7 +998,6 @@
             col[0],
             col[1],
             col[2],
-            whole((rows, 1)),
             whole((1, rows)),
         ]
         + [pl.BlockSpec((1,) + w.shape[1:], lambda p: (p, 0, 0)) for w in words],
@@ -991,7 +1013,7 @@
         compiler_params=pltpu.CompilerParams(vmem_limit_bytes=LIMIT),
         cost_estimate=cost(flops, 40_000_000),
         name="attend",
-    )(unit, qkv, qkv, qkv, *segments, *words)
+    )(unit, qkv, qkv, qkv, segments, *words)
 
 
 def attend_back_kernel(q_ref, k_ref, v_ref, g_ref, p_ref, ds_ref, dq_ref, dk_ref, dv_ref):
@@ -1038,7 +1060,7 @@
 
 
 def table_kernel(first, levels, block_ref, count_ref, rel_ref, x_ref, y_ref, *refs):
-    ds_refs, out_ref, rows_ref = refs[:-2], refs[-2], refs[-1]
+    ds_refs, out_ref = refs[:-1], refs[-1]
     place = pl.program_id(0)
     step = rel_ref.shape[1]
     every = rel_ref.shape[2] // 128
@@ -1046,9 +1068,8 @@
     @pl.when(place == 0)
     def _():
         out_ref[...] = jnp.zeros_like(out_ref)
-        rows_ref[...] = jnp.zeros_like(rows_ref)
-
-    heads = [(ref, n) for ref in ds_refs for n in range(ref.shape[0])]
+
+    heads = sum(ref.shape[0] for ref in ds_refs)
 
     def group(r, start, blocks):
         width = blocks * 128
@@ -1066,19 +1087,16 @@
 
         rows = pl.ds(pl.multiple_of(r * 16, 16), 16)
         lanes = pl.ds(pl.multiple_of(start * 128, 128), width)
-        for h, (ref, n) in enumerate(heads):
-            values = ref[n, rows, lanes].astype(F32)
-            for c in range(blocks):
-                rows_ref[c, pl.ds(h, 16, stride=16), :] = values[:, 128 * c : 128 * c + 128]
+        values = [ref[:, rows, lanes] for ref in ds_refs]
+        values.append(jnp.zeros((16 - heads, 16, width), BF16))
+        values = jnp.transpose(jnp.concatenate(values, 0), (1, 0, 2))
         total = out_ref[...]
         ids = [ref[0, rows, lanes].astype(F32) for ref in (x_ref, y_ref, rel_ref)]
         counts = (levels[1] // 2, levels[2] // 2, levels[0] // 2)
         tops = [(i >= count).astype(F32) for i, count in zip(ids, counts)]
         rest = [i - top * count for i, top, count in zip(ids, tops, counts)]
         for n in range(16):
-            grads = jnp.concatenate(
-                [rows_ref[c, 16 * n : 16 * n + 16, :].astype(BF16) for c in range(blocks)], 1
-            )
+            grads = values[n]
             hot, split = [], []
             for top, low, count in zip(tops, rest, counts):
                 hot += one_hot(low[n : n + 1], count)
@@ -1101,7 +1119,7 @@
 
 
 def table_sums(ranges, rel, x, y, ds, levels, first, steps):
-    step = 64
+    step = 96
     lanes = ds[0].shape[2]
     ids = pl.BlockSpec((1, step, lanes), lambda i, *_: (0, i + first, 0))
     return pl.pallas_call(
@@ -1112,7 +1130,6 @@
             in_specs=[ids, ids, ids]
             + [pl.BlockSpec((d.shape[0], step, lanes), lambda i, *_: (0, i + first, 0)) for d in ds],
             out_specs=whole((96, sum(levels) // 2)),
-            scratch_shapes=[pltpu.VMEM((lanes // 128, 256, 128), F32)],
         ),
         out_shape=jax.ShapeDtypeStruct((96, sum(levels) // 2), F32),
         compiler_params=pltpu.CompilerParams(vmem_limit_bytes=LIMIT),
@@ -1180,7 +1197,7 @@
     text_len = length - visual_len
     width = w_query.shape[1]
     dp, ffn = lax.axis_size("dp"), lax.axis_size("ffn")
-    place, here = lax.axis_index("dp"), lax.axis_index("ffn")
+    place = lax.axis_index("dp")
     devices = dp * ffn
     rows = pl.cdiv(length, 64) * 64
     count = visual_maps.shape[0] * devices
@@ -1192,8 +1209,14 @@
 
     first_set = Gather(*pack_first(w_query, w_key, w_value, vis_proj, visual_maps))
     plain = columns == width
+    early = plain and dp == 8
+    here = lax.axis_index("ffn")
     wide_shards = jnp.concatenate([outer_shard, w_inner], 0)
-    if plain:
+    if early:
+        late_set = Gather(
+            jnp.concatenate([w_output, wide_shards], 0), [w_output.shape[0]], 2 * inner_rows
+        )
+    elif plain:
         late_set = Gather(
             jnp.concatenate([w_output, wide_shards], 0), [w_output.shape[0], inner_rows, inner_rows]
         )
@@ -1201,21 +1224,28 @@
         late_set = Gather(w_output, [w_output.shape[0]])
         wide_set = Gather(wide_shards, [inner_rows, inner_rows])
 
+    first_set.own, wide_shards = epoch(first_set.own, wide_shards)
     first_set.along_ffn()
+    wides = [wide_shards]
+    if early:
+        wides += [send_dp(wide_shards, 2), send_dp(wide_shards, 4)]
     tables = jnp.concatenate([x_table, y_table, rel_table], 0).T
     tables = jnp.pad(tables, ((0, 0), (0, 256 - tables.shape[1])))
-    cuts = [0, steps * 2 // 9, steps * 6 // 9, steps]
+    cuts = [0, steps // 9, steps * 7 // 9, steps]
     words = [None] * 3
     words[0], unit = bias_words(rel_bucket, x_bucket, y_bucket, tables, 0, cuts[1])
     ranges = document_blocks(segment_ids[0], rows)
     lines = jnp.stack([first_gain, first_bias, b_outer, second_gain, second_bias])
     inner_b = b_inner.reshape(ffn, 1, columns)
-    segments = jnp.pad(segment_ids[0], (0, rows - length), constant_values=-1)
-    segments = (segments[:, None], segments[None, :])
+    segments = jnp.pad(segment_ids, ((0, 0), (0, rows - length)), constant_values=-1)
     bn_lines = jnp.stack([bn_scale, bn_shift])
-    state, late, words[0], tables, ranges, lines, inner_b, segments, bn_lines = epoch(
+    order = [(here - k + ffn) % ffn if early else jnp.int32(k) for k in range(ffn)]
+    place = jnp.stack([place] + order).astype(jnp.int32)
+    state, late, place, wides, words[0], tables, ranges, lines, inner_b, segments, bn_lines = epoch(
         first_set.state(),
         late_set.state(),
+        place,
+        wides,
         words[0],
         tables,
         ranges,
@@ -1248,18 +1278,20 @@
     late_set.hold(late)
 
     late_rows = w_output.shape[0] * ffn
-    late_set.near(late_rows + ffn * inner_rows if plain else 0)
+    late_set.near(late_rows + (inner_rows if early else ffn * inner_rows) if plain else 0)
+    if early:
+        wides += [send_dp(wide, 1) for wide in wides[:2]]
     layout, row = [], 0
     for n, size in enumerate(first_set.rows):
         layout.append((row, size * ffn, max(n - 2, 0), 0, n * width if n < 3 else 0))
         row += size * ffn
-    order_col = patch_order.reshape(visual_len, 1)
     qkv_full, proj_full, hidden, lowered, qkv, bn_rows, bn_stats = first_rows(
+        place,
         first_set.parts(),
         layout,
         text_hidden,
         visual_maps,
-        order_col,
+        patch_order,
         bn_lines,
         rows,
         vis_proj.shape[0] * devices,
@@ -1267,12 +1299,14 @@
     )
     qkv, tables = epoch(qkv, tables)
     words[2], _ = bias_words(rel_bucket, x_bucket, y_bucket, tables, cuts[2], cuts[3] - cuts[2])
-    qkv, state, words[2] = epoch(qkv, late_set.state(), words[2])
+    qkv, state, words[2], wides = epoch(qkv, late_set.state(), words[2], wides)
     late_set.hold(state)
 
     late_set.diagonal()
+    if early:
+        wides.append(send_dp(wides[1], 4))
     probs, mixed = attend(unit, qkv, words, segments)
-    probs, mixed, state = epoch(probs, mixed, late_set.state())
+    probs, mixed, state, wides = epoch(probs, mixed, late_set.state(), wides)
     late_set.hold(state)
     late_set.across()
     layout = [(0, late_rows, 0, 0, 0)]
@@ -1294,6 +1328,20 @@
     feeds = [(parts, layout + wide_layout if plain else layout)]
     if not plain:
         feeds.append((wide_set.parts(), wide_layout))
+    if early:
+        near_layout = [(n * inner_rows, inner_rows, 1 + n, 0, 0) for n in range(2)]
+        far_layout = [
+            (late_rows + (2 * k - 2 + n) * inner_rows, inner_rows, 1 + n, k * width, 0)
+            for k in range(1, ffn)
+            for n in range(2)
+        ]
+        own, from_x, from_y, other, other_x, from_xy = wides
+        crossed = [send_dp(from_y, 1), send_dp(from_xy, 1)]
+        blocks = [own, other, from_x, other_x, from_y, crossed[0], from_xy, crossed[1]]
+        feeds = [
+            (parts, layout + far_layout),
+            ([(block, bits, 0) for bits, block in enumerate(blocks)], near_layout),
+        ]
     (
         first_n,
         output_full,
@@ -1304,16 +1352,22 @@
         inner_sums,
         mine,
         away,
-    ) = feed_forward(feeds, mixed, hidden, lines, inner_b, cotangent, inner_rows)
-
-    wide = Scatter(mine, away, lambda value, index: pick(value, index, 1))
+        last,
+    ) = feed_forward(place, feeds, mixed, hidden, lines, inner_b, cotangent, inner_rows)
+
+    def wide_far(value, index):
+        return pick(value, (here - index + ffn) % ffn if early else index, 1)
+
+    wide = Scatter(mine, away, wide_far)
+    wide.ahead(last)
+    state, grad_first = epoch(wide.held(), grad_first)
+    wide.hold(state)
+    wide.near()
     wide.core()
-    grad_attn, attn_low, grad_mixed, sums_one = norm_rows(grad_first, first_n, first_r, lines, output_full)
-    state, grad_mixed = epoch(wide.held(), grad_mixed)
-    wide.hold(state)
-
-    wide.near()
-    half = pairs // 2
+    grad_attn, attn_low, grad_mixed, sums_one = norm_rows(
+        grad_first, first_n, first_r, lines, output_full
+    )
+    half = pairs // 3
     back_low = attend_back(qkv, grad_mixed, probs, 0, half)
     state, back_low, qkv = epoch(wide.held(), back_low, qkv)
     wide.hold(state)
@@ -1323,11 +1377,13 @@
     wide.quads()
     back_high = attend_back(qkv, grad_mixed, probs, half, pairs - half)
     back = list(zip(back_low[1:], back_high[1:]))
-    tokens_grad, mine, away = tail_rows(
-        back, qkv_full, grad_attn, attn_low, mixed, lowered, order_col, bn_rows, text_len
+    tokens_grad, mine, away, last = tail_rows(
+        place, back, qkv_full, grad_attn, attn_low, mixed, lowered, patch_order, bn_rows, text_len
     )
     ds = (back_low[0], back_high[0])
-    wide.blocks, mine, away, ds, tokens_grad = epoch(wide.blocks, mine, away, ds, tokens_grad)
+    wide.blocks, mine, away, last, ds, tokens_grad = epoch(
+        wide.blocks, mine, away, last, ds, tokens_grad
+    )
 
     def tail_far(value, index):
         size = 4 * (width // dp)
@@ -1336,7 +1392,7 @@
             [square.reshape(-1, width), pick(value[size:].reshape(ffn, -1, width), index, 0)], 0
         )
 
-    cuts = [0, steps // 3, steps]
+    cuts = [0, rows // 96 // 3, rows // 96]
     sums = []
 
     def tables(ds):
@@ -1348,30 +1404,27 @@
         ]
 
     tail = Scatter(mine, away, tail_far)
+    tail.ahead(last)
+    wide.join()
+    state, wide.value, tokens_grad = epoch(tail.held(), wide.value, tokens_grad)
+    tail.hold(state)
+    tail.near()
     tail.core()
-    wide.join()
-    wide.along_ffn(1, 2)
+    wide.along_ffn([1])
     grad_bn, bn_sums = batch_rows(tokens_grad, visual_maps, bn_stats, proj_full)
-    state, bn_sums, ds, wide.pieces = epoch(tail.held(), bn_sums, ds, wide.pieces)
-    tail.hold(state)
-
-    tail.near()
-    if ffn > 2:
-        wide.along_ffn(2, 3)
     sums = tables(ds)
-    state, ds, sums, wide.pieces = epoch(tail.held(), ds, sums, wide.pieces)
+    state, bn_sums, ds, sums, wide.pieces = epoch(tail.held(), bn_sums, ds, sums, wide.pieces)
     tail.hold(state)
     tail.prepare()
     tail.blocks, ds = epoch(tail.blocks, ds)
 
     tail.quads()
-    if ffn > 3:
-        wide.along_ffn(3)
+    wide.along_ffn(range(2, ffn))
     sums = tables(ds)
     tail.blocks, sums, back, wide.pieces = epoch(tail.blocks, sums, back, wide.pieces)
 
     tail.join()
-    tail.along_ffn(1, 2)
+    tail.along_ffn([1])
     total = Sum(
         pack_sums(
             bn_sums,
@@ -1387,8 +1440,7 @@
     wide_sum = wide.total()
     state, total.values, back = epoch(tail.held(), total.values, back)
     tail.hold(state)
-    if ffn > 2:
-        tail.along_ffn(2)
+    tail.along_ffn(range(2, ffn))
     while len(total.steps) > 1:
         total.step()
     text_grad = text_rows(back, qkv_full, grad_attn, text_len)

time: 323 us -> 305 us (0.944)
  waiting for transfers between devices: 72.7 us -> 47 us
  starting transfers between devices: 35.3 us -> 47.9 us
  local copies, waits for them, and re-layouts: 16.9 us -> 12.2 us
  Pallas kernels: 174 us -> 170 us
    ppermute x12, waiting for transfers between devices: 31.1 us -> 16.6 us  [send_ffn(): lax.ppermute(values, 'ffn', [(i, (i + shift) % size) for i in range(size)])]
    ppermute x31 -> x40, waiting for transfers between devices: 30.6 us -> 22.2 us  [send_dp(): return lax.ppermute(values, 'dp', [(i, i ^ bits) for i in range(size)])]
    ppermute x31 -> x40, starting transfers between devices: 19.8 us -> 27.3 us  [send_dp(): return lax.ppermute(values, 'dp', [(i, i ^ bits) for i in range(size)])]
    ppermute x12, starting transfers between devices: 15.4 us -> 18.8 us  [send_ffn(): lax.ppermute(values, 'ffn', [(i, (i + shift) % size) for i in range(size)])]
    unnamed x79 -> x103, local copies, waits for them, and re-layouts: 7.54 us -> 6.01 us
  transfers between devices with their start and end apart: 45 -> 54, of which waited for: 21 -> 20; matrix products, arithmetic and copies ran while one was open for 6% -> 6% of each run, Pallas kernels for 42% -> 43%
where the time goes in v2:
time: 305 us; the launch traced here: 300 us
  Pallas kernels  170 us (56%)
  starting transfers between devices  47.9 us (16%)
  waiting for transfers between devices  47 us (15%)
  other arithmetic  20.3 us (7%)
  local copies, waits for them, and re-layouts  12.2 us (4%)
    pallas_call x1, Pallas kernels, feed_forward(): pl.pallas_call(functools.partial(feed_kernel, entries, place_bits(parts),...  34.2 us
    ppermute x40, starting transfers between devices, send_dp(): return lax.ppermute(values, 'dp', [(i, i ^ bits) for i in range(size)])  27.3 us
    pallas_call x2, Pallas kernels, table_sums(): pl.pallas_call(functools.partial(table_kernel, first, levels), grid_spec=...  25.6 us
    pallas_call x3, Pallas kernels, bias_words(): pl.pallas_call(functools.partial(bias_kernel, step), grid=(steps,), in_sp...  24.7 us
    ppermute x40, waiting for transfers between devices, send_dp(): return lax.ppermute(values, 'dp', [(i, i ^ bits) for i in range(size)])  22.2 us
    pallas_call x2, Pallas kernels, attend_back(): pl.pallas_call(attend_back_kernel, grid=(pairs,), in_specs=[col[0], col[1...  19.4 us
    ppermute x12, starting transfers between devices, send_ffn(): lax.ppermute(values, 'ffn', [(i, (i + shift) % size) for i in range(size)])  18.8 us
    ppermute x12, waiting for transfers between devices, send_ffn(): lax.ppermute(values, 'ffn', [(i, (i + shift) % size) for i in range(size)])  16.6 us
  transfers between devices with their start and end apart: 54, of which 20 were waited for; matrix products, arithmetic and copies ran while one was open for 6% of the time, Pallas kernels for 43%

profile of v2, /device:TPU:0, one launch (start us, length us, event | category | flops | bytes accessed | tf_op | source)
XLA Modules:
  0.0 299.5 jit_solution(3332703065063842085)
XLA Ops:
  3.9 3.0 %collective-permute-start = (bf16[152,768]{1,0:T(8,128)(2,1)}, bf16[152,768]{1,0:T(8,128)(2,1)}, u32[]{:S(2)}, u32[]{:S(2)}) collective-permute-start(bf16[152,768]{1,0:T(8,128)(2,1)} %pack_first.1.refs_0_), channel_id=1, source_target_pairs={{0,1},{1,2},{2,3},{3,0},{4,5},{5,6},{6,7},{7,4},{8,9},{9,10},{10,1... | collective-permute-start | bytes 700424 | tf_op jit(solution)/shard_map/ppermute | solution.py:42
  6.9 2.6 collective-permute-start.1
  23.1 4.1 %bias_words.3 = (s32[6,64,640]{2,1,0:T(8,128)}, f32[1,1]{1,0:T(1,128)}) custom-call(s32[1,561,561]{2,1,0:T(8,128)} %copy.77.rel_ref, s32[1,561,561]{2,1,0:T(8,128)} %copy.78.x_ref, s32[1,561,561]{2,1,0:T(8,128)} %copy.79.y_ref, f32[12,256]{1,0:T(8,128)} %pad.8.tab_ref), custom_call_target="tpu_custom_call" | custom-call | bytes 6000 | tf_op jit(solution)/shard_map/bias_words/pallas_call | solution.py:939
  32.4 3.5 %collective-permute-start.8 = (bf16[216,768]{1,0:T(8,128)(2,1)S(1)}, bf16[216,768]{1,0:T(8,128)(2,1)S(1)}, u32[]{:S(2)}, u32[]{:S(2)}) collective-permute-start(bf16[216,768]{1,0:T(8,128)(2,1)S(1)} %pad_maximum_fusion.4.refs_0_), channel_id=1, source_target_pairs={{0,1},{1,2},{2,3},{3,0},{4,5},{5,6},{6,7},{7,4},{8,9},{9,10},{10,1... | collective-permute-start | bytes 995336 | tf_op jit(solution)/shard_map/ppermute | solution.py:42
  37.5 14.5 %bias_words.4 = (s32[6,384,640]{2,1,0:T(8,128)}, f32[1,1]{1,0:T(1,128)}) custom-call(s32[1,561,561]{2,1,0:T(8,128)} %copy.77.rel_ref, s32[1,561,561]{2,1,0:T(8,128)} %copy.78.x_ref, s32[1,561,561]{2,1,0:T(8,128)} %copy.79.y_ref, f32[12,256]{1,0:T(8,128)} %pad.8.tab_ref), custom_call_target="tpu_custom_call" | custom-call | bytes 36000 | tf_op jit(solution)/shard_map/bias_words/pallas_call | solution.py:939
  52.0 7.6 %collective-permute-done.9.refs_2_ = bf16[216,768]{1,0:T(8,128)(2,1)S(1)} collective-permute-done((bf16[216,768]{1,0:T(8,128)(2,1)S(1)}, bf16[216,768]{1,0:T(8,128)(2,1)S(1)}, u32[]{:S(2)}, u32[]{:S(2)}) %collective-permute-start.9) | collective-permute-done | bytes 331808 | tf_op jit(solution)/shard_map/ppermute | solution.py:42
  62.8 8.9 %collective-permute-done.14.refs_3_ = bf16[216,768]{1,0:T(8,128)(2,1)S(1)} collective-permute-done((bf16[216,768]{1,0:T(8,128)(2,1)S(1)}, bf16[216,768]{1,0:T(8,128)(2,1)S(1)}, u32[]{:S(2)}, u32[]{:S(2)}) %collective-permute-start.14) | collective-permute-done | bytes 331808 | tf_op jit(solution)/shard_map/ppermute | solution.py:42
  74.1 2.7 order_blocks.3.refs_0_
  79.6 11.3 %first_rows.1 = (bf16[768,2304]{1,0:T(8,128)(2,1)}, bf16[2048,768]{1,0:T(8,128)(2,1)}, f32[576,768]{1,0:T(8,128)}, bf16[768,576]{1,0:T(8,128)(2,1)}, bf16[576,23...) custom-call(s32[5]{0:T(128)} %stack.50.place_ref, bf16[608,768]{1,0:T(8,128)(2,1)} %order_blocks.2.refs_0_, ...), custom_call_target="tpu_custom_call" | custom-call | bytes 25000 | tf_op jit(solution)/shard_map/first_rows/pallas_call | solution.py:407
  90.9 6.1 %bias_words.5 = (s32[6,128,640]{2,1,0:T(8,128)}, f32[1,1]{1,0:T(1,128)}) custom-call(s32[1,561,561]{2,1,0:T(8,128)} %copy.77.rel_ref, s32[1,561,561]{2,1,0:T(8,128)} %copy.78.x_ref, s32[1,561,561]{2,1,0:T(8,128)} %copy.79.y_ref, f32[12,256]{1,0:T(8,128)} %pad.8.tab_ref), custom_call_target="tpu_custom_call" | custom-call | bytes 12000 | tf_op jit(solution)/shard_map/bias_words/pallas_call | solution.py:939
  97.1 4.7 %collective-permute-done.17.refs_2_ = bf16[672,768]{1,0:T(8,128)(2,1)S(1)} collective-permute-done((bf16[672,768]{1,0:T(8,128)(2,1)}, bf16[672,768]{1,0:T(8,128)(2,1)S(1)}, u32[]{:S(2)}, u32[]{:S(2)}) %collective-permute-start.17) | collective-permute-done | bytes 1032224 | tf_op jit(solution)/shard_map/ppermute | solution.py:37
  106.4 14.5 %attend.1 = (bf16[12,576,576]{2,1,0:T(8,128)(2,1)}, bf16[576,768]{1,0:T(8,128)(2,1)}) custom-call(f32[1,1]{1,0:T(1,128)} %get-tuple-element.227.unit_ref, bf16[576,2304]{1,0:T(8,128)(2,1)} %get-tuple-element.336.q_ref.k_ref.v_ref, bf16[576,2304]{1,0:T(8,128)(2,1)} %get-tuple-element.336.q_ref.k_ref.v_ref, ...), custom_call_target="tpu_custom_call" | custom-call | flops 2038431 | bytes 40000 | tf_op jit(solution)/shard_map/attend/pallas_call | solution.py:993
  126.0 34.2 %feed_forward.1 = (f32[576,768]{1,0:T(8,128)}, bf16[768,768]{1,0:T(8,128)(2,1)}, bf16[561,768]{1,0:T(8,128)(2,1)}, f32[576,1]{1,0:T(8,128)}, f32[576,768]{1,0:T(...) custom-call(s32[5]{0:T(128)} %stack.50.place_ref, ...), custom_call_target="tpu_custom_call" | custom-call | bytes 100000 | tf_op jit(solution)/shard_map/feed_forward/pallas_call | solution.py:587
  160.5 2.9 collective-permute-done.31
  167.2 5.4 %norm_rows.1 = (f32[576,768]{1,0:T(8,128)}, bf16[576,768]{1,0:T(8,128)(2,1)}, bf16[576,768]{1,0:T(8,128)(2,1)}, f32[2,768]{1,0:T(2,128)}) custom-call(f32[576,768]{1,0:T(8,128)} %get-tuple-element.318.grad_ref, f32[576,768]{1,0:T(8,128)} %get-tuple-element.319.normed_ref, f32[576,1]{1,0:T(8,128)} %get-tuple-element.320.scale_ref, ...), custom_call_target="tpu_custom_call" | custom-call | bytes 12000 | tf_op jit(solution)/shard_map/norm_rows/pallas_call | solution.py:647
  172.6 7.5 %attend_back.2 = (bf16[4,576,640]{2,1,0:T(8,128)(2,1)}, bf16[576,256]{1,0:T(8,128)(2,1)}, bf16[576,256]{1,0:T(8,128)(2,1)}, bf16[576,256]{1,0:T(8,128)(2,1)}) custom-call(bf16[576,2304]{1,0:T(8,128)(2,1)} %get-tuple-element.336.q_ref.k_ref.v_ref, bf16[576,2304]{1,0:T(8,128)(2,1)} %get-tuple-element.336.q_ref.k_ref.v_ref, ...), custom_call_target="tpu_custom_call" | custom-call | flops 1358954 | bytes 16000 | tf_op jit(solution)/shard_map/attend_back/pallas_call | solution.py:1050
  186.7 11.8 %attend_back.3 = (bf16[8,576,640]{2,1,0:T(8,128)(2,1)}, bf16[576,512]{1,0:T(8,128)(2,1)}, bf16[576,512]{1,0:T(8,128)(2,1)}, bf16[576,512]{1,0:T(8,128)(2,1)}) custom-call(bf16[576,2304]{1,0:T(8,128)(2,1)} %get-tuple-element.336.q_ref.k_ref.v_ref, bf16[576,2304]{1,0:T(8,128)(2,1)} %get-tuple-element.336.q_ref.k_ref.v_ref, ...), custom_call_target="tpu_custom_call" | custom-call | flops 2717908 | bytes 32000 | tf_op jit(solution)/shard_map/attend_back/pallas_call | solution.py:1050
  198.5 14.6 %tail_rows.1 = (bf16[49,768]{1,0:T(8,128)(2,1)}, bf16[4,640,768]{2,1,0:T(8,128)(2,1)}, bf16[4,640,768]{2,1,0:T(8,128)(2,1)}, bf16[640,768]{1,0:T(8,128)(2,1)}) custom-call(s32[5]{0:T(128)} %stack.50.place_ref, bf16[576,256]{1,0:T(8,128)(2,1)} %get-tuple-element.398.refs_0_, bf16[576,512]{1,0:T(8,128)(2,1)} %get-tuple-element.399.refs_1_, ...), custom_call_target="tpu_custom_call" | custom-call | bytes 40000 | tf_op jit(solution)/shard_map/tail_rows/pallas_call | solution.py:733
  219.8 9.6 %table_sums.2.refs_0_ = f32[96,80]{1,0:T(8,128)} custom-call(s32[36]{0:T(128)} %get-tuple-element.368.block_ref, s32[36]{0:T(128)} %get-tuple-element.369.count_ref, s32[1,561,561]{2,1,0:T(8,128)} %copy.77.rel_ref, s32[1,561,561]{2,1,0:T(8,128)} %copy.78.x_ref, s32[1,561,561]{2,1,0:T(8,128)} %copy.79.y_ref, bf16[4,576,640]{2,1,0:T(8,128)(2,1)} %get-tuple-element.380.refs_0_, ...), custom_call_target="tpu_custom_call" | custom-call | bytes 16000 | tf_op jit(solution)/shard_map/table_sums/pallas_call | solution.py:1125
  229.3 3.9 %batch_rows.1 = (f32[49,2048]{1,0:T(8,128)}, f32[2,2048]{1,0:T(2,128)}) custom-call(bf16[49,768]{1,0:T(8,128)(2,1)} %get-tuple-element.362.tokens_ref, bf16[49,2048]{1,0:T(8,128)(2,1)} %refs_3_.1, f32[2,2048]{1,0:T(2,128)} %get-tuple-element.363.stats_ref.refs_4_, bf16[2048,768]{1,0:T(8,128)(2,1)} %get-tuple-element.364.proj_ref), custom_call_target="tpu_custom_call" | custom-call | bytes 6000 | tf_op jit(solution)/shard_map/batch_rows/pallas_call | solution.py:764
  237.8 3.3 %collective-permute-start.43 = (bf16[640,768]{1,0:T(8,128)(2,1)S(1)}, bf16[640,768]{1,0:T(8,128)(2,1)}, u32[]{:S(2)}, u32[]{:S(2)}) collective-permute-start(bf16[640,768]{1,0:T(8,128)(2,1)S(1)} %pad_maximum_fusion.3), channel_id=1, source_target_pairs={{0,16},{4,20},{8,24},{12,28},{16,0},{20,4},{24,8},{28,12},{1,17},{... | collective-permute-start | bytes 2949128 | tf_op jit(solution)/shard_map/ppermute | solution.py:37
  243.7 16.1 %table_sums.3.refs_1_ = f32[96,80]{1,0:T(8,128)} custom-call(s32[36]{0:T(128)} %get-tuple-element.368.block_ref, s32[36]{0:T(128)} %get-tuple-element.369.count_ref, s32[1,561,561]{2,1,0:T(8,128)} %copy.77.rel_ref, s32[1,561,561]{2,1,0:T(8,128)} %copy.78.x_ref, s32[1,561,561]{2,1,0:T(8,128)} %copy.79.y_ref, bf16[4,576,640]{2,1,0:T(8,128)(2,1)} %get-tuple-element.380.refs_0_, ...), custom_call_target="tpu_custom_call" | custom-call | bytes 32000 | tf_op jit(solution)/shard_map/table_sums/pallas_call | solution.py:1125
  273.9 6.8 %collective-permute-done.48 = f32[24,768]{1,0:T(8,128)S(1)} collective-permute-done((f32[24,768]{1,0:T(8,128)S(1)}, f32[24,768]{1,0:T(8,128)S(1)}, u32[]{:S(2)}, u32[]{:S(2)}) %collective-permute-start.48) | collective-permute-done | bytes 73760 | tf_op jit(solution)/shard_map/ppermute | solution.py:47
  289.1 5.8 %text_rows.1 = f32[512,768]{1,0:T(8,128)} custom-call(bf16[576,256]{1,0:T(8,128)(2,1)} %get-tuple-element.398.refs_0_, bf16[576,512]{1,0:T(8,128)(2,1)} %get-tuple-element.399.refs_1_, bf16[576,256]{1,0:T(8,128)(2,1)} %get-tuple-element.400.refs_2_, bf16[576,512]{1,0:T(8,128)(2,1)} %get-tuple-element.401.refs_3_, ...), custom_call_target="tpu_custom_call" | custom-call | bytes 25000 | tf_op jit(solution)/shard_map/text_rows/pallas_call | solution.py:791
  (269 shorter events, 92.3 us)
Async XLA Ops:
  3.9 25.1 %collective-permute-start = (bf16[152,768]{1,0:T(8,128)(2,1)}, bf16[152,768]{1,0:T(8,128)(2,1)}, u32[]{:S(2)}, u32[]{:S(2)}) collective-permute-start(bf16[152,768]{1,0:T(8,128)(2,1)} %pack_first.1.refs_0_), channel_id=1, source_target_pairs={{0,1},{1,2},{2,3},{3,0},{4,5},{5,6},{6,7},{7,4},{8,9},{9,10},{10,1... | collective-permute-start | bytes 700424 | tf_op jit(solution)/shard_map/ppermute | solution.py:42
  6.9 22.1 %collective-permute-start.1 = (bf16[152,768]{1,0:T(8,128)(2,1)}, bf16[152,768]{1,0:T(8,128)(2,1)}, u32[]{:S(2)}, u32[]{:S(2)}) collective-permute-start(bf16[152,768]{1,0:T(8,128)(2,1)} %pack_first.1.refs_0_), channel_id=1, source_target_pairs={{0,2},{1,3},{2,0},{3,1},{4,6},{5,7},{6,4},{7,5},{8,10},{9,11},{10,... | collective-permute-start | bytes 700424 | tf_op jit(solution)/shard_map/ppermute | solution.py:42
  9.5 19.5 %collective-permute-start.2 = (bf16[152,768]{1,0:T(8,128)(2,1)}, bf16[152,768]{1,0:T(8,128)(2,1)}, u32[]{:S(2)}, u32[]{:S(2)}) collective-permute-start(bf16[152,768]{1,0:T(8,128)(2,1)} %pack_first.1.refs_0_), channel_id=1, source_target_pairs={{0,3},{1,0},{2,1},{3,2},{4,7},{5,4},{6,5},{7,6},{8,11},{9,8},{10,9... | collective-permute-start | bytes 700424 | tf_op jit(solution)/shard_map/ppermute | solution.py:42
  10.8 18.2 %collective-permute-start.3 = (bf16[192,768]{1,0:T(8,128)(2,1)S(1)}, bf16[192,768]{1,0:T(8,128)(2,1)}, u32[]{:S(2)}, u32[]{:S(2)}) collective-permute-start(bf16[192,768]{1,0:T(8,128)(2,1)S(1)} %pad_maximum_fusion.5.refs_10_), channel_id=1, source_target_pairs={{0,8},{4,12},{8,0},{12,4},{16,24},{20,28},{24,16},{28,20},{1,9},{5... | collective-permute-start | bytes 884744 | tf_op jit(solution)/shard_map/ppermute | solution.py:37
  31.4 28.2 %collective-permute-start.5 = (bf16[608,768]{1,0:T(8,128)(2,1)}, bf16[608,768]{1,0:T(8,128)(2,1)S(1)}, u32[]{:S(2)}, u32[]{:S(2)}) collective-permute-start(bf16[608,768]{1,0:T(8,128)(2,1)} %order_blocks.2.refs_0_), channel_id=1, source_target_pairs={{0,8},{4,12},{8,0},{12,4},{16,24},{20,28},{24,16},{28,20},{1,9},{5... | collective-permute-start | bytes 2801672 | tf_op jit(solution)/shard_map/ppermute | solution.py:37
  31.9 27.7 %collective-permute-start.6 = (bf16[608,768]{1,0:T(8,128)(2,1)}, bf16[608,768]{1,0:T(8,128)(2,1)S(1)}, u32[]{:S(2)}, u32[]{:S(2)}) collective-permute-start(bf16[608,768]{1,0:T(8,128)(2,1)} %order_blocks.2.refs_0_), channel_id=1, source_target_pairs={{0,16},{4,20},{8,24},{12,28},{16,0},{20,4},{24,8},{28,12},{1,17},{... | collective-permute-start | bytes 2801672 | tf_op jit(solution)/shard_map/ppermute | solution.py:37
  32.4 27.2 %collective-permute-start.7 = (bf16[608,768]{1,0:T(8,128)(2,1)}, bf16[608,768]{1,0:T(8,128)(2,1)S(1)}, u32[]{:S(2)}, u32[]{:S(2)}) collective-permute-start(bf16[608,768]{1,0:T(8,128)(2,1)} %order_blocks.2.refs_0_), channel_id=1, source_target_pairs={{0,4},{4,0},{8,12},{12,8},{16,20},{20,16},{24,28},{28,24},{1,5},{5... | collective-permute-start | bytes 2801672 | tf_op jit(solution)/shard_map/ppermute | solution.py:37
  32.4 19.5 %collective-permute-start.8 = (bf16[216,768]{1,0:T(8,128)(2,1)S(1)}, bf16[216,768]{1,0:T(8,128)(2,1)S(1)}, u32[]{:S(2)}, u32[]{:S(2)}) collective-permute-start(bf16[216,768]{1,0:T(8,128)(2,1)S(1)} %pad_maximum_fusion.4.refs_0_), channel_id=1, source_target_pairs={{0,1},{1,2},{2,3},{3,0},{4,5},{5,6},{6,7},{7,4},{8,9},{9,10},{10,1... | collective-permute-start | bytes 995336 | tf_op jit(solution)/shard_map/ppermute | solution.py:42
  35.9 23.7 %collective-permute-start.9 = (bf16[216,768]{1,0:T(8,128)(2,1)S(1)}, bf16[216,768]{1,0:T(8,128)(2,1)S(1)}, u32[]{:S(2)}, u32[]{:S(2)}) collective-permute-start(bf16[216,768]{1,0:T(8,128)(2,1)S(1)} %pad_maximum_fusion.4.refs_0_), channel_id=1, source_target_pairs={{0,2},{1,3},{2,0},{3,1},{4,6},{5,7},{6,4},{7,5},{8,10},{9,11},{10,... | collective-permute-start | bytes 995336 | tf_op jit(solution)/shard_map/ppermute | solution.py:42
  76.9 24.9 %collective-permute-start.17 = (bf16[672,768]{1,0:T(8,128)(2,1)}, bf16[672,768]{1,0:T(8,128)(2,1)S(1)}, u32[]{:S(2)}, u32[]{:S(2)}) collective-permute-start(bf16[672,768]{1,0:T(8,128)(2,1)} %order_blocks.3.refs_0_), channel_id=1, source_target_pairs={{0,8},{4,12},{8,0},{12,4},{16,24},{20,28},{24,16},{28,20},{1,9},{5... | collective-permute-start | bytes 3096584 | tf_op jit(solution)/shard_map/ppermute | solution.py:37
  77.9 24.4 %collective-permute-start.18 = (bf16[672,768]{1,0:T(8,128)(2,1)}, bf16[672,768]{1,0:T(8,128)(2,1)S(1)}, u32[]{:S(2)}, u32[]{:S(2)}) collective-permute-start(bf16[672,768]{1,0:T(8,128)(2,1)} %order_blocks.3.refs_0_), channel_id=1, source_target_pairs={{0,16},{4,20},{8,24},{12,28},{16,0},{20,4},{24,8},{28,12},{1,17},{... | collective-permute-start | bytes 3096584 | tf_op jit(solution)/shard_map/ppermute | solution.py:37
  79.1 23.3 %collective-permute-start.19 = (bf16[672,768]{1,0:T(8,128)(2,1)}, bf16[672,768]{1,0:T(8,128)(2,1)S(1)}, u32[]{:S(2)}, u32[]{:S(2)}) collective-permute-start(bf16[672,768]{1,0:T(8,128)(2,1)} %order_blocks.3.refs_0_), channel_id=1, source_target_pairs={{0,4},{4,0},{8,12},{12,8},{16,20},{20,16},{24,28},{28,24},{1,5},{5... | collective-permute-start | bytes 3096584 | tf_op jit(solution)/shard_map/ppermute | solution.py:37
  79.1 18.0 %collective-permute-start.20 = (bf16[192,768]{1,0:T(8,128)(2,1)S(1)}, bf16[192,768]{1,0:T(8,128)(2,1)S(1)}, u32[]{:S(2)}, u32[]{:S(2)}) collective-permute-start(bf16[192,768]{1,0:T(8,128)(2,1)S(1)} %pad_maximum_fusion.5.refs_10_), channel_id=1, source_target_pairs={{0,4},{4,0},{8,12},{12,8},{16,20},{20,16},{24,28},{28,24},{1,5},{5... | collective-permute-start | bytes 884744 | tf_op jit(solution)/shard_map/ppermute | solution.py:37
  79.6 17.5 %collective-permute-start.21 = (bf16[192,768]{1,0:T(8,128)(2,1)}, bf16[192,768]{1,0:T(8,128)(2,1)S(1)}, u32[]{:S(2)}, u32[]{:S(2)}) collective-permute-start(bf16[192,768]{1,0:T(8,128)(2,1)} %collective-permute-done.3.refs_12_), channel_id=1, source_target_pairs={{0,4},{4,0},{8,12},{12,8},{16,20},{20,16},{24,28},{28,24},{1,5},{5... | collective-permute-start | bytes 884744 | tf_op jit(solution)/shard_map/ppermute | solution.py:37
  102.3 19.2 %collective-permute-start.24 = (bf16[672,768]{1,0:T(8,128)(2,1)S(1)}, bf16[672,768]{1,0:T(8,128)(2,1)S(1)}, u32[]{:S(2)}, u32[]{:S(2)}) collective-permute-start(bf16[672,768]{1,0:T(8,128)(2,1)S(1)} %collective-permute-done.17.refs_2_), channel_id=1, source_target_pairs={{0,4},{4,0},{8,12},{12,8},{16,20},{20,16},{24,28},{28,24},{1,5},{5... | collective-permute-start | bytes 3096584 | tf_op jit(solution)/shard_map/ppermute | solution.py:37
  102.4 19.1 %collective-permute-start.25 = (bf16[672,768]{1,0:T(8,128)(2,1)S(1)}, bf16[672,768]{1,0:T(8,128)(2,1)S(1)}, u32[]{:S(2)}, u32[]{:S(2)}) collective-permute-start(bf16[672,768]{1,0:T(8,128)(2,1)S(1)} %collective-permute-done.18.refs_4_), channel_id=1, source_target_pairs={{0,4},{4,0},{8,12},{12,8},{16,20},{20,16},{24,28},{28,24},{1,5},{5... | collective-permute-start | bytes 3096584 | tf_op jit(solution)/shard_map/ppermute | solution.py:37
  103.0 18.5 %collective-permute-start.23 = (bf16[480,768]{1,0:T(8,128)(2,1)S(1)}, bf16[480,768]{1,0:T(8,128)(2,1)S(1)}, u32[]{:S(2)}, u32[]{:S(2)}) collective-permute-start(bf16[480,768]{1,0:T(8,128)(2,1)S(1)} %slice.179), channel_id=1, source_target_pairs={{0,8},{4,12},{8,0},{12,4},{16,24},{20,28},{24,16},{28,20},{1,9},{5... | collective-permute-start | bytes 2211848 | tf_op jit(solution)/shard_map/ppermute | solution.py:37
  163.4 18.3 %collective-permute-start.32 = (bf16[4,2,4,96,768]{4,3,2,1,0:T(8,128)(2,1)}, bf16[4,2,4,96,768]{4,3,2,1,0:T(8,128)(2,1)}, u32[]{:S(2)}, u32[]{:S(2)}) collective-permute-start(bf16[4,2,4,96,768]{4,3,2,1,0:T(8,128)(2,1)} %get-tuple-element.315), channel_id=1, source_target_pairs={{0,4},{4,0},{8,12},{12,8},{16,20},{20,16},{24,28},{28,24},{1,5},{5... | collective-permute-start | bytes 14155784 | tf_op jit(solution)/shard_map/ppermute | solution.py:37
  184.5 28.6 %collective-permute-start.35 = (bf16[2,4,96,768]{3,2,1,0:T(8,128)(2,1)S(1)}, bf16[2,4,96,768]{3,2,1,0:T(8,128)(2,1)S(1)}, u32[]{:S(2)}, u32[]{:S(2)}) collective-permute-start(bf16[2,4,96,768]{3,2,1,0:T(8,128)(2,1)S(1)} %pad_maximum_fusion), channel_id=1, source_target_pairs={{0,8},{4,12},{8,0},{12,4},{16,24},{20,28},{24,16},{28,20},{1,9},{5... | collective-permute-start | bytes 3538952 | tf_op jit(solution)/shard_map/ppermute | solution.py:37
  185.4 27.7 %collective-permute-start.36 = (bf16[2,4,96,768]{3,2,1,0:T(8,128)(2,1)S(1)}, bf16[2,4,96,768]{3,2,1,0:T(8,128)(2,1)}, u32[]{:S(2)}, u32[]{:S(2)}) collective-permute-start(bf16[2,4,96,768]{3,2,1,0:T(8,128)(2,1)S(1)} %pad_maximum_fusion.1), channel_id=1, source_target_pairs={{0,16},{4,20},{8,24},{12,28},{16,0},{20,4},{24,8},{28,12},{1,17},{... | collective-permute-start | bytes 3538952 | tf_op jit(solution)/shard_map/ppermute | solution.py:37
  237.8 24.0 %collective-permute-start.42 = (bf16[640,768]{1,0:T(8,128)(2,1)}, bf16[640,768]{1,0:T(8,128)(2,1)S(1)}, u32[]{:S(2)}, u32[]{:S(2)}) collective-permute-start(bf16[640,768]{1,0:T(8,128)(2,1)} %pad_maximum_fusion.2), channel_id=1, source_target_pairs={{0,8},{4,12},{8,0},{12,4},{16,24},{20,28},{24,16},{28,20},{1,9},{5... | collective-permute-start | bytes 2949128 | tf_op jit(solution)/shard_map/ppermute | solution.py:37
  237.8 25.3 %collective-permute-start.43 = (bf16[640,768]{1,0:T(8,128)(2,1)S(1)}, bf16[640,768]{1,0:T(8,128)(2,1)}, u32[]{:S(2)}, u32[]{:S(2)}) collective-permute-start(bf16[640,768]{1,0:T(8,128)(2,1)S(1)} %pad_maximum_fusion.3), channel_id=1, source_target_pairs={{0,16},{4,20},{8,24},{12,28},{16,0},{20,4},{24,8},{28,12},{1,17},{... | collective-permute-start | bytes 2949128 | tf_op jit(solution)/shard_map/ppermute | solution.py:37
  241.1 18.7 %collective-permute-start.44 = (bf16[2,96,768]{2,1,0:T(8,128)(2,1)S(1)}, bf16[2,96,768]{2,1,0:T(8,128)(2,1)S(1)}, u32[]{:S(2)}, u32[]{:S(2)}) collective-permute-start(bf16[2,96,768]{2,1,0:T(8,128)(2,1)S(1)} %get-tuple-element.438), channel_id=1, source_target_pairs={{0,2},{1,3},{2,0},{3,1},{4,6},{5,7},{6,4},{7,5},{8,10},{9,11},{10,... | collective-permute-start | bytes 884744 | tf_op jit(solution)/shard_map/ppermute | solution.py:42
  241.7 18.1 %collective-permute-start.45 = (bf16[2,96,768]{2,1,0:T(8,128)(2,1)S(1)}, bf16[2,96,768]{2,1,0:T(8,128)(2,1)}, u32[]{:S(2)}, u32[]{:S(2)}) collective-permute-start(bf16[2,96,768]{2,1,0:T(8,128)(2,1)S(1)} %get-tuple-element.437), channel_id=1, source_target_pairs={{0,3},{1,0},{2,1},{3,2},{4,7},{5,4},{6,5},{7,6},{8,11},{9,8},{10,9... | collective-permute-start | bytes 884744 | tf_op jit(solution)/shard_map/ppermute | solution.py:42
  (80 other events, 802.4 us)

commit v3 on v2

--- a/solution.py
+++ b/solution.py
@@ -1059,17 +1059,20 @@
     )(qkv, qkv, qkv, grad, probs)
 
 
+GROUP = 48
+
+
 def table_kernel(first, levels, block_ref, count_ref, rel_ref, x_ref, y_ref, *refs):
     ds_refs, out_ref = refs[:-1], refs[-1]
     place = pl.program_id(0)
     step = rel_ref.shape[1]
     every = rel_ref.shape[2] // 128
+    heads = sum(ref.shape[0] for ref in ds_refs)
+    counts = (levels[1] // 2, levels[2] // 2, levels[0] // 2)
 
     @pl.when(place == 0)
     def _():
         out_ref[...] = jnp.zeros_like(out_ref)
-
-    heads = sum(ref.shape[0] for ref in ds_refs)
 
     def group(r, start, blocks):
         width = blocks * 128
@@ -1085,29 +1088,32 @@
             chosen = jnp.broadcast_to(top, (16, width)).astype(BF16) == one
             return [jnp.where(chosen, none, values), jnp.where(chosen, values, none)]
 
-        rows = pl.ds(pl.multiple_of(r * 16, 16), 16)
+        rows = pl.ds(pl.multiple_of(r * GROUP, GROUP), GROUP)
         lanes = pl.ds(pl.multiple_of(start * 128, 128), width)
         values = [ref[:, rows, lanes] for ref in ds_refs]
-        values.append(jnp.zeros((16 - heads, 16, width), BF16))
+        values.append(jnp.zeros((16 - heads, GROUP, width), BF16))
         values = jnp.transpose(jnp.concatenate(values, 0), (1, 0, 2))
-        total = out_ref[...]
         ids = [ref[0, rows, lanes].astype(F32) for ref in (x_ref, y_ref, rel_ref)]
-        counts = (levels[1] // 2, levels[2] // 2, levels[0] // 2)
         tops = [(i >= count).astype(F32) for i, count in zip(ids, counts)]
         rest = [i - top * count for i, top, count in zip(ids, tops, counts)]
-        for n in range(16):
-            grads = values[n]
-            hot, split = [], []
-            for top, low, count in zip(tops, rest, counts):
-                hot += one_hot(low[n : n + 1], count)
-                split += halves(grads, top[n : n + 1])
-            total = total + dot_nt(jnp.concatenate(split, 0), jnp.concatenate(hot, 0))
+        total = out_ref[...]
+        for begin in range(0, GROUP, 2):
+            lefts, rights = [], []
+            for n in (begin, begin + 1):
+                hot, split = [], []
+                for top, low, count in zip(tops, rest, counts):
+                    hot += one_hot(low[n : n + 1], count)
+                    split += halves(values[n], top[n : n + 1])
+                lefts.append(jnp.concatenate(split, 0))
+                rights.append(jnp.concatenate(hot, 0))
+            total = total + dot_nt(jnp.concatenate(lefts, 1), jnp.concatenate(rights, 1))
         out_ref[...] = total
 
     def body(r, _):
-        index = (place + first) * (step // 16) + r
-        start, count = block_ref[index], count_ref[index]
-        for blocks in range(1, every + 1):
+        index = (place + first) * (step // GROUP) + r
+        count = jnp.maximum(count_ref[index], 2)
+        start = jnp.minimum(block_ref[index], every - count)
+        for blocks in range(2, every + 1):
 
             @pl.when(count == blocks)
             def _(blocks=blocks):
@@ -1115,11 +1121,11 @@
 
         return 0
 
-    lax.fori_loop(0, step // 16, body, 0)
+    lax.fori_loop(0, step // GROUP, body, 0)
 
 
 def table_sums(ranges, rel, x, y, ds, levels, first, steps):
-    step = 96
+    step = 2 * GROUP
     lanes = ds[0].shape[2]
     ids = pl.BlockSpec((1, step, lanes), lambda i, *_: (0, i + first, 0))
     return pl.pallas_call(
@@ -1140,8 +1146,8 @@
 
 def document_blocks(segments, rows):
     length = segments.shape[0]
-    first = segments[0:rows:16]
-    last = segments[jnp.minimum(jnp.arange(15, rows, 16), length - 1)]
+    first = segments[0:rows:GROUP]
+    last = segments[jnp.minimum(jnp.arange(GROUP - 1, rows, GROUP), length - 1)]
     begin = jnp.sum(segments[None, :] < first[:, None], 1, dtype=jnp.int32)
     end = jnp.sum(segments[None, :] <= last[:, None], 1, dtype=jnp.int32)
     return begin // 128, (end + 127) // 128 - begin // 128
@@ -1392,7 +1398,8 @@
             [square.reshape(-1, width), pick(value[size:].reshape(ffn, -1, width), index, 0)], 0
         )
 
-    cuts = [0, rows // 96 // 3, rows // 96]
+    groups = rows // (2 * GROUP)
+    cuts = [0, groups]
     sums = []
 
     def tables(ds):
@@ -1412,8 +1419,7 @@
     tail.core()
     wide.along_ffn([1])
     grad_bn, bn_sums = batch_rows(tokens_grad, visual_maps, bn_stats, proj_full)
-    sums = tables(ds)
-    state, bn_sums, ds, sums, wide.pieces = epoch(tail.held(), bn_sums, ds, sums, wide.pieces)
+    state, bn_sums, ds, wide.pieces = epoch(tail.held(), bn_sums, ds, wide.pieces)
     tail.hold(state)
     tail.prepare()
     tail.blocks, ds = epoch(tail.blocks, ds)

time: 305 us -> 302 us (level)
  waiting for transfers between devices: 47 us -> 56.9 us
  Pallas kernels: 170 us -> 162 us
  starting transfers between devices: 47.9 us -> 43 us
    pallas_call x2 -> x1, Pallas kernels: 25.6 us -> 17.3 us  [table_sums(): pl.pallas_call(functools.partial(table_kernel, first, levels), grid_spec=...]
    ppermute x12, waiting for transfers between devices: 16.6 us -> 22.9 us  [send_ffn(): lax.ppermute(values, 'ffn', [(i, (i + shift) % size) for i in range(size)])]
  transfers between devices with their start and end apart: 54 -> 54, of which waited for: 20 -> 23; matrix products, arithmetic and copies ran while one was open for 6% -> 6% of each run, Pallas kernels for 43% -> 41%
where the time goes in v3:
time: 302 us; the launch traced here: 296 us
  Pallas kernels  162 us (54%)
  waiting for transfers between devices  56.9 us (19%)
  starting transfers between devices  43 us (14%)
  other arithmetic  20.2 us (7%)
  local copies, waits for them, and re-layouts  12.1 us (4%)
    pallas_call x1, Pallas kernels, feed_forward(): pl.pallas_call(functools.partial(feed_kernel, entries, place_bits(parts),...  34.2 us
    ppermute x40, starting transfers between devices, send_dp(): return lax.ppermute(values, 'dp', [(i, i ^ bits) for i in range(size)])  26.4 us
    pallas_call x3, Pallas kernels, bias_words(): pl.pallas_call(functools.partial(bias_kernel, step), grid=(steps,), in_sp...  24.7 us
    ppermute x40, waiting for transfers between devices, send_dp(): return lax.ppermute(values, 'dp', [(i, i ^ bits) for i in range(size)])  24 us
    ppermute x12, waiting for transfers between devices, send_ffn(): lax.ppermute(values, 'ffn', [(i, (i + shift) % size) for i in range(size)])  22.9 us
    pallas_call x2, Pallas kernels, attend_back(): pl.pallas_call(attend_back_kernel, grid=(pairs,), in_specs=[col[0], col[1...  19.4 us
    pallas_call x1, Pallas kernels, table_sums(): pl.pallas_call(functools.partial(table_kernel, first, levels), grid_spec=...  17.3 us
    ppermute x12, starting transfers between devices, send_ffn(): lax.ppermute(values, 'ffn', [(i, (i + shift) % size) for i in range(size)])  16.5 us
  transfers between devices with their start and end apart: 54, of which 23 were waited for; matrix products, arithmetic and copies ran while one was open for 6% of the time, Pallas kernels for 41%

profile of v3, /device:TPU:0, one launch (start us, length us, event | category | flops | bytes accessed | tf_op | source)
XLA Modules:
  0.0 296.2 jit_solution(13988607571929975142)
XLA Ops:
  3.9 3.0 %collective-permute-start = (bf16[152,768]{1,0:T(8,128)(2,1)}, bf16[152,768]{1,0:T(8,128)(2,1)}, u32[]{:S(2)}, u32[]{:S(2)}) collective-permute-start(bf16[152,768]{1,0:T(8,128)(2,1)} %pack_first.1.refs_0_), channel_id=1, source_target_pairs={{0,1},{1,2},{2,3},{3,0},{4,5},{5,6},{6,7},{7,4},{8,9},{9,10},{10,1... | collective-permute-start | bytes 700424 | tf_op jit(solution)/shard_map/ppermute | solution.py:42
  23.0 4.1 %bias_words.3 = (s32[6,64,640]{2,1,0:T(8,128)}, f32[1,1]{1,0:T(1,128)}) custom-call(s32[1,561,561]{2,1,0:T(8,128)} %copy.71.rel_ref, s32[1,561,561]{2,1,0:T(8,128)} %copy.72.x_ref, s32[1,561,561]{2,1,0:T(8,128)} %copy.73.y_ref, f32[12,256]{1,0:T(8,128)} %pad.8.tab_ref), custom_call_target="tpu_custom_call" | custom-call | bytes 6000 | tf_op jit(solution)/shard_map/bias_words/pallas_call | solution.py:939
  32.3 3.6 %collective-permute-start.8 = (bf16[216,768]{1,0:T(8,128)(2,1)S(1)}, bf16[216,768]{1,0:T(8,128)(2,1)S(1)}, u32[]{:S(2)}, u32[]{:S(2)}) collective-permute-start(bf16[216,768]{1,0:T(8,128)(2,1)S(1)} %pad_maximum_fusion.4.refs_0_), channel_id=1, source_target_pairs={{0,1},{1,2},{2,3},{3,0},{4,5},{5,6},{6,7},{7,4},{8,9},{9,10},{10,1... | collective-permute-start | bytes 995336 | tf_op jit(solution)/shard_map/ppermute | solution.py:42
  37.5 14.5 %bias_words.4 = (s32[6,384,640]{2,1,0:T(8,128)}, f32[1,1]{1,0:T(1,128)}) custom-call(s32[1,561,561]{2,1,0:T(8,128)} %copy.71.rel_ref, s32[1,561,561]{2,1,0:T(8,128)} %copy.72.x_ref, s32[1,561,561]{2,1,0:T(8,128)} %copy.73.y_ref, f32[12,256]{1,0:T(8,128)} %pad.8.tab_ref), custom_call_target="tpu_custom_call" | custom-call | bytes 36000 | tf_op jit(solution)/shard_map/bias_words/pallas_call | solution.py:939
  52.0 7.6 %collective-permute-done.9.refs_2_ = bf16[216,768]{1,0:T(8,128)(2,1)S(1)} collective-permute-done((bf16[216,768]{1,0:T(8,128)(2,1)S(1)}, bf16[216,768]{1,0:T(8,128)(2,1)S(1)}, u32[]{:S(2)}, u32[]{:S(2)}) %collective-permute-start.9) | collective-permute-done | bytes 331808 | tf_op jit(solution)/shard_map/ppermute | solution.py:42
  62.8 8.8 %collective-permute-done.14.refs_3_ = bf16[216,768]{1,0:T(8,128)(2,1)S(1)} collective-permute-done((bf16[216,768]{1,0:T(8,128)(2,1)S(1)}, bf16[216,768]{1,0:T(8,128)(2,1)S(1)}, u32[]{:S(2)}, u32[]{:S(2)}) %collective-permute-start.14) | collective-permute-done | bytes 331808 | tf_op jit(solution)/shard_map/ppermute | solution.py:42
  74.1 2.7 order_blocks.3.refs_0_
  79.5 11.4 %first_rows.1 = (bf16[768,2304]{1,0:T(8,128)(2,1)}, bf16[2048,768]{1,0:T(8,128)(2,1)}, f32[576,768]{1,0:T(8,128)}, bf16[768,576]{1,0:T(8,128)(2,1)}, bf16[576,23...) custom-call(s32[5]{0:T(128)} %stack.50.place_ref, bf16[608,768]{1,0:T(8,128)(2,1)} %order_blocks.2.refs_0_, ...), custom_call_target="tpu_custom_call" | custom-call | bytes 25000 | tf_op jit(solution)/shard_map/first_rows/pallas_call | solution.py:407
  90.9 6.1 %bias_words.5 = (s32[6,128,640]{2,1,0:T(8,128)}, f32[1,1]{1,0:T(1,128)}) custom-call(s32[1,561,561]{2,1,0:T(8,128)} %copy.71.rel_ref, s32[1,561,561]{2,1,0:T(8,128)} %copy.72.x_ref, s32[1,561,561]{2,1,0:T(8,128)} %copy.73.y_ref, f32[12,256]{1,0:T(8,128)} %pad.8.tab_ref), custom_call_target="tpu_custom_call" | custom-call | bytes 12000 | tf_op jit(solution)/shard_map/bias_words/pallas_call | solution.py:939
  97.1 4.7 %collective-permute-done.17.refs_2_ = bf16[672,768]{1,0:T(8,128)(2,1)S(1)} collective-permute-done((bf16[672,768]{1,0:T(8,128)(2,1)}, bf16[672,768]{1,0:T(8,128)(2,1)S(1)}, u32[]{:S(2)}, u32[]{:S(2)}) %collective-permute-start.17) | collective-permute-done | bytes 1032224 | tf_op jit(solution)/shard_map/ppermute | solution.py:37
  106.4 14.5 %attend.1 = (bf16[12,576,576]{2,1,0:T(8,128)(2,1)}, bf16[576,768]{1,0:T(8,128)(2,1)}) custom-call(f32[1,1]{1,0:T(1,128)} %get-tuple-element.225.unit_ref, bf16[576,2304]{1,0:T(8,128)(2,1)} %get-tuple-element.334.q_ref.k_ref.v_ref, bf16[576,2304]{1,0:T(8,128)(2,1)} %get-tuple-element.334.q_ref.k_ref.v_ref, ...), custom_call_target="tpu_custom_call" | custom-call | flops 2038431 | bytes 40000 | tf_op jit(solution)/shard_map/attend/pallas_call | solution.py:993
  126.0 34.2 %feed_forward.1 = (f32[576,768]{1,0:T(8,128)}, bf16[768,768]{1,0:T(8,128)(2,1)}, bf16[561,768]{1,0:T(8,128)(2,1)}, f32[576,1]{1,0:T(8,128)}, f32[576,768]{1,0:T(...) custom-call(s32[5]{0:T(128)} %stack.50.place_ref, ...), custom_call_target="tpu_custom_call" | custom-call | bytes 100000 | tf_op jit(solution)/shard_map/feed_forward/pallas_call | solution.py:587
  160.5 2.9 collective-permute-done.31
  167.1 5.4 %norm_rows.1 = (f32[576,768]{1,0:T(8,128)}, bf16[576,768]{1,0:T(8,128)(2,1)}, bf16[576,768]{1,0:T(8,128)(2,1)}, f32[2,768]{1,0:T(2,128)}) custom-call(f32[576,768]{1,0:T(8,128)} %get-tuple-element.316.grad_ref, f32[576,768]{1,0:T(8,128)} %get-tuple-element.317.normed_ref, f32[576,1]{1,0:T(8,128)} %get-tuple-element.318.scale_ref, ...), custom_call_target="tpu_custom_call" | custom-call | bytes 12000 | tf_op jit(solution)/shard_map/norm_rows/pallas_call | solution.py:647
  172.5 7.5 %attend_back.2 = (bf16[4,576,640]{2,1,0:T(8,128)(2,1)}, bf16[576,256]{1,0:T(8,128)(2,1)}, bf16[576,256]{1,0:T(8,128)(2,1)}, bf16[576,256]{1,0:T(8,128)(2,1)}) custom-call(bf16[576,2304]{1,0:T(8,128)(2,1)} %get-tuple-element.334.q_ref.k_ref.v_ref, bf16[576,2304]{1,0:T(8,128)(2,1)} %get-tuple-element.334.q_ref.k_ref.v_ref, ...), custom_call_target="tpu_custom_call" | custom-call | flops 1358954 | bytes 16000 | tf_op jit(solution)/shard_map/attend_back/pallas_call | solution.py:1050
  186.6 11.8 %attend_back.3 = (bf16[8,576,640]{2,1,0:T(8,128)(2,1)}, bf16[576,512]{1,0:T(8,128)(2,1)}, bf16[576,512]{1,0:T(8,128)(2,1)}, bf16[576,512]{1,0:T(8,128)(2,1)}) custom-call(bf16[576,2304]{1,0:T(8,128)(2,1)} %get-tuple-element.334.q_ref.k_ref.v_ref, bf16[576,2304]{1,0:T(8,128)(2,1)} %get-tuple-element.334.q_ref.k_ref.v_ref, ...), custom_call_target="tpu_custom_call" | custom-call | flops 2717908 | bytes 32000 | tf_op jit(solution)/shard_map/attend_back/pallas_call | solution.py:1050
  198.4 14.6 %tail_rows.1 = (bf16[49,768]{1,0:T(8,128)(2,1)}, bf16[4,640,768]{2,1,0:T(8,128)(2,1)}, bf16[4,640,768]{2,1,0:T(8,128)(2,1)}, bf16[640,768]{1,0:T(8,128)(2,1)}) custom-call(s32[5]{0:T(128)} %stack.50.place_ref, bf16[576,256]{1,0:T(8,128)(2,1)} %get-tuple-element.394.refs_0_, bf16[576,512]{1,0:T(8,128)(2,1)} %get-tuple-element.395.refs_1_, ...), custom_call_target="tpu_custom_call" | custom-call | bytes 40000 | tf_op jit(solution)/shard_map/tail_rows/pallas_call | solution.py:733
  219.8 4.0 %batch_rows.1 = (f32[49,2048]{1,0:T(8,128)}, f32[2,2048]{1,0:T(2,128)}) custom-call(bf16[49,768]{1,0:T(8,128)(2,1)} %get-tuple-element.360.tokens_ref, bf16[49,2048]{1,0:T(8,128)(2,1)} %refs_3_.1, f32[2,2048]{1,0:T(2,128)} %get-tuple-element.361.stats_ref.refs_4_, bf16[2048,768]{1,0:T(8,128)(2,1)} %get-tuple-element.362.proj_ref), custom_call_target="tpu_custom_call" | custom-call | bytes 6000 | tf_op jit(solution)/shard_map/batch_rows/pallas_call | solution.py:764
  223.8 6.5 %collective-permute-done.41 = bf16[2,96,768]{2,1,0:T(8,128)(2,1)S(1)} collective-permute-done((bf16[2,96,768]{2,1,0:T(8,128)(2,1)S(1)}, bf16[2,96,768]{2,1,0:T(8,128)(2,1)S(1)}, u32[]{:S(2)}, u32[]{:S(2)}) %collective-permute-start.41) | collective-permute-done | bytes 294944 | tf_op jit(solution)/shard_map/ppermute | solution.py:42
  239.7 17.3 %table_sums.1.refs_0_ = f32[96,80]{1,0:T(8,128)} custom-call(s32[12]{0:T(128)} %get-tuple-element.375.block_ref, s32[12]{0:T(128)} %get-tuple-element.376.count_ref, s32[1,561,561]{2,1,0:T(8,128)} %copy.71.rel_ref, s32[1,561,561]{2,1,0:T(8,128)} %copy.72.x_ref, s32[1,561,561]{2,1,0:T(8,128)} %copy.73.y_ref, bf16[4,576,640]{2,1,0:T(8,128)(2,1)} %get-tuple-element.377.refs_0_, ...), custom_call_target="tpu_custom_call" | custom-call | bytes 48000 | tf_op jit(solution)/shard_map/table_sums/pallas_call | solution.py:1131
  267.5 4.7 %collective-permute-done.47 = f32[24,768]{1,0:T(8,128)S(1)} collective-permute-done((f32[24,768]{1,0:T(8,128)}, f32[24,768]{1,0:T(8,128)S(1)}, u32[]{:S(2)}, u32[]{:S(2)}) %collective-permute-start.47) | collective-permute-done | bytes 73760 | tf_op jit(solution)/shard_map/ppermute | solution.py:47
  272.3 5.2 %collective-permute-done.48 = f32[24,768]{1,0:T(8,128)S(1)} collective-permute-done((f32[24,768]{1,0:T(8,128)S(1)}, f32[24,768]{1,0:T(8,128)S(1)}, u32[]{:S(2)}, u32[]{:S(2)}) %collective-permute-start.48) | collective-permute-done | bytes 73760 | tf_op jit(solution)/shard_map/ppermute | solution.py:47
  280.3 3.2 %collective-permute-done.50 = f32[24,768]{1,0:T(8,128)S(1)} collective-permute-done((f32[24,768]{1,0:T(8,128)S(1)}, f32[24,768]{1,0:T(8,128)S(1)}, u32[]{:S(2)}, u32[]{:S(2)}) %collective-permute-start.50) | collective-permute-done | bytes 73760 | tf_op jit(solution)/shard_map/ppermute | solution.py:37
  285.8 5.8 %text_rows.1 = f32[512,768]{1,0:T(8,128)} custom-call(bf16[576,256]{1,0:T(8,128)(2,1)} %get-tuple-element.394.refs_0_, bf16[576,512]{1,0:T(8,128)(2,1)} %get-tuple-element.395.refs_1_, bf16[576,256]{1,0:T(8,128)(2,1)} %get-tuple-element.396.refs_2_, bf16[576,512]{1,0:T(8,128)(2,1)} %get-tuple-element.397.refs_3_, ...), custom_call_target="tpu_custom_call" | custom-call | bytes 25000 | tf_op jit(solution)/shard_map/text_rows/pallas_call | solution.py:791
  (268 shorter events, 90.1 us)
Async XLA Ops:
  3.9 25.0 %collective-permute-start = (bf16[152,768]{1,0:T(8,128)(2,1)}, bf16[152,768]{1,0:T(8,128)(2,1)}, u32[]{:S(2)}, u32[]{:S(2)}) collective-permute-start(bf16[152,768]{1,0:T(8,128)(2,1)} %pack_first.1.refs_0_), channel_id=1, source_target_pairs={{0,1},{1,2},{2,3},{3,0},{4,5},{5,6},{6,7},{7,4},{8,9},{9,10},{10,1... | collective-permute-start | bytes 700424 | tf_op jit(solution)/shard_map/ppermute | solution.py:42
  6.9 22.0 %collective-permute-start.1 = (bf16[152,768]{1,0:T(8,128)(2,1)}, bf16[152,768]{1,0:T(8,128)(2,1)}, u32[]{:S(2)}, u32[]{:S(2)}) collective-permute-start(bf16[152,768]{1,0:T(8,128)(2,1)} %pack_first.1.refs_0_), channel_id=1, source_target_pairs={{0,2},{1,3},{2,0},{3,1},{4,6},{5,7},{6,4},{7,5},{8,10},{9,11},{10,... | collective-permute-start | bytes 700424 | tf_op jit(solution)/shard_map/ppermute | solution.py:42
  9.5 19.4 %collective-permute-start.2 = (bf16[152,768]{1,0:T(8,128)(2,1)}, bf16[152,768]{1,0:T(8,128)(2,1)}, u32[]{:S(2)}, u32[]{:S(2)}) collective-permute-start(bf16[152,768]{1,0:T(8,128)(2,1)} %pack_first.1.refs_0_), channel_id=1, source_target_pairs={{0,3},{1,0},{2,1},{3,2},{4,7},{5,4},{6,5},{7,6},{8,11},{9,8},{10,9... | collective-permute-start | bytes 700424 | tf_op jit(solution)/shard_map/ppermute | solution.py:42
  10.8 18.1 %collective-permute-start.3 = (bf16[192,768]{1,0:T(8,128)(2,1)S(1)}, bf16[192,768]{1,0:T(8,128)(2,1)}, u32[]{:S(2)}, u32[]{:S(2)}) collective-permute-start(bf16[192,768]{1,0:T(8,128)(2,1)S(1)} %pad_maximum_fusion.5.refs_10_), channel_id=1, source_target_pairs={{0,8},{4,12},{8,0},{12,4},{16,24},{20,28},{24,16},{28,20},{1,9},{5... | collective-permute-start | bytes 884744 | tf_op jit(solution)/shard_map/ppermute | solution.py:37
  31.3 28.3 %collective-permute-start.5 = (bf16[608,768]{1,0:T(8,128)(2,1)}, bf16[608,768]{1,0:T(8,128)(2,1)S(1)}, u32[]{:S(2)}, u32[]{:S(2)}) collective-permute-start(bf16[608,768]{1,0:T(8,128)(2,1)} %order_blocks.2.refs_0_), channel_id=1, source_target_pairs={{0,8},{4,12},{8,0},{12,4},{16,24},{20,28},{24,16},{28,20},{1,9},{5... | collective-permute-start | bytes 2801672 | tf_op jit(solution)/shard_map/ppermute | solution.py:37
  31.8 27.8 %collective-permute-start.6 = (bf16[608,768]{1,0:T(8,128)(2,1)}, bf16[608,768]{1,0:T(8,128)(2,1)S(1)}, u32[]{:S(2)}, u32[]{:S(2)}) collective-permute-start(bf16[608,768]{1,0:T(8,128)(2,1)} %order_blocks.2.refs_0_), channel_id=1, source_target_pairs={{0,16},{4,20},{8,24},{12,28},{16,0},{20,4},{24,8},{28,12},{1,17},{... | collective-permute-start | bytes 2801672 | tf_op jit(solution)/shard_map/ppermute | solution.py:37
  32.3 27.3 %collective-permute-start.7 = (bf16[608,768]{1,0:T(8,128)(2,1)}, bf16[608,768]{1,0:T(8,128)(2,1)S(1)}, u32[]{:S(2)}, u32[]{:S(2)}) collective-permute-start(bf16[608,768]{1,0:T(8,128)(2,1)} %order_blocks.2.refs_0_), channel_id=1, source_target_pairs={{0,4},{4,0},{8,12},{12,8},{16,20},{20,16},{24,28},{28,24},{1,5},{5... | collective-permute-start | bytes 2801672 | tf_op jit(solution)/shard_map/ppermute | solution.py:37
  32.3 19.6 %collective-permute-start.8 = (bf16[216,768]{1,0:T(8,128)(2,1)S(1)}, bf16[216,768]{1,0:T(8,128)(2,1)S(1)}, u32[]{:S(2)}, u32[]{:S(2)}) collective-permute-start(bf16[216,768]{1,0:T(8,128)(2,1)S(1)} %pad_maximum_fusion.4.refs_0_), channel_id=1, source_target_pairs={{0,1},{1,2},{2,3},{3,0},{4,5},{5,6},{6,7},{7,4},{8,9},{9,10},{10,1... | collective-permute-start | bytes 995336 | tf_op jit(solution)/shard_map/ppermute | solution.py:42
  35.9 23.7 %collective-permute-start.9 = (bf16[216,768]{1,0:T(8,128)(2,1)S(1)}, bf16[216,768]{1,0:T(8,128)(2,1)S(1)}, u32[]{:S(2)}, u32[]{:S(2)}) collective-permute-start(bf16[216,768]{1,0:T(8,128)(2,1)S(1)} %pad_maximum_fusion.4.refs_0_), channel_id=1, source_target_pairs={{0,2},{1,3},{2,0},{3,1},{4,6},{5,7},{6,4},{7,5},{8,10},{9,11},{10,... | collective-permute-start | bytes 995336 | tf_op jit(solution)/shard_map/ppermute | solution.py:42
  76.9 24.9 %collective-permute-start.17 = (bf16[672,768]{1,0:T(8,128)(2,1)}, bf16[672,768]{1,0:T(8,128)(2,1)S(1)}, u32[]{:S(2)}, u32[]{:S(2)}) collective-permute-start(bf16[672,768]{1,0:T(8,128)(2,1)} %order_blocks.3.refs_0_), channel_id=1, source_target_pairs={{0,8},{4,12},{8,0},{12,4},{16,24},{20,28},{24,16},{28,20},{1,9},{5... | collective-permute-start | bytes 3096584 | tf_op jit(solution)/shard_map/ppermute | solution.py:37
  77.9 24.4 %collective-permute-start.18 = (bf16[672,768]{1,0:T(8,128)(2,1)}, bf16[672,768]{1,0:T(8,128)(2,1)S(1)}, u32[]{:S(2)}, u32[]{:S(2)}) collective-permute-start(bf16[672,768]{1,0:T(8,128)(2,1)} %order_blocks.3.refs_0_), channel_id=1, source_target_pairs={{0,16},{4,20},{8,24},{12,28},{16,0},{20,4},{24,8},{28,12},{1,17},{... | collective-permute-start | bytes 3096584 | tf_op jit(solution)/shard_map/ppermute | solution.py:37
  79.0 23.4 %collective-permute-start.19 = (bf16[672,768]{1,0:T(8,128)(2,1)}, bf16[672,768]{1,0:T(8,128)(2,1)S(1)}, u32[]{:S(2)}, u32[]{:S(2)}) collective-permute-start(bf16[672,768]{1,0:T(8,128)(2,1)} %order_blocks.3.refs_0_), channel_id=1, source_target_pairs={{0,4},{4,0},{8,12},{12,8},{16,20},{20,16},{24,28},{28,24},{1,5},{5... | collective-permute-start | bytes 3096584 | tf_op jit(solution)/shard_map/ppermute | solution.py:37
  79.0 18.1 %collective-permute-start.20 = (bf16[192,768]{1,0:T(8,128)(2,1)S(1)}, bf16[192,768]{1,0:T(8,128)(2,1)S(1)}, u32[]{:S(2)}, u32[]{:S(2)}) collective-permute-start(bf16[192,768]{1,0:T(8,128)(2,1)S(1)} %pad_maximum_fusion.5.refs_10_), channel_id=1, source_target_pairs={{0,4},{4,0},{8,12},{12,8},{16,20},{20,16},{24,28},{28,24},{1,5},{5... | collective-permute-start | bytes 884744 | tf_op jit(solution)/shard_map/ppermute | solution.py:37
  79.5 17.6 %collective-permute-start.21 = (bf16[192,768]{1,0:T(8,128)(2,1)}, bf16[192,768]{1,0:T(8,128)(2,1)S(1)}, u32[]{:S(2)}, u32[]{:S(2)}) collective-permute-start(bf16[192,768]{1,0:T(8,128)(2,1)} %collective-permute-done.3.refs_12_), channel_id=1, source_target_pairs={{0,4},{4,0},{8,12},{12,8},{16,20},{20,16},{24,28},{28,24},{1,5},{5... | collective-permute-start | bytes 884744 | tf_op jit(solution)/shard_map/ppermute | solution.py:37
  102.3 19.2 %collective-permute-start.24 = (bf16[672,768]{1,0:T(8,128)(2,1)S(1)}, bf16[672,768]{1,0:T(8,128)(2,1)S(1)}, u32[]{:S(2)}, u32[]{:S(2)}) collective-permute-start(bf16[672,768]{1,0:T(8,128)(2,1)S(1)} %collective-permute-done.17.refs_2_), channel_id=1, source_target_pairs={{0,4},{4,0},{8,12},{12,8},{16,20},{20,16},{24,28},{28,24},{1,5},{5... | collective-permute-start | bytes 3096584 | tf_op jit(solution)/shard_map/ppermute | solution.py:37
  102.4 19.1 %collective-permute-start.25 = (bf16[672,768]{1,0:T(8,128)(2,1)S(1)}, bf16[672,768]{1,0:T(8,128)(2,1)S(1)}, u32[]{:S(2)}, u32[]{:S(2)}) collective-permute-start(bf16[672,768]{1,0:T(8,128)(2,1)S(1)} %collective-permute-done.18.refs_4_), channel_id=1, source_target_pairs={{0,4},{4,0},{8,12},{12,8},{16,20},{20,16},{24,28},{28,24},{1,5},{5... | collective-permute-start | bytes 3096584 | tf_op jit(solution)/shard_map/ppermute | solution.py:37
  103.0 18.5 %collective-permute-start.23 = (bf16[480,768]{1,0:T(8,128)(2,1)S(1)}, bf16[480,768]{1,0:T(8,128)(2,1)S(1)}, u32[]{:S(2)}, u32[]{:S(2)}) collective-permute-start(bf16[480,768]{1,0:T(8,128)(2,1)S(1)} %slice.179), channel_id=1, source_target_pairs={{0,8},{4,12},{8,0},{12,4},{16,24},{20,28},{24,16},{28,20},{1,9},{5... | collective-permute-start | bytes 2211848 | tf_op jit(solution)/shard_map/ppermute | solution.py:37
  163.4 18.3 %collective-permute-start.32 = (bf16[4,2,4,96,768]{4,3,2,1,0:T(8,128)(2,1)}, bf16[4,2,4,96,768]{4,3,2,1,0:T(8,128)(2,1)}, u32[]{:S(2)}, u32[]{:S(2)}) collective-permute-start(bf16[4,2,4,96,768]{4,3,2,1,0:T(8,128)(2,1)} %get-tuple-element.313), channel_id=1, source_target_pairs={{0,4},{4,0},{8,12},{12,8},{16,20},{20,16},{24,28},{28,24},{1,5},{5... | collective-permute-start | bytes 14155784 | tf_op jit(solution)/shard_map/ppermute | solution.py:37
  184.5 28.5 %collective-permute-start.35 = (bf16[2,4,96,768]{3,2,1,0:T(8,128)(2,1)S(1)}, bf16[2,4,96,768]{3,2,1,0:T(8,128)(2,1)S(1)}, u32[]{:S(2)}, u32[]{:S(2)}) collective-permute-start(bf16[2,4,96,768]{3,2,1,0:T(8,128)(2,1)S(1)} %pad_maximum_fusion), channel_id=1, source_target_pairs={{0,8},{4,12},{8,0},{12,4},{16,24},{20,28},{24,16},{28,20},{1,9},{5... | collective-permute-start | bytes 3538952 | tf_op jit(solution)/shard_map/ppermute | solution.py:37
  185.4 27.6 %collective-permute-start.36 = (bf16[2,4,96,768]{3,2,1,0:T(8,128)(2,1)S(1)}, bf16[2,4,96,768]{3,2,1,0:T(8,128)(2,1)}, u32[]{:S(2)}, u32[]{:S(2)}) collective-permute-start(bf16[2,4,96,768]{3,2,1,0:T(8,128)(2,1)S(1)} %pad_maximum_fusion.1), channel_id=1, source_target_pairs={{0,16},{4,20},{8,24},{12,28},{16,0},{20,4},{24,8},{28,12},{1,17},{... | collective-permute-start | bytes 3538952 | tf_op jit(solution)/shard_map/ppermute | solution.py:37
  236.1 23.1 %collective-permute-start.42 = (bf16[640,768]{1,0:T(8,128)(2,1)}, bf16[640,768]{1,0:T(8,128)(2,1)S(1)}, u32[]{:S(2)}, u32[]{:S(2)}) collective-permute-start(bf16[640,768]{1,0:T(8,128)(2,1)} %pad_maximum_fusion.2), channel_id=1, source_target_pairs={{0,8},{4,12},{8,0},{12,4},{16,24},{20,28},{24,16},{28,20},{1,9},{5... | collective-permute-start | bytes 2949128 | tf_op jit(solution)/shard_map/ppermute | solution.py:37
  237.3 22.7 %collective-permute-start.43 = (bf16[640,768]{1,0:T(8,128)(2,1)S(1)}, bf16[640,768]{1,0:T(8,128)(2,1)}, u32[]{:S(2)}, u32[]{:S(2)}) collective-permute-start(bf16[640,768]{1,0:T(8,128)(2,1)S(1)} %pad_maximum_fusion.3), channel_id=1, source_target_pairs={{0,16},{4,20},{8,24},{12,28},{16,0},{20,4},{24,8},{28,12},{1,17},{... | collective-permute-start | bytes 2949128 | tf_op jit(solution)/shard_map/ppermute | solution.py:37
  238.2 18.9 %collective-permute-start.44 = (bf16[2,96,768]{2,1,0:T(8,128)(2,1)S(1)}, bf16[2,96,768]{2,1,0:T(8,128)(2,1)S(1)}, u32[]{:S(2)}, u32[]{:S(2)}) collective-permute-start(bf16[2,96,768]{2,1,0:T(8,128)(2,1)S(1)} %get-tuple-element.434), channel_id=1, source_target_pairs={{0,2},{1,3},{2,0},{3,1},{4,6},{5,7},{6,4},{7,5},{8,10},{9,11},{10,... | collective-permute-start | bytes 884744 | tf_op jit(solution)/shard_map/ppermute | solution.py:42
  238.2 18.9 %collective-permute-start.45 = (bf16[2,96,768]{2,1,0:T(8,128)(2,1)S(1)}, bf16[2,96,768]{2,1,0:T(8,128)(2,1)}, u32[]{:S(2)}, u32[]{:S(2)}) collective-permute-start(bf16[2,96,768]{2,1,0:T(8,128)(2,1)S(1)} %get-tuple-element.433), channel_id=1, source_target_pairs={{0,3},{1,0},{2,1},{3,2},{4,7},{5,4},{6,5},{7,6},{8,11},{9,8},{10,9... | collective-permute-start | bytes 884744 | tf_op jit(solution)/shard_map/ppermute | solution.py:42
  (80 other events, 795.2 us)

commit v4 on v3

--- a/solution.py
+++ b/solution.py
@@ -231,24 +231,16 @@
     mean = jnp.sum(visual, 0, keepdims=True) * (1.0 / count)
     gap = visual - mean
     spread = jnp.sum(gap * gap, 0, keepdims=True)
-    channels = visual_ref.shape[1]
-    chunks = pl.cdiv(channels, width)
-    blank = jnp.zeros((1, chunks * width - channels), F32)
-    pieces = []
-    for values, times in ((mean, 3), (spread, 2)):
-        if chunks * width > channels:
-            values = jnp.concatenate([values, blank], 1)
-        for _ in range(times):
-            piece = values.astype(BF16).astype(F32)
-            values = values - piece
-            pieces += [piece[:, n * width : (n + 1) * width] for n in range(chunks)]
-    pieces += [jnp.zeros((1, width), F32)] * (out_ref.shape[0] - row - len(pieces))
-    out_ref[row:, :] = jnp.concatenate(pieces, 0).astype(BF16)
+    high = mean.astype(BF16)
+    rest = (mean - high.astype(F32)).astype(BF16)
+    flat = jnp.concatenate([high.astype(F32), rest.astype(F32), spread], 1)
+    rows = [flat[:, n * width : (n + 1) * width] for n in range(out_ref.shape[0] - row)]
+    out_ref[row:, :] = jnp.concatenate(rows, 0).astype(BF16)
 
 
 def pack_first(w_query, w_key, w_value, vis_proj, visual):
     width = w_query.shape[1]
-    moments = pl.cdiv(5 * pl.cdiv(visual.shape[1], width), 16) * 16
+    moments = 3 * visual.shape[1] // width
     rows = [w.shape[0] for w in (w_query, w_key, w_value, vis_proj)] + [moments]
     own = pl.pallas_call(
         pack_kernel,
@@ -349,21 +341,15 @@
     for out, copy in copies:
         if out == 2:
             copy.wait()
-    chunks = pl.cdiv(channels, width)
     moments = moments_ref[...].astype(F32).reshape(devices, -1, width)
-    means = sum(moments[:, n * chunks : (n + 1) * chunks] for n in range(3))
-    spreads = sum(moments[:, n * chunks : (n + 1) * chunks] for n in range(3, 5))
-    average = jnp.sum(means, 0) * (1.0 / devices)
-    gap = means - average[None]
+    moments = jnp.concatenate([moments[:, n] for n in range(moments.shape[1])], 1)
+    means = moments[:, :channels] + moments[:, channels : 2 * channels]
+    spreads = moments[:, 2 * channels :]
+    average = jnp.sum(means, 0, keepdims=True) * (1.0 / devices)
+    gap = means - average
     rows = visual_len * devices
-    spread = (jnp.sum(spreads, 0) + visual_len * jnp.sum(gap * gap, 0)) * (1.0 / rows)
-    inverse = lax.rsqrt(spread + EPS)
-
-    def flat(values):
-        pieces = [values[n : n + 1, :] for n in range(chunks)]
-        return jnp.concatenate(pieces, 1)[:, :channels]
-
-    average, inverse = flat(average), flat(inverse)
+    spread = jnp.sum(spreads, 0, keepdims=True) + visual_len * jnp.sum(gap * gap, 0, keepdims=True)
+    inverse = lax.rsqrt(spread * (1.0 / rows) + EPS)
     stats_ref[0:1, :] = average
     stats_ref[1:2, :] = inverse
     normed = (visual_ref[...].astype(F32) - average) * inverse
@@ -1450,7 +1436,6 @@
     while len(total.steps) > 1:
         total.step()
     text_grad = text_rows(back, qkv_full, grad_attn, text_len)
-    tail_sum = tail.total()
     other = total.steps[0](total.values)
     (
         shift_grad,
@@ -1478,7 +1463,7 @@
     )
     shards, row = [], 0
     for size in [w_query.shape[0]] * 4 + [vis_proj.shape[0]]:
-        shards.append(tail_sum[row : row + size])
+        shards.append(sum(piece[row : row + size].astype(F32) for piece in tail.pieces))
         row += size
     return (
         output,

time: 302 us -> 300 us (level)
    unnamed x103 -> x115, local copies, waits for them, and re-layouts: 6.01 us -> 6.08 us
where the time goes in v4:
time: 300 us; the launch traced here: 295 us
  Pallas kernels  162 us (54%)
  waiting for transfers between devices  57.2 us (19%)
  starting transfers between devices  42.3 us (14%)
  other arithmetic  20.4 us (7%)
  local copies, waits for them, and re-layouts  11.5 us (4%)
    pallas_call x1, Pallas kernels, feed_forward(): pl.pallas_call(functools.partial(feed_kernel, entries, place_bits(parts),...  34.2 us
    ppermute x40, starting transfers between devices, send_dp(): return lax.ppermute(values, 'dp', [(i, i ^ bits) for i in range(size)])  26.3 us
    ppermute x40, waiting for transfers between devices, send_dp(): return lax.ppermute(values, 'dp', [(i, i ^ bits) for i in range(size)])  24.8 us
    pallas_call x3, Pallas kernels, bias_words(): pl.pallas_call(functools.partial(bias_kernel, step), grid=(steps,), in_sp...  24.7 us
    ppermute x12, waiting for transfers between devices, send_ffn(): lax.ppermute(values, 'ffn', [(i, (i + shift) % size) for i in range(size)])  23 us
    pallas_call x2, Pallas kernels, attend_back(): pl.pallas_call(attend_back_kernel, grid=(pairs,), in_specs=[col[0], col[1...  19.4 us
    pallas_call x1, Pallas kernels, table_sums(): pl.pallas_call(functools.partial(table_kernel, first, levels), grid_spec=...  17 us
    ppermute x12, starting transfers between devices, send_ffn(): lax.ppermute(values, 'ffn', [(i, (i + shift) % size) for i in range(size)])  16 us
  transfers between devices with their start and end apart: 54, of which 23 were waited for; matrix products, arithmetic and copies ran while one was open for 6% of the time, Pallas kernels for 41%

profile of v4, /device:TPU:0, one launch (start us, length us, event | category | flops | bytes accessed | tf_op | source)
XLA Modules:
  0.0 294.7 jit_solution(13265164794777180018)
XLA Ops:
  3.8 3.0 %collective-permute-start = (bf16[144,768]{1,0:T(8,128)(2,1)}, bf16[144,768]{1,0:T(8,128)(2,1)}, u32[]{:S(2)}, u32[]{:S(2)}) collective-permute-start(bf16[144,768]{1,0:T(8,128)(2,1)} %pack_first.1.refs_0_), channel_id=1, source_target_pairs={{0,1},{1,2},{2,3},{3,0},{4,5},{5,6},{6,7},{7,4},{8,9},{9,10},{10,1... | collective-permute-start | bytes 663560 | tf_op jit(solution)/shard_map/ppermute | solution.py:42
  21.8 4.1 %bias_words.3 = (s32[6,64,640]{2,1,0:T(8,128)}, f32[1,1]{1,0:T(1,128)}) custom-call(s32[1,561,561]{2,1,0:T(8,128)} %copy.71.rel_ref, s32[1,561,561]{2,1,0:T(8,128)} %copy.72.x_ref, s32[1,561,561]{2,1,0:T(8,128)} %copy.73.y_ref, f32[12,256]{1,0:T(8,128)} %pad.8.tab_ref), custom_call_target="tpu_custom_call" | custom-call | bytes 6000 | tf_op jit(solution)/shard_map/bias_words/pallas_call | solution.py:925
  31.3 3.6 %collective-permute-start.8 = (bf16[216,768]{1,0:T(8,128)(2,1)S(1)}, bf16[216,768]{1,0:T(8,128)(2,1)S(1)}, u32[]{:S(2)}, u32[]{:S(2)}) collective-permute-start(bf16[216,768]{1,0:T(8,128)(2,1)S(1)} %pad_maximum_fusion.4.refs_0_), channel_id=1, source_target_pairs={{0,1},{1,2},{2,3},{3,0},{4,5},{5,6},{6,7},{7,4},{8,9},{9,10},{10,1... | collective-permute-start | bytes 995336 | tf_op jit(solution)/shard_map/ppermute | solution.py:42
  36.5 14.5 %bias_words.4 = (s32[6,384,640]{2,1,0:T(8,128)}, f32[1,1]{1,0:T(1,128)}) custom-call(s32[1,561,561]{2,1,0:T(8,128)} %copy.71.rel_ref, s32[1,561,561]{2,1,0:T(8,128)} %copy.72.x_ref, s32[1,561,561]{2,1,0:T(8,128)} %copy.73.y_ref, f32[12,256]{1,0:T(8,128)} %pad.8.tab_ref), custom_call_target="tpu_custom_call" | custom-call | bytes 36000 | tf_op jit(solution)/shard_map/bias_words/pallas_call | solution.py:925
  50.9 7.6 %collective-permute-done.9.refs_2_ = bf16[216,768]{1,0:T(8,128)(2,1)S(1)} collective-permute-done((bf16[216,768]{1,0:T(8,128)(2,1)S(1)}, bf16[216,768]{1,0:T(8,128)(2,1)S(1)}, u32[]{:S(2)}, u32[]{:S(2)}) %collective-permute-start.9) | collective-permute-done | bytes 331808 | tf_op jit(solution)/shard_map/ppermute | solution.py:42
  61.7 8.8 %collective-permute-done.14.refs_3_ = bf16[216,768]{1,0:T(8,128)(2,1)S(1)} collective-permute-done((bf16[216,768]{1,0:T(8,128)(2,1)S(1)}, bf16[216,768]{1,0:T(8,128)(2,1)S(1)}, u32[]{:S(2)}, u32[]{:S(2)}) %collective-permute-start.14) | collective-permute-done | bytes 331808 | tf_op jit(solution)/shard_map/ppermute | solution.py:42
  77.8 11.0 %first_rows.1 = (bf16[768,2304]{1,0:T(8,128)(2,1)}, bf16[2048,768]{1,0:T(8,128)(2,1)}, f32[576,768]{1,0:T(8,128)}, bf16[768,576]{1,0:T(8,128)(2,1)}, bf16[576,23...) custom-call(s32[5]{0:T(128)} %stack.50.place_ref, bf16[576,768]{1,0:T(8,128)(2,1)} %order_blocks.2.refs_0_, ...), custom_call_target="tpu_custom_call" | custom-call | bytes 25000 | tf_op jit(solution)/shard_map/first_rows/pallas_call | solution.py:393
  88.8 6.2 %bias_words.5 = (s32[6,128,640]{2,1,0:T(8,128)}, f32[1,1]{1,0:T(1,128)}) custom-call(s32[1,561,561]{2,1,0:T(8,128)} %copy.71.rel_ref, s32[1,561,561]{2,1,0:T(8,128)} %copy.72.x_ref, s32[1,561,561]{2,1,0:T(8,128)} %copy.73.y_ref, f32[12,256]{1,0:T(8,128)} %pad.8.tab_ref), custom_call_target="tpu_custom_call" | custom-call | bytes 12000 | tf_op jit(solution)/shard_map/bias_words/pallas_call | solution.py:925
  95.0 5.0 %collective-permute-done.17.refs_2_ = bf16[672,768]{1,0:T(8,128)(2,1)S(1)} collective-permute-done((bf16[672,768]{1,0:T(8,128)(2,1)}, bf16[672,768]{1,0:T(8,128)(2,1)S(1)}, u32[]{:S(2)}, u32[]{:S(2)}) %collective-permute-start.17) | collective-permute-done | bytes 1032224 | tf_op jit(solution)/shard_map/ppermute | solution.py:37
  105.2 14.5 %attend.1 = (bf16[12,576,576]{2,1,0:T(8,128)(2,1)}, bf16[576,768]{1,0:T(8,128)(2,1)}) custom-call(f32[1,1]{1,0:T(1,128)} %get-tuple-element.225.unit_ref, bf16[576,2304]{1,0:T(8,128)(2,1)} %get-tuple-element.334.q_ref.k_ref.v_ref, bf16[576,2304]{1,0:T(8,128)(2,1)} %get-tuple-element.334.q_ref.k_ref.v_ref, ...), custom_call_target="tpu_custom_call" | custom-call | flops 2038431 | bytes 40000 | tf_op jit(solution)/shard_map/attend/pallas_call | solution.py:979
  124.9 34.2 %feed_forward.1 = (f32[576,768]{1,0:T(8,128)}, bf16[768,768]{1,0:T(8,128)(2,1)}, bf16[561,768]{1,0:T(8,128)(2,1)}, f32[576,1]{1,0:T(8,128)}, f32[576,768]{1,0:T(...) custom-call(s32[5]{0:T(128)} %stack.50.place_ref, ...), custom_call_target="tpu_custom_call" | custom-call | bytes 100000 | tf_op jit(solution)/shard_map/feed_forward/pallas_call | solution.py:573
  159.3 2.9 collective-permute-done.31
  166.1 5.4 %norm_rows.1 = (f32[576,768]{1,0:T(8,128)}, bf16[576,768]{1,0:T(8,128)(2,1)}, bf16[576,768]{1,0:T(8,128)(2,1)}, f32[2,768]{1,0:T(2,128)}) custom-call(f32[576,768]{1,0:T(8,128)} %get-tuple-element.316.grad_ref, f32[576,768]{1,0:T(8,128)} %get-tuple-element.317.normed_ref, f32[576,1]{1,0:T(8,128)} %get-tuple-element.318.scale_ref, ...), custom_call_target="tpu_custom_call" | custom-call | bytes 12000 | tf_op jit(solution)/shard_map/norm_rows/pallas_call | solution.py:633
  171.5 7.5 %attend_back.2 = (bf16[4,576,640]{2,1,0:T(8,128)(2,1)}, bf16[576,256]{1,0:T(8,128)(2,1)}, bf16[576,256]{1,0:T(8,128)(2,1)}, bf16[576,256]{1,0:T(8,128)(2,1)}) custom-call(bf16[576,2304]{1,0:T(8,128)(2,1)} %get-tuple-element.334.q_ref.k_ref.v_ref, bf16[576,2304]{1,0:T(8,128)(2,1)} %get-tuple-element.334.q_ref.k_ref.v_ref, ...), custom_call_target="tpu_custom_call" | custom-call | flops 1358954 | bytes 16000 | tf_op jit(solution)/shard_map/attend_back/pallas_call | solution.py:1036
  185.3 11.8 %attend_back.3 = (bf16[8,576,640]{2,1,0:T(8,128)(2,1)}, bf16[576,512]{1,0:T(8,128)(2,1)}, bf16[576,512]{1,0:T(8,128)(2,1)}, bf16[576,512]{1,0:T(8,128)(2,1)}) custom-call(bf16[576,2304]{1,0:T(8,128)(2,1)} %get-tuple-element.334.q_ref.k_ref.v_ref, bf16[576,2304]{1,0:T(8,128)(2,1)} %get-tuple-element.334.q_ref.k_ref.v_ref, ...), custom_call_target="tpu_custom_call" | custom-call | flops 2717908 | bytes 32000 | tf_op jit(solution)/shard_map/attend_back/pallas_call | solution.py:1036
  197.2 14.6 %tail_rows.1 = (bf16[49,768]{1,0:T(8,128)(2,1)}, bf16[4,640,768]{2,1,0:T(8,128)(2,1)}, bf16[4,640,768]{2,1,0:T(8,128)(2,1)}, bf16[640,768]{1,0:T(8,128)(2,1)}) custom-call(s32[5]{0:T(128)} %stack.50.place_ref, bf16[576,256]{1,0:T(8,128)(2,1)} %get-tuple-element.394.refs_0_, bf16[576,512]{1,0:T(8,128)(2,1)} %get-tuple-element.395.refs_1_, ...), custom_call_target="tpu_custom_call" | custom-call | bytes 40000 | tf_op jit(solution)/shard_map/tail_rows/pallas_call | solution.py:719
  218.4 4.0 %batch_rows.1 = (f32[49,2048]{1,0:T(8,128)}, f32[2,2048]{1,0:T(2,128)}) custom-call(bf16[49,768]{1,0:T(8,128)(2,1)} %get-tuple-element.360.tokens_ref, bf16[49,2048]{1,0:T(8,128)(2,1)} %refs_3_.1, f32[2,2048]{1,0:T(2,128)} %get-tuple-element.361.stats_ref.refs_4_, bf16[2048,768]{1,0:T(8,128)(2,1)} %get-tuple-element.362.proj_ref), custom_call_target="tpu_custom_call" | custom-call | bytes 6000 | tf_op jit(solution)/shard_map/batch_rows/pallas_call | solution.py:750
  222.4 6.5 %collective-permute-done.41 = bf16[2,96,768]{2,1,0:T(8,128)(2,1)S(1)} collective-permute-done((bf16[2,96,768]{2,1,0:T(8,128)(2,1)S(1)}, bf16[2,96,768]{2,1,0:T(8,128)(2,1)S(1)}, u32[]{:S(2)}, u32[]{:S(2)}) %collective-permute-start.41) | collective-permute-done | bytes 294944 | tf_op jit(solution)/shard_map/ppermute | solution.py:42
  238.2 17.0 %table_sums.1.refs_0_ = f32[96,80]{1,0:T(8,128)} custom-call(s32[12]{0:T(128)} %get-tuple-element.375.block_ref, s32[12]{0:T(128)} %get-tuple-element.376.count_ref, s32[1,561,561]{2,1,0:T(8,128)} %copy.71.rel_ref, s32[1,561,561]{2,1,0:T(8,128)} %copy.72.x_ref, s32[1,561,561]{2,1,0:T(8,128)} %copy.73.y_ref, bf16[4,576,640]{2,1,0:T(8,128)(2,1)} %get-tuple-element.377.refs_0_, ...), custom_call_target="tpu_custom_call" | custom-call | bytes 48000 | tf_op jit(solution)/shard_map/table_sums/pallas_call | solution.py:1117
  255.2 3.0 %collective-permute-done.42 = bf16[640,768]{1,0:T(8,128)(2,1)S(1)} collective-permute-done((bf16[640,768]{1,0:T(8,128)(2,1)}, bf16[640,768]{1,0:T(8,128)(2,1)S(1)}, u32[]{:S(2)}, u32[]{:S(2)}) %collective-permute-start.42) | collective-permute-done | bytes 983072 | tf_op jit(solution)/shard_map/ppermute | solution.py:37
  266.0 4.2 %collective-permute-done.47 = f32[24,768]{1,0:T(8,128)S(1)} collective-permute-done((f32[24,768]{1,0:T(8,128)}, f32[24,768]{1,0:T(8,128)S(1)}, u32[]{:S(2)}, u32[]{:S(2)}) %collective-permute-start.47) | collective-permute-done | bytes 73760 | tf_op jit(solution)/shard_map/ppermute | solution.py:47
  270.3 5.2 %collective-permute-done.48 = f32[24,768]{1,0:T(8,128)S(1)} collective-permute-done((f32[24,768]{1,0:T(8,128)S(1)}, f32[24,768]{1,0:T(8,128)S(1)}, u32[]{:S(2)}, u32[]{:S(2)}) %collective-permute-start.48) | collective-permute-done | bytes 73760 | tf_op jit(solution)/shard_map/ppermute | solution.py:47
  278.2 3.3 %collective-permute-done.50 = f32[24,768]{1,0:T(8,128)S(1)} collective-permute-done((f32[24,768]{1,0:T(8,128)S(1)}, f32[24,768]{1,0:T(8,128)S(1)}, u32[]{:S(2)}, u32[]{:S(2)}) %collective-permute-start.50) | collective-permute-done | bytes 73760 | tf_op jit(solution)/shard_map/ppermute | solution.py:37
  284.4 5.8 %text_rows.1 = f32[512,768]{1,0:T(8,128)} custom-call(bf16[576,256]{1,0:T(8,128)(2,1)} %get-tuple-element.394.refs_0_, bf16[576,512]{1,0:T(8,128)(2,1)} %get-tuple-element.395.refs_1_, bf16[576,256]{1,0:T(8,128)(2,1)} %get-tuple-element.396.refs_2_, bf16[576,512]{1,0:T(8,128)(2,1)} %get-tuple-element.397.refs_3_, ...), custom_call_target="tpu_custom_call" | custom-call | bytes 25000 | tf_op jit(solution)/shard_map/text_rows/pallas_call | solution.py:777
  (279 shorter events, 89.2 us)
Async XLA Ops:
  3.8 24.0 %collective-permute-start = (bf16[144,768]{1,0:T(8,128)(2,1)}, bf16[144,768]{1,0:T(8,128)(2,1)}, u32[]{:S(2)}, u32[]{:S(2)}) collective-permute-start(bf16[144,768]{1,0:T(8,128)(2,1)} %pack_first.1.refs_0_), channel_id=1, source_target_pairs={{0,1},{1,2},{2,3},{3,0},{4,5},{5,6},{6,7},{7,4},{8,9},{9,10},{10,1... | collective-permute-start | bytes 663560 | tf_op jit(solution)/shard_map/ppermute | solution.py:42
  6.9 21.0 %collective-permute-start.1 = (bf16[144,768]{1,0:T(8,128)(2,1)}, bf16[144,768]{1,0:T(8,128)(2,1)}, u32[]{:S(2)}, u32[]{:S(2)}) collective-permute-start(bf16[144,768]{1,0:T(8,128)(2,1)} %pack_first.1.refs_0_), channel_id=1, source_target_pairs={{0,2},{1,3},{2,0},{3,1},{4,6},{5,7},{6,4},{7,5},{8,10},{9,11},{10,... | collective-permute-start | bytes 663560 | tf_op jit(solution)/shard_map/ppermute | solution.py:42
  9.5 18.4 %collective-permute-start.2 = (bf16[144,768]{1,0:T(8,128)(2,1)}, bf16[144,768]{1,0:T(8,128)(2,1)}, u32[]{:S(2)}, u32[]{:S(2)}) collective-permute-start(bf16[144,768]{1,0:T(8,128)(2,1)} %pack_first.1.refs_0_), channel_id=1, source_target_pairs={{0,3},{1,0},{2,1},{3,2},{4,7},{5,4},{6,5},{7,6},{8,11},{9,8},{10,9... | collective-permute-start | bytes 663560 | tf_op jit(solution)/shard_map/ppermute | solution.py:42
  30.2 28.3 %collective-permute-start.5 = (bf16[576,768]{1,0:T(8,128)(2,1)}, bf16[576,768]{1,0:T(8,128)(2,1)S(1)}, u32[]{:S(2)}, u32[]{:S(2)}) collective-permute-start(bf16[576,768]{1,0:T(8,128)(2,1)} %order_blocks.2.refs_0_), channel_id=1, source_target_pairs={{0,8},{4,12},{8,0},{12,4},{16,24},{20,28},{24,16},{28,20},{1,9},{5... | collective-permute-start | bytes 2654216 | tf_op jit(solution)/shard_map/ppermute | solution.py:37
  30.8 27.8 %collective-permute-start.6 = (bf16[576,768]{1,0:T(8,128)(2,1)}, bf16[576,768]{1,0:T(8,128)(2,1)S(1)}, u32[]{:S(2)}, u32[]{:S(2)}) collective-permute-start(bf16[576,768]{1,0:T(8,128)(2,1)} %order_blocks.2.refs_0_), channel_id=1, source_target_pairs={{0,16},{4,20},{8,24},{12,28},{16,0},{20,4},{24,8},{28,12},{1,17},{... | collective-permute-start | bytes 2654216 | tf_op jit(solution)/shard_map/ppermute | solution.py:37
  31.3 27.3 %collective-permute-start.7 = (bf16[576,768]{1,0:T(8,128)(2,1)}, bf16[576,768]{1,0:T(8,128)(2,1)S(1)}, u32[]{:S(2)}, u32[]{:S(2)}) collective-permute-start(bf16[576,768]{1,0:T(8,128)(2,1)} %order_blocks.2.refs_0_), channel_id=1, source_target_pairs={{0,4},{4,0},{8,12},{12,8},{16,20},{20,16},{24,28},{28,24},{1,5},{5... | collective-permute-start | bytes 2654216 | tf_op jit(solution)/shard_map/ppermute | solution.py:37
  31.3 19.7 %collective-permute-start.8 = (bf16[216,768]{1,0:T(8,128)(2,1)S(1)}, bf16[216,768]{1,0:T(8,128)(2,1)S(1)}, u32[]{:S(2)}, u32[]{:S(2)}) collective-permute-start(bf16[216,768]{1,0:T(8,128)(2,1)S(1)} %pad_maximum_fusion.4.refs_0_), channel_id=1, source_target_pairs={{0,1},{1,2},{2,3},{3,0},{4,5},{5,6},{6,7},{7,4},{8,9},{9,10},{10,1... | collective-permute-start | bytes 995336 | tf_op jit(solution)/shard_map/ppermute | solution.py:42
  34.9 23.7 %collective-permute-start.9 = (bf16[216,768]{1,0:T(8,128)(2,1)S(1)}, bf16[216,768]{1,0:T(8,128)(2,1)S(1)}, u32[]{:S(2)}, u32[]{:S(2)}) collective-permute-start(bf16[216,768]{1,0:T(8,128)(2,1)S(1)} %pad_maximum_fusion.4.refs_0_), channel_id=1, source_target_pairs={{0,2},{1,3},{2,0},{3,1},{4,6},{5,7},{6,4},{7,5},{8,10},{9,11},{10,... | collective-permute-start | bytes 995336 | tf_op jit(solution)/shard_map/ppermute | solution.py:42
  75.1 24.9 %collective-permute-start.17 = (bf16[672,768]{1,0:T(8,128)(2,1)}, bf16[672,768]{1,0:T(8,128)(2,1)S(1)}, u32[]{:S(2)}, u32[]{:S(2)}) collective-permute-start(bf16[672,768]{1,0:T(8,128)(2,1)} %order_blocks.3.refs_0_), channel_id=1, source_target_pairs={{0,8},{4,12},{8,0},{12,4},{16,24},{20,28},{24,16},{28,20},{1,9},{5... | collective-permute-start | bytes 3096584 | tf_op jit(solution)/shard_map/ppermute | solution.py:37
  76.6 24.6 %collective-permute-start.18 = (bf16[672,768]{1,0:T(8,128)(2,1)}, bf16[672,768]{1,0:T(8,128)(2,1)S(1)}, u32[]{:S(2)}, u32[]{:S(2)}) collective-permute-start(bf16[672,768]{1,0:T(8,128)(2,1)} %order_blocks.3.refs_0_), channel_id=1, source_target_pairs={{0,16},{4,20},{8,24},{12,28},{16,0},{20,4},{24,8},{28,12},{1,17},{... | collective-permute-start | bytes 3096584 | tf_op jit(solution)/shard_map/ppermute | solution.py:37
  77.2 24.0 %collective-permute-start.19 = (bf16[672,768]{1,0:T(8,128)(2,1)}, bf16[672,768]{1,0:T(8,128)(2,1)S(1)}, u32[]{:S(2)}, u32[]{:S(2)}) collective-permute-start(bf16[672,768]{1,0:T(8,128)(2,1)} %order_blocks.3.refs_0_), channel_id=1, source_target_pairs={{0,4},{4,0},{8,12},{12,8},{16,20},{20,16},{24,28},{28,24},{1,5},{5... | collective-permute-start | bytes 3096584 | tf_op jit(solution)/shard_map/ppermute | solution.py:37
  77.2 17.8 %collective-permute-start.20 = (bf16[192,768]{1,0:T(8,128)(2,1)S(1)}, bf16[192,768]{1,0:T(8,128)(2,1)S(1)}, u32[]{:S(2)}, u32[]{:S(2)}) collective-permute-start(bf16[192,768]{1,0:T(8,128)(2,1)S(1)} %pad_maximum_fusion.5.refs_10_), channel_id=1, source_target_pairs={{0,4},{4,0},{8,12},{12,8},{16,20},{20,16},{24,28},{28,24},{1,5},{5... | collective-permute-start | bytes 884744 | tf_op jit(solution)/shard_map/ppermute | solution.py:37
  77.7 17.3 %collective-permute-start.21 = (bf16[192,768]{1,0:T(8,128)(2,1)S(1)}, bf16[192,768]{1,0:T(8,128)(2,1)S(1)}, u32[]{:S(2)}, u32[]{:S(2)}) collective-permute-start(bf16[192,768]{1,0:T(8,128)(2,1)S(1)} %copy-done.28), channel_id=1, source_target_pairs={{0,4},{4,0},{8,12},{12,8},{16,20},{20,16},{24,28},{28,24},{1,5},{5... | collective-permute-start | bytes 884744 | tf_op jit(solution)/shard_map/ppermute | solution.py:37
  101.2 19.2 %collective-permute-start.24 = (bf16[672,768]{1,0:T(8,128)(2,1)S(1)}, bf16[672,768]{1,0:T(8,128)(2,1)S(1)}, u32[]{:S(2)}, u32[]{:S(2)}) collective-permute-start(bf16[672,768]{1,0:T(8,128)(2,1)S(1)} %collective-permute-done.17.refs_2_), channel_id=1, source_target_pairs={{0,4},{4,0},{8,12},{12,8},{16,20},{20,16},{24,28},{28,24},{1,5},{5... | collective-permute-start | bytes 3096584 | tf_op jit(solution)/shard_map/ppermute | solution.py:37
  101.2 19.1 %collective-permute-start.25 = (bf16[672,768]{1,0:T(8,128)(2,1)S(1)}, bf16[672,768]{1,0:T(8,128)(2,1)S(1)}, u32[]{:S(2)}, u32[]{:S(2)}) collective-permute-start(bf16[672,768]{1,0:T(8,128)(2,1)S(1)} %collective-permute-done.18.refs_4_), channel_id=1, source_target_pairs={{0,4},{4,0},{8,12},{12,8},{16,20},{20,16},{24,28},{28,24},{1,5},{5... | collective-permute-start | bytes 3096584 | tf_op jit(solution)/shard_map/ppermute | solution.py:37
  101.8 18.5 %collective-permute-start.23 = (bf16[480,768]{1,0:T(8,128)(2,1)S(1)}, bf16[480,768]{1,0:T(8,128)(2,1)S(1)}, u32[]{:S(2)}, u32[]{:S(2)}) collective-permute-start(bf16[480,768]{1,0:T(8,128)(2,1)S(1)} %slice.224), channel_id=1, source_target_pairs={{0,8},{4,12},{8,0},{12,4},{16,24},{20,28},{24,16},{28,20},{1,9},{5... | collective-permute-start | bytes 2211848 | tf_op jit(solution)/shard_map/ppermute | solution.py:37
  162.2 18.0 %collective-permute-start.32 = (bf16[4,2,4,96,768]{4,3,2,1,0:T(8,128)(2,1)}, bf16[4,2,4,96,768]{4,3,2,1,0:T(8,128)(2,1)}, u32[]{:S(2)}, u32[]{:S(2)}) collective-permute-start(bf16[4,2,4,96,768]{4,3,2,1,0:T(8,128)(2,1)} %get-tuple-element.313), channel_id=1, source_target_pairs={{0,4},{4,0},{8,12},{12,8},{16,20},{20,16},{24,28},{28,24},{1,5},{5... | collective-permute-start | bytes 14155784 | tf_op jit(solution)/shard_map/ppermute | solution.py:37
  183.1 28.7 %collective-permute-start.35 = (bf16[2,4,96,768]{3,2,1,0:T(8,128)(2,1)S(1)}, bf16[2,4,96,768]{3,2,1,0:T(8,128)(2,1)S(1)}, u32[]{:S(2)}, u32[]{:S(2)}) collective-permute-start(bf16[2,4,96,768]{3,2,1,0:T(8,128)(2,1)S(1)} %pad_maximum_fusion), channel_id=1, source_target_pairs={{0,8},{4,12},{8,0},{12,4},{16,24},{20,28},{24,16},{28,20},{1,9},{5... | collective-permute-start | bytes 3538952 | tf_op jit(solution)/shard_map/ppermute | solution.py:37
  184.3 27.6 %collective-permute-start.36 = (bf16[2,4,96,768]{3,2,1,0:T(8,128)(2,1)S(1)}, bf16[2,4,96,768]{3,2,1,0:T(8,128)(2,1)}, u32[]{:S(2)}, u32[]{:S(2)}) collective-permute-start(bf16[2,4,96,768]{3,2,1,0:T(8,128)(2,1)S(1)} %pad_maximum_fusion.1), channel_id=1, source_target_pairs={{0,16},{4,20},{8,24},{12,28},{16,0},{20,4},{24,8},{28,12},{1,17},{... | collective-permute-start | bytes 3538952 | tf_op jit(solution)/shard_map/ppermute | solution.py:37
  235.1 23.1 %collective-permute-start.42 = (bf16[640,768]{1,0:T(8,128)(2,1)}, bf16[640,768]{1,0:T(8,128)(2,1)S(1)}, u32[]{:S(2)}, u32[]{:S(2)}) collective-permute-start(bf16[640,768]{1,0:T(8,128)(2,1)} %pad_maximum_fusion.2), channel_id=1, source_target_pairs={{0,8},{4,12},{8,0},{12,4},{16,24},{20,28},{24,16},{28,20},{1,9},{5... | collective-permute-start | bytes 2949128 | tf_op jit(solution)/shard_map/ppermute | solution.py:37
  236.1 22.7 %collective-permute-start.43 = (bf16[640,768]{1,0:T(8,128)(2,1)S(1)}, bf16[640,768]{1,0:T(8,128)(2,1)}, u32[]{:S(2)}, u32[]{:S(2)}) collective-permute-start(bf16[640,768]{1,0:T(8,128)(2,1)S(1)} %pad_maximum_fusion.3), channel_id=1, source_target_pairs={{0,16},{4,20},{8,24},{12,28},{16,0},{20,4},{24,8},{28,12},{1,17},{... | collective-permute-start | bytes 2949128 | tf_op jit(solution)/shard_map/ppermute | solution.py:37
  237.1 18.2 %collective-permute-start.44 = (bf16[2,96,768]{2,1,0:T(8,128)(2,1)S(1)}, bf16[2,96,768]{2,1,0:T(8,128)(2,1)S(1)}, u32[]{:S(2)}, u32[]{:S(2)}) collective-permute-start(bf16[2,96,768]{2,1,0:T(8,128)(2,1)S(1)} %get-tuple-element.434), channel_id=1, source_target_pairs={{0,2},{1,3},{2,0},{3,1},{4,6},{5,7},{6,4},{7,5},{8,10},{9,11},{10,... | collective-permute-start | bytes 884744 | tf_op jit(solution)/shard_map/ppermute | solution.py:42
  237.1 18.2 %collective-permute-start.45 = (bf16[2,96,768]{2,1,0:T(8,128)(2,1)S(1)}, bf16[2,96,768]{2,1,0:T(8,128)(2,1)}, u32[]{:S(2)}, u32[]{:S(2)}) collective-permute-start(bf16[2,96,768]{2,1,0:T(8,128)(2,1)S(1)} %get-tuple-element.433), channel_id=1, source_target_pairs={{0,3},{1,0},{2,1},{3,2},{4,7},{5,4},{6,5},{7,6},{8,11},{9,8},{10,9... | collective-permute-start | bytes 884744 | tf_op jit(solution)/shard_map/ppermute | solution.py:42
  275.8 17.2 %collective-permute-start.52 = (bf16[160,768]{1,0:T(8,128)(2,1)S(1)}, bf16[160,768]{1,0:T(8,128)(2,1)S(1)}, u32[]{:S(2)}, u32[]{:S(2)}) collective-permute-start(bf16[160,768]{1,0:T(8,128)(2,1)S(1)} %pad_maximum_fusion.8), channel_id=1, source_target_pairs={{0,2},{1,3},{2,0},{3,1},{4,6},{5,7},{6,4},{7,5},{8,10},{9,11},{10,... | collective-permute-start | bytes 737288 | tf_op jit(solution)/shard_map/ppermute | solution.py:42
  (86 other events, 807.5 us)

commit v5 on v4

--- a/solution.py
+++ b/solution.py
@@ -220,7 +220,15 @@
     return pl.CostEstimate(flops=flops // 1000, bytes_accessed=nbytes // 1000, transcendentals=0)
 
 
-def pack_kernel(q_ref, k_ref, v_ref, p_ref, visual_ref, out_ref):
+def pack_kernel(q_ref, k_ref, v_ref, p_ref, visual_ref, *refs):
+    out_ref = refs[-1]
+    if len(refs) > 1:
+        output_ref, outer_ref, inner_ref, out_ref, wide_ref, late_ref = refs
+        size, first = inner_ref.shape[0], output_ref.shape[0]
+        late_ref[:first, :] = output_ref[...]
+        for n, value in enumerate((outer_ref[...], inner_ref[...])):
+            wide_ref[n * size : (n + 1) * size, :] = value
+            late_ref[first + n * size : first + (n + 1) * size, :] = value
     row = 0
     for ref in (q_ref, k_ref, v_ref, p_ref):
         out_ref[row : row + ref.shape[0], :] = ref[...]
@@ -238,16 +246,19 @@
     out_ref[row:, :] = jnp.concatenate(rows, 0).astype(BF16)
 
 
-def pack_first(w_query, w_key, w_value, vis_proj, visual):
+def pack_first(w_query, w_key, w_value, vis_proj, visual, late=()):
     width = w_query.shape[1]
     moments = 3 * visual.shape[1] // width
     rows = [w.shape[0] for w in (w_query, w_key, w_value, vis_proj)] + [moments]
-    own = pl.pallas_call(
+    sizes = [sum(rows)]
+    if late:
+        sizes += [2 * late[2].shape[0], late[0].shape[0] + 2 * late[2].shape[0]]
+    packed = pl.pallas_call(
         pack_kernel,
-        out_shape=jax.ShapeDtypeStruct((sum(rows), width), BF16),
+        out_shape=[jax.ShapeDtypeStruct((size, width), BF16) for size in sizes],
         name="pack_first",
-    )(w_query, w_key, w_value, vis_proj, visual)
-    return own, rows
+    )(w_query, w_key, w_value, vis_proj, visual, *late)
+    return packed, rows
 
 
 def order_kernel(rows, rest, here_ref, *refs):
@@ -1199,15 +1210,21 @@
     outer_shard = w_outer.T
     steps = rows // 64
 
-    first_set = Gather(*pack_first(w_query, w_key, w_value, vis_proj, visual_maps))
     plain = columns == width
     early = plain and dp == 8
     here = lax.axis_index("ffn")
-    wide_shards = jnp.concatenate([outer_shard, w_inner], 0)
+    packed, sizes = pack_first(
+        w_query,
+        w_key,
+        w_value,
+        vis_proj,
+        visual_maps,
+        (w_output, outer_shard, w_inner) if early else (),
+    )
+    first_set = Gather(packed[0], sizes)
+    wide_shards = packed[1] if early else jnp.concatenate([outer_shard, w_inner], 0)
     if early:
-        late_set = Gather(
-            jnp.concatenate([w_output, wide_shards], 0), [w_output.shape[0]], 2 * inner_rows
-        )
+        late_set = Gather(packed[2], [w_output.shape[0]], 2 * inner_rows)
     elif plain:
         late_set = Gather(
             jnp.concatenate([w_output, wide_shards], 0), [w_output.shape[0], inner_rows, inner_rows]
@@ -1223,9 +1240,8 @@
         wides += [send_dp(wide_shards, 2), send_dp(wide_shards, 4)]
     tables = jnp.concatenate([x_table, y_table, rel_table], 0).T
     tables = jnp.pad(tables, ((0, 0), (0, 256 - tables.shape[1])))
-    cuts = [0, steps // 9, steps * 7 // 9, steps]
-    words = [None] * 3
-    words[0], unit = bias_words(rel_bucket, x_bucket, y_bucket, tables, 0, cuts[1])
+    cut = steps * 7 // 9
+    words = [None] * 2
     ranges = document_blocks(segment_ids[0], rows)
     lines = jnp.stack([first_gain, first_bias, b_outer, second_gain, second_bias])
     inner_b = b_inner.reshape(ffn, 1, columns)
@@ -1233,12 +1249,11 @@
     bn_lines = jnp.stack([bn_scale, bn_shift])
     order = [(here - k + ffn) % ffn if early else jnp.int32(k) for k in range(ffn)]
     place = jnp.stack([place] + order).astype(jnp.int32)
-    state, late, place, wides, words[0], tables, ranges, lines, inner_b, segments, bn_lines = epoch(
+    state, late, place, wides, tables, ranges, lines, inner_b, segments, bn_lines = epoch(
         first_set.state(),
         late_set.state(),
         place,
         wides,
-        words[0],
         tables,
         ranges,
         lines,
@@ -1252,8 +1267,8 @@
     first_set.order()
     first_set.near(3 * w_query.shape[0] * ffn)
     late_set.along_ffn(1, ffn - 1)
-    words[1], _ = bias_words(rel_bucket, x_bucket, y_bucket, tables, cuts[1], cuts[2] - cuts[1])
-    state, late, words[1], tables = epoch(first_set.state(), late_set.state(), words[1], tables)
+    words[0], unit = bias_words(rel_bucket, x_bucket, y_bucket, tables, 0, cut)
+    state, late, words[0], tables = epoch(first_set.state(), late_set.state(), words[0], tables)
     first_set.hold(state)
     late_set.hold(late)
 
@@ -1290,8 +1305,8 @@
         first_set.rows[-1],
     )
     qkv, tables = epoch(qkv, tables)
-    words[2], _ = bias_words(rel_bucket, x_bucket, y_bucket, tables, cuts[2], cuts[3] - cuts[2])
-    qkv, state, words[2], wides = epoch(qkv, late_set.state(), words[2], wides)
+    words[1], _ = bias_words(rel_bucket, x_bucket, y_bucket, tables, cut, steps - cut)
+    qkv, state, words[1], wides = epoch(qkv, late_set.state(), words[1], wides)
     late_set.hold(state)
 
     late_set.diagonal()

time: 300 us -> 299 us (level)
  waiting for transfers between devices: 57.2 us -> 50.4 us
  starting transfers between devices: 42.3 us -> 47.1 us
  local copies, waits for them, and re-layouts: 11.5 us -> 16.3 us
  Pallas kernels: 162 us -> 158 us
    ppermute x12, waiting for transfers between devices: 23 us -> 15.8 us  [send_ffn(): lax.ppermute(values, 'ffn', [(i, (i + shift) % size) for i in range(size)])]
    ppermute x12, starting transfers between devices: 16 us -> 19.5 us  [send_ffn(): lax.ppermute(values, 'ffn', [(i, (i + shift) % size) for i in range(size)])]
    another operation x6, local copies, waits for them, and re-layouts: 0.66 us -> 4.09 us  [on_device(): jnp.stack([first_gain, first_bias, b_outer, second_gain, second_bias])]
    pallas_call x3 -> x2, Pallas kernels: 24.7 us -> 22.7 us  [bias_words(): pl.pallas_call(functools.partial(bias_kernel, step), grid=(steps,), in_sp...]
    unnamed x115 -> x95, local copies, waits for them, and re-layouts: 6.08 us -> 6.72 us
  transfers between devices with their start and end apart: 54 -> 54, of which waited for: 23 -> 22; matrix products, arithmetic and copies ran while one was open for 6% -> 8% of each run, Pallas kernels for 41% -> 40%
where the time goes in v5:
time: 299 us; the launch traced here: 294 us
  Pallas kernels  158 us (53%)
  waiting for transfers between devices  50.4 us (17%)
  starting transfers between devices  47.1 us (16%)
  other arithmetic  20.7 us (7%)
  local copies, waits for them, and re-layouts  16.3 us (5%)
    pallas_call x1, Pallas kernels, feed_forward(): pl.pallas_call(functools.partial(feed_kernel, entries, place_bits(parts),...  34.2 us
    ppermute x40, starting transfers between devices, send_dp(): return lax.ppermute(values, 'dp', [(i, i ^ bits) for i in range(size)])  27.5 us
    ppermute x40, waiting for transfers between devices, send_dp(): return lax.ppermute(values, 'dp', [(i, i ^ bits) for i in range(size)])  25.2 us
    pallas_call x2, Pallas kernels, bias_words(): pl.pallas_call(functools.partial(bias_kernel, step), grid=(steps,), in_sp...  22.7 us
    ppermute x12, starting transfers between devices, send_ffn(): lax.ppermute(values, 'ffn', [(i, (i + shift) % size) for i in range(size)])  19.5 us
    pallas_call x2, Pallas kernels, attend_back(): pl.pallas_call(attend_back_kernel, grid=(pairs,), in_specs=[col[0], col[1...  19.4 us
    ppermute x12, waiting for transfers between devices, send_ffn(): lax.ppermute(values, 'ffn', [(i, (i + shift) % size) for i in range(size)])  15.8 us
    pallas_call x1, Pallas kernels, table_sums(): pl.pallas_call(functools.partial(table_kernel, first, levels), grid_spec=...  15.5 us
  transfers between devices with their start and end apart: 54, of which 22 were waited for; matrix products, arithmetic and copies ran while one was open for 8% of the time, Pallas kernels for 40%

profile of v5, /device:TPU:0, one launch (start us, length us, event | category | flops | bytes accessed | tf_op | source)
XLA Modules:
  0.0 294.4 jit_solution(8097065121819543151)
XLA Ops:
  2.9 3.0 %collective-permute-start = (bf16[144,768]{1,0:T(8,128)(2,1)}, bf16[144,768]{1,0:T(8,128)(2,1)S(1)}, u32[]{:S(2)}, u32[]{:S(2)}) collective-permute-start(bf16[144,768]{1,0:T(8,128)(2,1)} %get-tuple-element.230.refs_0_), channel_id=1, source_target_pairs={{0,1},{1,2},{2,3},{3,0},{4,5},{5,6},{6,7},{7,4},{8,9},{9,10},{10,1... | collective-permute-start | bytes 663560 | tf_op jit(solution)/shard_map/ppermute | solution.py:42
  6.0 2.6 collective-permute-start.1
  29.4 5.1 %collective-permute-start.8 = (bf16[216,768]{1,0:T(8,128)(2,1)S(1)}, bf16[216,768]{1,0:T(8,128)(2,1)S(1)}, u32[]{:S(2)}, u32[]{:S(2)}) collective-permute-start(bf16[216,768]{1,0:T(8,128)(2,1)S(1)} %copy-done.20), channel_id=1, source_target_pairs={{0,1},{1,2},{2,3},{3,0},{4,5},{5,6},{6,7},{7,4},{8,9},{9,10},{10,1... | collective-permute-start | bytes 995336 | tf_op jit(solution)/shard_map/ppermute | solution.py:42
  40.4 16.5 %bias_words.2 = (s32[6,448,640]{2,1,0:T(8,128)}, f32[1,1]{1,0:T(1,128)}) custom-call(s32[1,561,561]{2,1,0:T(8,128)} %copy.65.rel_ref, s32[1,561,561]{2,1,0:T(8,128)} %copy.66.x_ref, s32[1,561,561]{2,1,0:T(8,128)} %copy.67.y_ref, f32[12,256]{1,0:T(8,128)} %pad.8.tab_ref), custom_call_target="tpu_custom_call" | custom-call | bytes 42000 | tf_op jit(solution)/shard_map/bias_words/pallas_call | solution.py:936
  61.4 7.9 %collective-permute-done.14.refs_3_ = bf16[216,768]{1,0:T(8,128)(2,1)S(1)} collective-permute-done((bf16[216,768]{1,0:T(8,128)(2,1)S(1)}, bf16[216,768]{1,0:T(8,128)(2,1)S(1)}, u32[]{:S(2)}, u32[]{:S(2)}) %collective-permute-start.14) | collective-permute-done | bytes 331808 | tf_op jit(solution)/shard_map/ppermute | solution.py:42
  72.0 2.7 order_blocks.3.refs_0_
  77.5 11.0 %first_rows.1 = (bf16[768,2304]{1,0:T(8,128)(2,1)}, bf16[2048,768]{1,0:T(8,128)(2,1)}, f32[576,768]{1,0:T(8,128)}, bf16[768,576]{1,0:T(8,128)(2,1)}, bf16[576,23...) custom-call(s32[5]{0:T(128)} %stack.50.place_ref, bf16[576,768]{1,0:T(8,128)(2,1)} %order_blocks.2.refs_0_, ...), custom_call_target="tpu_custom_call" | custom-call | bytes 25000 | tf_op jit(solution)/shard_map/first_rows/pallas_call | solution.py:404
  88.5 6.2 %bias_words.3 = (s32[6,128,640]{2,1,0:T(8,128)}, f32[1,1]{1,0:T(1,128)}) custom-call(s32[1,561,561]{2,1,0:T(8,128)} %copy.65.rel_ref, s32[1,561,561]{2,1,0:T(8,128)} %copy.66.x_ref, s32[1,561,561]{2,1,0:T(8,128)} %copy.67.y_ref, f32[12,256]{1,0:T(8,128)} %pad.8.tab_ref), custom_call_target="tpu_custom_call" | custom-call | bytes 12000 | tf_op jit(solution)/shard_map/bias_words/pallas_call | solution.py:936
  94.7 5.0 %collective-permute-done.17.refs_2_ = bf16[672,768]{1,0:T(8,128)(2,1)S(1)} collective-permute-done((bf16[672,768]{1,0:T(8,128)(2,1)}, bf16[672,768]{1,0:T(8,128)(2,1)S(1)}, u32[]{:S(2)}, u32[]{:S(2)}) %collective-permute-start.17) | collective-permute-done | bytes 1032224 | tf_op jit(solution)/shard_map/ppermute | solution.py:37
  104.9 14.5 %attend.1 = (bf16[12,576,576]{2,1,0:T(8,128)(2,1)}, bf16[576,768]{1,0:T(8,128)(2,1)}) custom-call(f32[1,1]{1,0:T(1,128)} %get-tuple-element.229.unit_ref, bf16[576,2304]{1,0:T(8,128)(2,1)} %get-tuple-element.336.q_ref.k_ref.v_ref, bf16[576,2304]{1,0:T(8,128)(2,1)} %get-tuple-element.336.q_ref.k_ref.v_ref, ...), custom_call_target="tpu_custom_call" | custom-call | flops 2038431 | bytes 40000 | tf_op jit(solution)/shard_map/attend/pallas_call | solution.py:990
  124.1 34.2 %feed_forward.1 = (f32[576,768]{1,0:T(8,128)}, bf16[768,768]{1,0:T(8,128)(2,1)}, bf16[561,768]{1,0:T(8,128)(2,1)}, f32[576,1]{1,0:T(8,128)}, f32[576,768]{1,0:T(...) custom-call(s32[5]{0:T(128)} %stack.50.place_ref, ...), custom_call_target="tpu_custom_call" | custom-call | bytes 100000 | tf_op jit(solution)/shard_map/feed_forward/pallas_call | solution.py:584
  158.5 2.9 collective-permute-done.31
  165.8 5.4 %norm_rows.1 = (f32[576,768]{1,0:T(8,128)}, bf16[576,768]{1,0:T(8,128)(2,1)}, bf16[576,768]{1,0:T(8,128)(2,1)}, f32[2,768]{1,0:T(2,128)}) custom-call(f32[576,768]{1,0:T(8,128)} %get-tuple-element.318.grad_ref, f32[576,768]{1,0:T(8,128)} %get-tuple-element.319.normed_ref, f32[576,1]{1,0:T(8,128)} %get-tuple-element.320.scale_ref, ...), custom_call_target="tpu_custom_call" | custom-call | bytes 12000 | tf_op jit(solution)/shard_map/norm_rows/pallas_call | solution.py:644
  171.2 7.6 %attend_back.2 = (bf16[4,576,640]{2,1,0:T(8,128)(2,1)}, bf16[576,256]{1,0:T(8,128)(2,1)}, bf16[576,256]{1,0:T(8,128)(2,1)}, bf16[576,256]{1,0:T(8,128)(2,1)}) custom-call(bf16[576,2304]{1,0:T(8,128)(2,1)} %get-tuple-element.336.q_ref.k_ref.v_ref, bf16[576,2304]{1,0:T(8,128)(2,1)} %get-tuple-element.336.q_ref.k_ref.v_ref, ...), custom_call_target="tpu_custom_call" | custom-call | flops 1358954 | bytes 16000 | tf_op jit(solution)/shard_map/attend_back/pallas_call | solution.py:1047
  185.0 11.8 %attend_back.3 = (bf16[8,576,640]{2,1,0:T(8,128)(2,1)}, bf16[576,512]{1,0:T(8,128)(2,1)}, bf16[576,512]{1,0:T(8,128)(2,1)}, bf16[576,512]{1,0:T(8,128)(2,1)}) custom-call(bf16[576,2304]{1,0:T(8,128)(2,1)} %get-tuple-element.336.q_ref.k_ref.v_ref, bf16[576,2304]{1,0:T(8,128)(2,1)} %get-tuple-element.336.q_ref.k_ref.v_ref, ...), custom_call_target="tpu_custom_call" | custom-call | flops 2717908 | bytes 32000 | tf_op jit(solution)/shard_map/attend_back/pallas_call | solution.py:1047
  196.8 14.6 %tail_rows.1 = (bf16[49,768]{1,0:T(8,128)(2,1)}, bf16[4,640,768]{2,1,0:T(8,128)(2,1)}, bf16[4,640,768]{2,1,0:T(8,128)(2,1)}, bf16[640,768]{1,0:T(8,128)(2,1)}) custom-call(s32[5]{0:T(128)} %stack.50.place_ref, bf16[576,256]{1,0:T(8,128)(2,1)} %get-tuple-element.396.refs_0_, bf16[576,512]{1,0:T(8,128)(2,1)} %get-tuple-element.397.refs_1_, ...), custom_call_target="tpu_custom_call" | custom-call | bytes 40000 | tf_op jit(solution)/shard_map/tail_rows/pallas_call | solution.py:730
  217.7 4.0 %batch_rows.1 = (f32[49,2048]{1,0:T(8,128)}, f32[2,2048]{1,0:T(2,128)}) custom-call(bf16[49,768]{1,0:T(8,128)(2,1)} %get-tuple-element.362.tokens_ref, bf16[49,2048]{1,0:T(8,128)(2,1)} %refs_3_.1, f32[2,2048]{1,0:T(2,128)} %get-tuple-element.363.stats_ref.refs_4_, bf16[2048,768]{1,0:T(8,128)(2,1)} %get-tuple-element.364.proj_ref), custom_call_target="tpu_custom_call" | custom-call | bytes 6000 | tf_op jit(solution)/shard_map/batch_rows/pallas_call | solution.py:761
  221.7 6.5 %collective-permute-done.41 = bf16[2,96,768]{2,1,0:T(8,128)(2,1)S(1)} collective-permute-done((bf16[2,96,768]{2,1,0:T(8,128)(2,1)S(1)}, bf16[2,96,768]{2,1,0:T(8,128)(2,1)S(1)}, u32[]{:S(2)}, u32[]{:S(2)}) %collective-permute-start.41) | collective-permute-done | bytes 294944 | tf_op jit(solution)/shard_map/ppermute | solution.py:42
  237.8 15.5 %table_sums.1.refs_0_ = f32[96,80]{1,0:T(8,128)} custom-call(s32[12]{0:T(128)} %get-tuple-element.377.block_ref, s32[12]{0:T(128)} %get-tuple-element.378.count_ref, s32[1,561,561]{2,1,0:T(8,128)} %copy.65.rel_ref, s32[1,561,561]{2,1,0:T(8,128)} %copy.66.x_ref, s32[1,561,561]{2,1,0:T(8,128)} %copy.67.y_ref, bf16[4,576,640]{2,1,0:T(8,128)(2,1)} %get-tuple-element.379.refs_0_, ...), custom_call_target="tpu_custom_call" | custom-call | bytes 48000 | tf_op jit(solution)/shard_map/table_sums/pallas_call | solution.py:1128
  253.3 4.6 %collective-permute-done.42 = bf16[640,768]{1,0:T(8,128)(2,1)S(1)} collective-permute-done((bf16[640,768]{1,0:T(8,128)(2,1)}, bf16[640,768]{1,0:T(8,128)(2,1)S(1)}, u32[]{:S(2)}, u32[]{:S(2)}) %collective-permute-start.42) | collective-permute-done | bytes 983072 | tf_op jit(solution)/shard_map/ppermute | solution.py:37
  265.6 4.2 %collective-permute-done.47 = f32[24,768]{1,0:T(8,128)S(1)} collective-permute-done((f32[24,768]{1,0:T(8,128)}, f32[24,768]{1,0:T(8,128)S(1)}, u32[]{:S(2)}, u32[]{:S(2)}) %collective-permute-start.47) | collective-permute-done | bytes 73760 | tf_op jit(solution)/shard_map/ppermute | solution.py:47
  269.9 5.2 %collective-permute-done.48 = f32[24,768]{1,0:T(8,128)S(1)} collective-permute-done((f32[24,768]{1,0:T(8,128)S(1)}, f32[24,768]{1,0:T(8,128)S(1)}, u32[]{:S(2)}, u32[]{:S(2)}) %collective-permute-start.48) | collective-permute-done | bytes 73760 | tf_op jit(solution)/shard_map/ppermute | solution.py:47
  278.4 2.7 collective-permute-done.50
  284.0 5.8 %text_rows.1 = f32[512,768]{1,0:T(8,128)} custom-call(bf16[576,256]{1,0:T(8,128)(2,1)} %get-tuple-element.396.refs_0_, bf16[576,512]{1,0:T(8,128)(2,1)} %get-tuple-element.397.refs_1_, bf16[576,256]{1,0:T(8,128)(2,1)} %get-tuple-element.398.refs_2_, bf16[576,512]{1,0:T(8,128)(2,1)} %get-tuple-element.399.refs_3_, ...), custom_call_target="tpu_custom_call" | custom-call | bytes 25000 | tf_op jit(solution)/shard_map/text_rows/pallas_call | solution.py:788
  (256 shorter events, 93.2 us)
Async XLA Ops:
  2.9 20.9 %collective-permute-start = (bf16[144,768]{1,0:T(8,128)(2,1)}, bf16[144,768]{1,0:T(8,128)(2,1)S(1)}, u32[]{:S(2)}, u32[]{:S(2)}) collective-permute-start(bf16[144,768]{1,0:T(8,128)(2,1)} %get-tuple-element.230.refs_0_), channel_id=1, source_target_pairs={{0,1},{1,2},{2,3},{3,0},{4,5},{5,6},{6,7},{7,4},{8,9},{9,10},{10,1... | collective-permute-start | bytes 663560 | tf_op jit(solution)/shard_map/ppermute | solution.py:42
  6.0 17.8 %collective-permute-start.1 = (bf16[144,768]{1,0:T(8,128)(2,1)}, bf16[144,768]{1,0:T(8,128)(2,1)S(1)}, u32[]{:S(2)}, u32[]{:S(2)}) collective-permute-start(bf16[144,768]{1,0:T(8,128)(2,1)} %get-tuple-element.230.refs_0_), channel_id=1, source_target_pairs={{0,2},{1,3},{2,0},{3,1},{4,6},{5,7},{6,4},{7,5},{8,10},{9,11},{10,... | collective-permute-start | bytes 663560 | tf_op jit(solution)/shard_map/ppermute | solution.py:42
  27.0 31.3 %collective-permute-start.5 = (bf16[576,768]{1,0:T(8,128)(2,1)}, bf16[576,768]{1,0:T(8,128)(2,1)S(1)}, u32[]{:S(2)}, u32[]{:S(2)}) collective-permute-start(bf16[576,768]{1,0:T(8,128)(2,1)} %order_blocks.2.refs_0_), channel_id=1, source_target_pairs={{0,8},{4,12},{8,0},{12,4},{16,24},{20,28},{24,16},{28,20},{1,9},{5... | collective-permute-start | bytes 2654216 | tf_op jit(solution)/shard_map/ppermute | solution.py:37
  27.8 30.4 %collective-permute-start.6 = (bf16[576,768]{1,0:T(8,128)(2,1)}, bf16[576,768]{1,0:T(8,128)(2,1)S(1)}, u32[]{:S(2)}, u32[]{:S(2)}) collective-permute-start(bf16[576,768]{1,0:T(8,128)(2,1)} %order_blocks.2.refs_0_), channel_id=1, source_target_pairs={{0,16},{4,20},{8,24},{12,28},{16,0},{20,4},{24,8},{28,12},{1,17},{... | collective-permute-start | bytes 2654216 | tf_op jit(solution)/shard_map/ppermute | solution.py:37
  29.4 28.9 %collective-permute-start.7 = (bf16[576,768]{1,0:T(8,128)(2,1)}, bf16[576,768]{1,0:T(8,128)(2,1)S(1)}, u32[]{:S(2)}, u32[]{:S(2)}) collective-permute-start(bf16[576,768]{1,0:T(8,128)(2,1)} %order_blocks.2.refs_0_), channel_id=1, source_target_pairs={{0,4},{4,0},{8,12},{12,8},{16,20},{20,16},{24,28},{28,24},{1,5},{5... | collective-permute-start | bytes 2654216 | tf_op jit(solution)/shard_map/ppermute | solution.py:37
  29.4 27.6 %collective-permute-start.8 = (bf16[216,768]{1,0:T(8,128)(2,1)S(1)}, bf16[216,768]{1,0:T(8,128)(2,1)S(1)}, u32[]{:S(2)}, u32[]{:S(2)}) collective-permute-start(bf16[216,768]{1,0:T(8,128)(2,1)S(1)} %copy-done.20), channel_id=1, source_target_pairs={{0,1},{1,2},{2,3},{3,0},{4,5},{5,6},{6,7},{7,4},{8,9},{9,10},{10,1... | collective-permute-start | bytes 995336 | tf_op jit(solution)/shard_map/ppermute | solution.py:42
  34.5 23.8 %collective-permute-start.9 = (bf16[216,768]{1,0:T(8,128)(2,1)S(1)}, bf16[216,768]{1,0:T(8,128)(2,1)S(1)}, u32[]{:S(2)}, u32[]{:S(2)}) collective-permute-start(bf16[216,768]{1,0:T(8,128)(2,1)S(1)} %copy-done.20), channel_id=1, source_target_pairs={{0,2},{1,3},{2,0},{3,1},{4,6},{5,7},{6,4},{7,5},{8,10},{9,11},{10,... | collective-permute-start | bytes 995336 | tf_op jit(solution)/shard_map/ppermute | solution.py:42
  74.8 24.9 %collective-permute-start.17 = (bf16[672,768]{1,0:T(8,128)(2,1)}, bf16[672,768]{1,0:T(8,128)(2,1)S(1)}, u32[]{:S(2)}, u32[]{:S(2)}) collective-permute-start(bf16[672,768]{1,0:T(8,128)(2,1)} %order_blocks.3.refs_0_), channel_id=1, source_target_pairs={{0,8},{4,12},{8,0},{12,4},{16,24},{20,28},{24,16},{28,20},{1,9},{5... | collective-permute-start | bytes 3096584 | tf_op jit(solution)/shard_map/ppermute | solution.py:37
  75.4 24.6 %collective-permute-start.18 = (bf16[672,768]{1,0:T(8,128)(2,1)}, bf16[672,768]{1,0:T(8,128)(2,1)S(1)}, u32[]{:S(2)}, u32[]{:S(2)}) collective-permute-start(bf16[672,768]{1,0:T(8,128)(2,1)} %order_blocks.3.refs_0_), channel_id=1, source_target_pairs={{0,16},{4,20},{8,24},{12,28},{16,0},{20,4},{24,8},{28,12},{1,17},{... | collective-permute-start | bytes 3096584 | tf_op jit(solution)/shard_map/ppermute | solution.py:37
  76.9 23.1 %collective-permute-start.19 = (bf16[672,768]{1,0:T(8,128)(2,1)}, bf16[672,768]{1,0:T(8,128)(2,1)S(1)}, u32[]{:S(2)}, u32[]{:S(2)}) collective-permute-start(bf16[672,768]{1,0:T(8,128)(2,1)} %order_blocks.3.refs_0_), channel_id=1, source_target_pairs={{0,4},{4,0},{8,12},{12,8},{16,20},{20,16},{24,28},{28,24},{1,5},{5... | collective-permute-start | bytes 3096584 | tf_op jit(solution)/shard_map/ppermute | solution.py:37
  76.9 17.8 %collective-permute-start.20 = (bf16[192,768]{1,0:T(8,128)(2,1)S(1)}, bf16[192,768]{1,0:T(8,128)(2,1)S(1)}, u32[]{:S(2)}, u32[]{:S(2)}) collective-permute-start(bf16[192,768]{1,0:T(8,128)(2,1)S(1)} %copy-done.24), channel_id=1, source_target_pairs={{0,4},{4,0},{8,12},{12,8},{16,20},{20,16},{24,28},{28,24},{1,5},{5... | collective-permute-start | bytes 884744 | tf_op jit(solution)/shard_map/ppermute | solution.py:37
  77.4 17.3 %collective-permute-start.21 = (bf16[192,768]{1,0:T(8,128)(2,1)}, bf16[192,768]{1,0:T(8,128)(2,1)S(1)}, u32[]{:S(2)}, u32[]{:S(2)}) collective-permute-start(bf16[192,768]{1,0:T(8,128)(2,1)} %copy-done.25), channel_id=1, source_target_pairs={{0,4},{4,0},{8,12},{12,8},{16,20},{20,16},{24,28},{28,24},{1,5},{5... | collective-permute-start | bytes 884744 | tf_op jit(solution)/shard_map/ppermute | solution.py:37
  100.0 19.6 %collective-permute-start.24 = (bf16[672,768]{1,0:T(8,128)(2,1)S(1)}, bf16[672,768]{1,0:T(8,128)(2,1)S(1)}, u32[]{:S(2)}, u32[]{:S(2)}) collective-permute-start(bf16[672,768]{1,0:T(8,128)(2,1)S(1)} %collective-permute-done.17.refs_2_), channel_id=1, source_target_pairs={{0,4},{4,0},{8,12},{12,8},{16,20},{20,16},{24,28},{28,24},{1,5},{5... | collective-permute-start | bytes 3096584 | tf_op jit(solution)/shard_map/ppermute | solution.py:37
  100.1 19.5 %collective-permute-start.25 = (bf16[672,768]{1,0:T(8,128)(2,1)S(1)}, bf16[672,768]{1,0:T(8,128)(2,1)S(1)}, u32[]{:S(2)}, u32[]{:S(2)}) collective-permute-start(bf16[672,768]{1,0:T(8,128)(2,1)S(1)} %collective-permute-done.18.refs_4_), channel_id=1, source_target_pairs={{0,4},{4,0},{8,12},{12,8},{16,20},{20,16},{24,28},{28,24},{1,5},{5... | collective-permute-start | bytes 3096584 | tf_op jit(solution)/shard_map/ppermute | solution.py:37
  100.6 18.9 %collective-permute-start.23 = (bf16[480,768]{1,0:T(8,128)(2,1)S(1)}, bf16[480,768]{1,0:T(8,128)(2,1)S(1)}, u32[]{:S(2)}, u32[]{:S(2)}) collective-permute-start(bf16[480,768]{1,0:T(8,128)(2,1)S(1)} %slice.224), channel_id=1, source_target_pairs={{0,8},{4,12},{8,0},{12,4},{16,24},{20,28},{24,16},{28,20},{1,9},{5... | collective-permute-start | bytes 2211848 | tf_op jit(solution)/shard_map/ppermute | solution.py:37
  102.9 16.6 %collective-permute-start.22 = (bf16[192,768]{1,0:T(8,128)(2,1)}, bf16[192,768]{1,0:T(8,128)(2,1)S(1)}, u32[]{:S(2)}, u32[]{:S(2)}) collective-permute-start(bf16[192,768]{1,0:T(8,128)(2,1)} %slice.223), channel_id=1, source_target_pairs={{0,16},{4,20},{8,24},{12,28},{16,0},{20,4},{24,8},{28,12},{1,17},{... | collective-permute-start | bytes 884744 | tf_op jit(solution)/shard_map/ppermute | solution.py:37
  161.4 18.2 %collective-permute-start.32 = (bf16[4,2,4,96,768]{4,3,2,1,0:T(8,128)(2,1)}, bf16[4,2,4,96,768]{4,3,2,1,0:T(8,128)(2,1)}, u32[]{:S(2)}, u32[]{:S(2)}) collective-permute-start(bf16[4,2,4,96,768]{4,3,2,1,0:T(8,128)(2,1)} %get-tuple-element.315), channel_id=1, source_target_pairs={{0,4},{4,0},{8,12},{12,8},{16,20},{20,16},{24,28},{28,24},{1,5},{5... | collective-permute-start | bytes 14155784 | tf_op jit(solution)/shard_map/ppermute | solution.py:37
  182.5 28.9 %collective-permute-start.35 = (bf16[2,4,96,768]{3,2,1,0:T(8,128)(2,1)S(1)}, bf16[2,4,96,768]{3,2,1,0:T(8,128)(2,1)S(1)}, u32[]{:S(2)}, u32[]{:S(2)}) collective-permute-start(bf16[2,4,96,768]{3,2,1,0:T(8,128)(2,1)S(1)} %pad_maximum_fusion), channel_id=1, source_target_pairs={{0,8},{4,12},{8,0},{12,4},{16,24},{20,28},{24,16},{28,20},{1,9},{5... | collective-permute-start | bytes 3538952 | tf_op jit(solution)/shard_map/ppermute | solution.py:37
  183.5 28.0 %collective-permute-start.36 = (bf16[2,4,96,768]{3,2,1,0:T(8,128)(2,1)S(1)}, bf16[2,4,96,768]{3,2,1,0:T(8,128)(2,1)}, u32[]{:S(2)}, u32[]{:S(2)}) collective-permute-start(bf16[2,4,96,768]{3,2,1,0:T(8,128)(2,1)S(1)} %pad_maximum_fusion.1), channel_id=1, source_target_pairs={{0,16},{4,20},{8,24},{12,28},{16,0},{20,4},{24,8},{28,12},{1,17},{... | collective-permute-start | bytes 3538952 | tf_op jit(solution)/shard_map/ppermute | solution.py:37
  234.8 23.1 %collective-permute-start.42 = (bf16[640,768]{1,0:T(8,128)(2,1)}, bf16[640,768]{1,0:T(8,128)(2,1)S(1)}, u32[]{:S(2)}, u32[]{:S(2)}) collective-permute-start(bf16[640,768]{1,0:T(8,128)(2,1)} %pad_maximum_fusion.2), channel_id=1, source_target_pairs={{0,8},{4,12},{8,0},{12,4},{16,24},{20,28},{24,16},{28,20},{1,9},{5... | collective-permute-start | bytes 2949128 | tf_op jit(solution)/shard_map/ppermute | solution.py:37
  235.7 22.7 %collective-permute-start.43 = (bf16[640,768]{1,0:T(8,128)(2,1)S(1)}, bf16[640,768]{1,0:T(8,128)(2,1)}, u32[]{:S(2)}, u32[]{:S(2)}) collective-permute-start(bf16[640,768]{1,0:T(8,128)(2,1)S(1)} %pad_maximum_fusion.3), channel_id=1, source_target_pairs={{0,16},{4,20},{8,24},{12,28},{16,0},{20,4},{24,8},{28,12},{1,17},{... | collective-permute-start | bytes 2949128 | tf_op jit(solution)/shard_map/ppermute | solution.py:37
  236.2 17.1 %collective-permute-start.44 = (bf16[2,96,768]{2,1,0:T(8,128)(2,1)S(1)}, bf16[2,96,768]{2,1,0:T(8,128)(2,1)S(1)}, u32[]{:S(2)}, u32[]{:S(2)}) collective-permute-start(bf16[2,96,768]{2,1,0:T(8,128)(2,1)S(1)} %get-tuple-element.436), channel_id=1, source_target_pairs={{0,2},{1,3},{2,0},{3,1},{4,6},{5,7},{6,4},{7,5},{8,10},{9,11},{10,... | collective-permute-start | bytes 884744 | tf_op jit(solution)/shard_map/ppermute | solution.py:42
  236.2 17.1 %collective-permute-start.45 = (bf16[2,96,768]{2,1,0:T(8,128)(2,1)S(1)}, bf16[2,96,768]{2,1,0:T(8,128)(2,1)}, u32[]{:S(2)}, u32[]{:S(2)}) collective-permute-start(bf16[2,96,768]{2,1,0:T(8,128)(2,1)S(1)} %get-tuple-element.435), channel_id=1, source_target_pairs={{0,3},{1,0},{2,1},{3,2},{4,7},{5,4},{6,5},{7,6},{8,11},{9,8},{10,9... | collective-permute-start | bytes 884744 | tf_op jit(solution)/shard_map/ppermute | solution.py:42
  275.4 17.3 %collective-permute-start.52 = (bf16[160,768]{1,0:T(8,128)(2,1)S(1)}, bf16[160,768]{1,0:T(8,128)(2,1)S(1)}, u32[]{:S(2)}, u32[]{:S(2)}) collective-permute-start(bf16[160,768]{1,0:T(8,128)(2,1)S(1)} %pad_maximum_fusion.6), channel_id=1, source_target_pairs={{0,2},{1,3},{2,0},{3,1},{4,6},{5,7},{6,4},{7,5},{8,10},{9,11},{10,... | collective-permute-start | bytes 737288 | tf_op jit(solution)/shard_map/ppermute | solution.py:42
  (76 other events, 690.5 us)
